TPU v7x, 32 devices: a whole 2x2x4 slice. The times are simulated.
32 devices in a mesh: samp: 8 (over y, x, core), var: 4 (over z).
Axes of the slice: x: 2, y: 2, z: 4, core: 2. Of those that a mesh axis runs over, the one named last changes fastest.
Arguments:
- dosage: bfloat16 [5376, 8192], P('samp', 'var'), may hold values from 0 to 2
- cohort: int32 [5376], P('samp'), may hold values from 0 to 7, as said below
- live_blocks: int32 [8], P('samp'), may hold values from 1 to 7, as said below
- weight_counts: int32 [8], replicated, may hold values from 50 to 1999
Outputs:
- ld_matrix: float32 [8192, 8192], P('samp', 'var')
Inputs may be any that keep to these rules, and one draw needn't show every extreme that they name: Every cohort has a live sample on every sample-axis device. live_blocks[i] + live_blocks[i + N/2] = 8 for every i below N/2, N the length of live_blocks; some device has 7.
All inputs are finite; a program needn't handle non-finite values.
Results may differ from a plain program's by a relative error of at most 0.0032.
Values may be sent and summed in bfloat16 or wider, within the bound.
No kernel may reach another device: no remote copies, remote signals or barrier semaphores. Data moves between devices by JAX's collectives and lax.ppermute only.
A program may use at most 128 MiB of HBM per device.

v0:
```python
import jax
import jax.numpy as jnp
from jax import lax
from jax.sharding import PartitionSpec as P

COHORTS = 8
BLOCK = 96
HALF = 4


EPSILON = 1e-05


def passed_along(block, axis, distance):
    devices = range(lax.axis_size(axis))
    route = [((i - distance) % len(devices), i) for i in devices]
    return lax.ppermute(block, axis, route)


def member_rows(code_rows, weight_row):
    labels = lax.broadcasted_iota(jnp.int32, (COHORTS, code_rows.shape[0]), 0)
    return jnp.where(code_rows[None, :] == labels, weight_row[None, :], 0.0)


def lookup(member, cohort_values):
    return lax.dot_general(
        member,
        cohort_values,
        (((0,), (0,)), ((), ())),
        precision=lax.Precision.HIGHEST,
        preferred_element_type=jnp.float32,
    )


def shards(dosage, cohort, live_blocks, weight_counts):
    own_live = live_blocks[0]
    kept_rows = HALF * BLOCK
    surplus_dose = dosage[kept_rows:]
    surplus_code = cohort[kept_rows:].astype(jnp.bfloat16)
    moved_dose, moved_code = passed_along(
        (surplus_dose, surplus_code), "samp", lax.axis_size("samp") // 2
    )
    offset = own_live * BLOCK
    placed_dose = lax.dynamic_update_slice_in_dim(jnp.zeros_like(dosage), moved_dose, offset, 0)
    placed_code = lax.dynamic_update_slice_in_dim(
        jnp.zeros(cohort.shape, jnp.int32), moved_code.astype(jnp.int32), offset, 0
    )
    row_index = lax.broadcasted_iota(jnp.int32, (kept_rows,), 0)
    from_own = row_index < offset
    dose_rows = jnp.where(from_own[:, None], dosage[:kept_rows], placed_dose[:kept_rows])
    code_rows = jnp.where(from_own, cohort[:kept_rows], placed_code[:kept_rows])
    live_row = jnp.ones((kept_rows,), jnp.float32)
    member = member_rows(code_rows, live_row)
    values = dose_rows.astype(jnp.float32)
    sum_one = jnp.dot(member, values, precision=lax.Precision.HIGHEST)
    sum_two = jnp.dot(member, values * values, precision=lax.Precision.HIGHEST)
    cohort_size = jnp.sum(member, axis=1)
    sum_one, sum_two, cohort_size = lax.psum((sum_one, sum_two, cohort_size), "samp")
    cohort_mean = sum_one / cohort_size[:, None]
    cohort_var = sum_two / cohort_size[:, None] - cohort_mean * cohort_mean
    inv_spread = lax.rsqrt(cohort_var + EPSILON)
    counts_float = weight_counts.astype(jnp.float32)
    cohort_share = counts_float / jnp.sum(counts_float)
    cohort_scale = jnp.sqrt(cohort_share / cohort_size)
    multiplier = inv_spread * cohort_scale[:, None]
    labels_only = member_rows(code_rows, jnp.ones_like(live_row))
    centered = values - lookup(labels_only, cohort_mean)
    scaled = (live_row[:, None] * centered * lookup(labels_only, multiplier)).astype(jnp.bfloat16)
    panels = lax.all_gather(scaled, "var", axis=1, tiled=True)
    return lax.psum_scatter(
        lax.dot_general(
            panels, scaled, (((0,), (0,)), ((), ())), preferred_element_type=jnp.float32
        ),
        "samp",
        scatter_dimension=0,
        tiled=True,
    )


def solution(mesh):
    placed = (P("samp", "var"), P("samp"), P("samp"), P())
    return jax.shard_map(
        shards, mesh=mesh, in_specs=placed, out_specs=P("samp", "var"), check_vma=False
    )
```

profile of v0, /device:TPU:15, one launch (start us, length us, event | category | flops | bytes accessed | tf_op | source)
XLA Modules:
  0.0 648.5 jit_solution(3433342223740219236)
XLA Ops:
  6.5 1.3 slice.20
  7.9 0.3 collective-permute-start
  8.2 0.7 convert.3
  8.9 1.2 collective-permute-start.1
  10.1 1.3 convert_reduce_fusion
  12.1 22.7 %collective-permute-done.1 = bf16[288]{0:T(512)(128)(2,1)S(1)} collective-permute-done((bf16[288]{0:T(512)(128)(2,1)S(1)}, bf16[288]{0:T(512)(128)(2,1)S(1)}, u32[]{:S(2)}, u32[]{:S(2)}) %collective-permute-start.1) | collective-permute-done | bytes 608 | tf_op jit(solution)/shard_map/ppermute | solution.py:17
  34.8 0.1 convert_dynamic-update-slice_fusion
  34.9 0.7 slice_select_fusion.1
  35.6 0.1 select_reduce_fusion
  35.7 11.3 %psum.22 = f32[8]{0:T(128)S(1)} all-reduce(f32[8]{0:T(128)S(1)} %select_reduce_fusion), channel_id=1, replica_groups=mesh['samp'=8,'var'=4] {'samp'}, use_global_device_ids=true, to_apply=%region_2.3 | all-reduce | flops 8 | bytes 64 | tf_op jit(solution)/shard_map/psum | solution.py:58
  47.0 0.3 broadcast_in_dim.37
  47.3 0.2 constant_dynamic-update-slice_fusion
  47.5 1.7 slice_select_fusion
  49.2 2.4 fusion.2
  51.6 1.4 fusion.16
  52.9 0.0 all-gather.2.cloned.1.call-start
  53.0 0.6 fusion.30
  53.7 51.8 %all-reduce.3.cloned.1.call-done = (f32[8,2048]{1,0:T(8,128)}, f32[8,2048]{1,0:T(8,128)}) async-done(((f32[8,2048]{1,0:T(8,128)}, f32[8,2048]{1,0:T(8,128)}), (f32[8,2048]{1,0:T(8,128)}, f32[8,2048]{1,0:T(8,128)})) %all-reduce.3.cloned.1.call-update) | async-done | bytes 131088 | tf_op jit(solution)/shard_map/psum | solution.py:58
  105.5 3.6 fusion.3
  109.1 4.1 fusion.1
  113.2 0.2 reduce-scatter.2.cloned.1.call-start
  113.4 114.2 %all-gather.2.cloned.1.call-done = bf16[384,8192]{1,0:T(8,128)(2,1)} async-done(((bf16[384,2048]{1,0:T(8,128)(2,1)}), bf16[384,8192]{1,0:T(8,128)(2,1)}) %all-gather.2.cloned.1.call-update) | async-done | bytes 6291472 | tf_op jit(solution)/shard_map/all_gather | solution.py:69
  227.6 30.4 %fusion.40 = f32[8192,2048]{1,0:T(8,128)} fusion(bf16[384,8192]{1,0:T(8,128)(2,1)} %all-gather.2.cloned.1.call-done, bf16[384,2048]{1,0:T(8,128)(2,1)} %fusion.1), kind=kOutput, calls=%fused_computation.52 | convolution fusion | flops 12884901888 | bytes 74973184 | tf_op jit(solution)/shard_map/dot_general | solution.py:71
  258.1 383.9 %reduce-scatter.2.cloned.1.call-done = f32[1024,2048]{1,0:T(8,128)} async-done(((f32[8192,2048]{1,0:T(8,128)}), f32[1024,2048]{1,0:T(8,128)}) %reduce-scatter.2.cloned.1.call-update) | async-done | bytes 8388624 | tf_op jit(solution)/shard_map/reduce_scatter | solution.py:70
  (12 shorter events, 0.1 us)
Async XLA Ops:
  6.5 99.0 %all-reduce.3.cloned.1.call-start = ((), (), s32[]{:S(2)}) async-start(), calls=%async_computation.3 | async-start | bytes 262144 | tf_op jit(solution)/shard_map/psum | solution.py:58
  7.9 39.1 %collective-permute-start = (bf16[288,2048]{1,0:T(8,128)(2,1)S(1)}, bf16[288,2048]{1,0:T(8,128)(2,1)S(1)}, u32[]{:S(2)}, u32[]{:S(2)}) collective-permute-start(bf16[288,2048]{1,0:T(8,128)(2,1)S(1)} %slice.20), channel_id=1, source_target_pairs={{16,0},{20,4},{24,8},{28,12},{0,16},{4,20},{8,24},{12,28},{17,1},{... | collective-permute-start | bytes 3538952 | tf_op jit(solution)/shard_map/ppermute | solution.py:17
  8.9 25.9 %collective-permute-start.1 = (bf16[288]{0:T(512)(128)(2,1)S(1)}, bf16[288]{0:T(512)(128)(2,1)S(1)}, u32[]{:S(2)}, u32[]{:S(2)}) collective-permute-start(bf16[288]{0:T(512)(128)(2,1)S(1)} %slice.23), channel_id=1, source_target_pairs={{16,0},{20,4},{24,8},{28,12},{0,16},{4,20},{8,24},{12,28},{17,1},{... | collective-permute-start | bytes 1736 | tf_op jit(solution)/shard_map/ppermute | solution.py:17
  49.2 3.8 copy-start.1
  52.9 174.7 %all-gather.2.cloned.1.call-start = ((), (), s32[]{:S(2)}) async-start(), calls=%async_computation.1 | async-start | bytes 7864320 | tf_op jit(solution)/shard_map/all_gather | solution.py:69
  105.5 3.6 copy-start
  113.2 528.8 %reduce-scatter.2.cloned.1.call-start = ((), (), s32[]{:S(2)}) async-start(), calls=%async_computation.2 | async-start | bytes 75497472 | tf_op jit(solution)/shard_map/reduce_scatter | solution.py:70
Sparse Core Ops, SparseCore 0:
  53.1 52.3 all-reduce.2
  113.3 114.2 all-gather.1
  258.2 383.7 reduce-scatter.1
where the time goes:
time: 651 us; the launch traced here: 648 us
  waiting for transfers between devices  573 us (88%)
  matrix products  41.8 us (6%)
  between operations  13.8 us (2%)
  blocking collectives  11.3 us (2%)
    reduce_scatter x1, waiting for transfers between devices, shards(): lax.psum_scatter(lax.dot_general(panels, scaled, (((0,), (0,)), ((), ()))...  384 us
    all_gather x1, waiting for transfers between devices, shards(): panels = lax.all_gather(scaled, 'var', axis=1, tiled=True)  114 us
    psum x1, waiting for transfers between devices, shards(): lax.psum((sum_one, sum_two, cohort_size), 'samp')  51.8 us
    dot_general x1, matrix products, shards(): lax.dot_general(panels, scaled, (((0,), (0,)), ((), ())), preferred_eleme...  30.4 us
    ppermute x2, waiting for transfers between devices, passed_along(): return lax.ppermute(block, axis, route)  22.7 us
  transfers between devices with their start and end apart: 5, of which 4 were waited for; matrix products, arithmetic and copies ran while one was open for 1% of the time, Pallas kernels for 0%

commit v1 on v0

v1 whole, which is shorter than its diff:
```python
import functools

import jax
import jax.numpy as jnp
from jax import lax
from jax.experimental import pallas as pl
from jax.experimental.pallas import tpu as pltpu
from jax.sharding import PartitionSpec as P

COHORTS = 8
BLOCK = 96
HALF = 4
EPSILON = 1e-05
PARTS = 3
TABLE = 128


def swapped(block, distance):
    return lax.ppermute(
        block, "samp", [(i, i ^ distance) for i in range(lax.axis_size("samp"))]
    )


def route(start, count):
    down, up = list(range(start - 1, -1, -1)), list(range(start + 1, count))
    return [start] + (down + up if start < count // 2 else up + down)


def split_parts(table):
    parts, rest = [], table
    for _ in range(PARTS):
        part = lax.reduce_precision(rest, exponent_bits=8, mantissa_bits=7)
        parts.append(part.astype(jnp.bfloat16))
        rest = rest - part
    used = PARTS * COHORTS
    parts.append(jnp.zeros((TABLE - used, table.shape[1]), jnp.bfloat16))
    return jnp.concatenate(parts, 0)


def sums_kernel(member_ref, dose_ref, sums_ref):
    member = member_ref[...]
    dose = dose_ref[...]
    wide = dose.astype(jnp.float32)
    square = wide * wide
    high = square.astype(jnp.bfloat16)
    low = (square - high.astype(jnp.float32)).astype(jnp.bfloat16)
    dot = functools.partial(jnp.dot, preferred_element_type=jnp.float32)
    sums_ref[:COHORTS, :] = dot(member, dose)[:COHORTS]
    sums_ref[COHORTS:, :] = (dot(member, high) + dot(member, low))[:COHORTS]


def cohort_sums(member, dose):
    rows, columns = dose.shape
    tile = min(512, columns)
    return pl.pallas_call(
        sums_kernel,
        grid=(columns // tile,),
        in_specs=[
            pl.BlockSpec((16, rows), lambda j: (0, 0)),
            pl.BlockSpec((rows, tile), lambda j: (0, j)),
        ],
        out_specs=pl.BlockSpec((2 * COHORTS, tile), lambda j: (0, j)),
        out_shape=jax.ShapeDtypeStruct((2 * COHORTS, columns), jnp.float32),
        cost_estimate=pl.CostEstimate(
            flops=6 * 16 * rows * columns, bytes_accessed=2 * rows * columns, transcendentals=0
        ),
        compiler_params=pltpu.CompilerParams(vmem_limit_bytes=24 * 2**20),
    )(member, dose)


def standardized(dose, onehot, mean_table, scale_table):
    dot = functools.partial(jnp.dot, preferred_element_type=jnp.float32)
    centered = dose.astype(jnp.float32) - dot(onehot, mean_table)
    return (centered * dot(onehot, scale_table)).astype(jnp.bfloat16)


def gram_kernel(sizes, has_total, *refs):
    n = len(sizes)
    cols, rows, hots = refs[:n], refs[n : 2 * n], refs[2 * n : 3 * n]
    col_mean, col_scale, row_mean, row_scale = refs[3 * n : 3 * n + 4]
    rest = refs[3 * n + 4 :]
    out, row_ready, col_ready = rest[-3:]

    @pl.when(pl.program_id(0) == 0)
    def _():
        at = 0
        for j, size in enumerate(sizes):
            ready = standardized(rows[j][...], hots[j][...], row_mean[...], row_scale[...])
            row_ready[:, at : at + size] = ready.T
            at += size

    at = 0
    for j, size in enumerate(sizes):
        col_ready[at : at + size, :] = standardized(
            cols[j][...], hots[j][...], col_mean[...], col_scale[...]
        )
        at += size
    product = jnp.dot(row_ready[...], col_ready[...], preferred_element_type=jnp.float32)
    if has_total:
        product += rest[0][...]
    out[...] = product


def gram(total, cols, rows, hots, col_tables, row_tables):
    sizes = tuple(c.shape[0] for c in cols)
    depth, width, height = sum(sizes), cols[0].shape[1], rows[0].shape[1]
    tile = min(512, width)
    whole = lambda shape: pl.BlockSpec(shape, lambda j: (0, 0))
    by_tile = lambda height: pl.BlockSpec((height, tile), lambda j: (0, j))
    in_specs = (
        [by_tile(s) for s in sizes]
        + [whole((s, height)) for s in sizes]
        + [whole((s, TABLE)) for s in sizes]
        + [by_tile(TABLE)] * 2
        + [whole((TABLE, height))] * 2
    )
    operands = [*cols, *rows, *hots, *col_tables, *row_tables]
    aliases = {}
    if total is not None:
        aliases = {len(operands): 0}
        operands.append(total)
        in_specs.append(by_tile(height))
    return pl.pallas_call(
        functools.partial(gram_kernel, sizes, total is not None),
        grid=(width // tile,),
        in_specs=in_specs,
        out_specs=by_tile(height),
        out_shape=jax.ShapeDtypeStruct((height, width), jnp.float32),
        scratch_shapes=[
            pltpu.VMEM((height, depth), jnp.bfloat16),
            pltpu.VMEM((depth, tile), jnp.bfloat16),
        ],
        input_output_aliases=aliases,
        cost_estimate=pl.CostEstimate(
            flops=2 * depth * height * width,
            bytes_accessed=8 * height * width + 2 * depth * (height + width),
            transcendentals=0,
        ),
        compiler_params=pltpu.CompilerParams(vmem_limit_bytes=48 * 2**20),
    )(*operands)


def shards(dosage, cohort, live_blocks, weight_counts):
    n_samp, n_var = lax.axis_size("samp"), lax.axis_size("var")
    samp, var = lax.axis_index("samp"), lax.axis_index("var")
    slots, width = dosage.shape
    height = width * n_var // n_samp
    kept = HALF * BLOCK
    owner = [i * height // width for i in range(n_samp)]
    routes = [route(owner[i], n_var) for i in range(n_samp)]
    place_on_route = [[r.index(v) for v in range(n_var)] for r in routes]
    place = jnp.asarray(place_on_route, jnp.int32)[samp, var]
    row_start = samp * height % width
    bits = [n_samp >> (b + 1) for b in range(n_samp.bit_length() - 1)]

    def along_line(block):
        result = moving = block
        for hop in range(1, n_var):
            pairs = [
                (s * n_var + r[hop - 1], s * n_var + r[hop]) for s, r in enumerate(routes)
            ]
            moving = lax.ppermute(moving, ("samp", "var"), pairs)
            result = jnp.where(place == hop, moving, result)
        return result

    def row_part(block):
        return lax.dynamic_slice_in_dim(block, row_start, height, 1)

    own_live = live_blocks[0]
    info = jnp.concatenate([cohort, jnp.broadcast_to(own_live, (TABLE,))])
    infos = lax.all_gather(info, "samp", axis=0)
    surplus = swapped(dosage[kept:], n_samp // 2)

    position = lax.broadcasted_iota(jnp.int32, (16, slots), 1)
    label = lax.broadcasted_iota(jnp.int32, (16, slots), 0)
    member = (cohort[None, :] == label) & (position < own_live * BLOCK)
    sums = cohort_sums(member.astype(jnp.bfloat16), dosage)
    for bit in bits:
        sums = sums + swapped(sums, bit)

    offset = own_live * BLOCK
    placed = lax.dynamic_update_slice_in_dim(jnp.zeros_like(dosage), surplus, offset, 0)
    row_index = lax.broadcasted_iota(jnp.int32, (kept, 1), 0)
    balanced = jnp.where(row_index < offset, dosage[:kept], placed[:kept])

    pieces = [(0, balanced)]
    for bit in bits:
        pieces += [(m ^ bit, swapped(block, bit)) for m, block in pieces]
    order = [m for m, _ in pieces]

    lives = infos[:, slots]
    codes = infos[:, :slots]
    devices = jnp.arange(n_samp)
    partner = codes[devices ^ (n_samp // 2)]
    slot = lax.broadcasted_iota(jnp.int32, (n_samp, kept), 1)
    moved_from = kept + slot - lives[:, None] * BLOCK
    moved = jnp.take_along_axis(partner, jnp.clip(moved_from, 0, slots - 1), axis=1)
    codes = jnp.where(slot < lives[:, None] * BLOCK, codes[:, :kept], moved)
    cohort_size = jnp.sum(
        (codes[None] == jnp.arange(COHORTS)[:, None, None]).astype(jnp.float32), axis=(1, 2)
    )
    lane = lax.broadcasted_iota(jnp.int32, (kept, TABLE), 1)
    lane = jnp.where(lane < PARTS * COHORTS, lane % COHORTS, -1)
    hots = [
        (codes[samp ^ m][:, None] == lane).astype(jnp.bfloat16) for m in order
    ]

    sum_one, sum_two = sums[:COHORTS], sums[COHORTS:]
    cohort_mean = sum_one / cohort_size[:, None]
    cohort_var = sum_two / cohort_size[:, None] - cohort_mean * cohort_mean
    inv_spread = lax.rsqrt(cohort_var + EPSILON)
    counts_float = weight_counts.astype(jnp.float32)
    cohort_share = counts_float / jnp.sum(counts_float)
    multiplier = inv_spread * jnp.sqrt(cohort_share / cohort_size)[:, None]
    tables = jnp.concatenate([cohort_mean, multiplier], 0)
    row_tables = along_line(row_part(tables))
    col_tables = [split_parts(cohort_mean), split_parts(multiplier)]
    row_tables = [split_parts(row_tables[:COHORTS]), split_parts(row_tables[COHORTS:])]

    rows = [along_line(row_part(block)) for _, block in pieces]
    cols = [block for _, block in pieces]
    total = None
    step = max(1, len(cols) // 4)
    for at in range(0, len(cols), step):
        part = slice(at, at + step)
        total = gram(total, cols[part], rows[part], hots[part], col_tables, row_tables)
    return total


def solution(mesh):
    placed = (P("samp", "var"), P("samp"), P("samp"), P())
    return jax.shard_map(
        shards, mesh=mesh, in_specs=placed, out_specs=P("samp", "var"), check_vma=False
    )
```

time: 651 us -> 287 us (0.44)
  waiting for transfers between devices: 573 us -> 107 us
  starting transfers between devices: 1.8 us -> 55.3 us
  Pallas kernels: 0 us -> 44.4 us
  matrix products: 41.8 us -> 0 us
  local copies, waits for them, and re-layouts: 1.85 us -> 34.4 us
  blocking collectives: 11.3 us -> 22.3 us
  between operations: 13.8 us -> 3.96 us
  other arithmetic: 5.2 us -> 14.5 us
    reduce_scatter x1 -> x0, waiting for transfers between devices: 384 us -> none  [shards(): lax.psum_scatter(lax.dot_general(panels, scaled, (((0,), (0,)), ((), ()))...]
    all_gather x1 -> x0, waiting for transfers between devices: 114 us -> none  [shards(): panels = lax.all_gather(scaled, 'var', axis=1, tiled=True)]
    ppermute x2 -> x38, waiting for transfers between devices: 22.7 us -> 107 us  [the longest x27 100 us: along_line(): moving = lax.ppermute(moving, ('samp', 'var'), pairs)]
    ppermute x2 -> x38, starting transfers between devices: 1.53 us -> 55.3 us  [the longest x27 40.2 us: along_line(): moving = lax.ppermute(moving, ('samp', 'var'), pairs)]
    psum x1 -> x0, waiting for transfers between devices: 51.8 us -> none  [shards(): lax.psum((sum_one, sum_two, cohort_size), 'samp')]
    pallas_call x0 -> x5, Pallas kernels: none -> 44.4 us  [the longest x4 42.3 us: gram(): pl.pallas_call(functools.partial(gram_kernel, sizes, total is not None),...]
    dot_general x5 -> x0, matrix products: 41.8 us -> none  [the longest x1 30.4 us: shards(): lax.dot_general(panels, scaled, (((0,), (0,)), ((), ())), preferred_eleme...]
    unnamed x0 -> x1, blocking collectives: none -> 22.3 us
  transfers between devices with their start and end apart: 5 -> 38, of which waited for: 4 -> 16; matrix products, arithmetic and copies ran while one was open for 1% -> 15% of each run, Pallas kernels for 0% -> 12%
where the time goes in v1:
time: 287 us; the launch traced here: 282 us
  waiting for transfers between devices  107 us (37%)
  starting transfers between devices  55.3 us (19%)
  Pallas kernels  44.4 us (15%)
  local copies, waits for them, and re-layouts  34.4 us (12%)
  blocking collectives  22.3 us (8%)
  other arithmetic  14.5 us (5%)
  between operations  3.96 us (1%)
    ppermute x27, waiting for transfers between devices, along_line(): moving = lax.ppermute(moving, ('samp', 'var'), pairs)  100 us
    pallas_call x4, Pallas kernels, gram(): pl.pallas_call(functools.partial(gram_kernel, sizes, total is not None),...  42.3 us
    ppermute x27, starting transfers between devices, along_line(): moving = lax.ppermute(moving, ('samp', 'var'), pairs)  40.2 us
    unnamed x1, blocking collectives  22.3 us
    gather x3, local copies, waits for them, and re-layouts, shards(): jnp.take_along_axis(partner, jnp.clip(moved_from, 0, slots - 1), axis=1)  19.1 us
    ppermute x11, starting transfers between devices, swapped(): lax.ppermute(block, 'samp', [(i, i ^ distance) for i in range(lax.axis_si...  15 us
    select_n x9, other arithmetic, along_line(): result = jnp.where(place == hop, moving, result)  11.4 us
    dynamic_slice x8, local copies, waits for them, and re-layouts, row_part(): return lax.dynamic_slice_in_dim(block, row_start, height, 1)  6.59 us
  transfers between devices with their start and end apart: 38, of which 16 were waited for; matrix products, arithmetic and copies ran while one was open for 15% of the time, Pallas kernels for 12%

profile of v1, /device:TPU:15, one launch (start us, length us, event | category | flops | bytes accessed | tf_op | source)
XLA Modules:
  0.0 281.9 jit_solution(18294011640655649221)
XLA Ops:
  4.2 2.2 shard_map.55
  9.0 22.3 %all-reduce.1 = s32[6400]{0:T(1024)S(1)} all-reduce(s32[6400]{0:T(1024)S(1)} %pad_dynamic-update-slice_fusion), channel_id=2, replica_groups=mesh['samp'=8,'var'=4] {'samp'}, use_global_device_ids=true, to_apply=%add.1 | all-reduce | flops 6400 | bytes 51200
  37.2 19.1 %gather_fusion.1 = s32[3072]{0:T(1024)S(1)} fusion(s32[8,672]{1,0:T(8,128)S(1)} %gather_fusion, s32[3072]{0:T(1024)S(1)} %reshape.123), kind=kCustom, calls=%fused_computation.1 | custom fusion | bytes 49152 | tf_op jit(solution)/shard_map/jit(take_along_axis)/gather | solution.py:197
  60.7 4.2 %collective-permute-start.14 = (f32[16,2048]{1,0:T(8,128)S(1)}, f32[16,2048]{1,0:T(8,128)S(1)}, u32[]{:S(2)}, u32[]{:S(2)}) collective-permute-start(f32[16,2048]{1,0:T(8,128)S(1)} %add.140), channel_id=1, source_target_pairs={{0,4},{4,0},{8,12},{12,8},{16,20},{20,16},{24,28},{28,24},{1,5},{5... | collective-permute-start | bytes 393224 | tf_op jit(solution)/shard_map/ppermute | solution.py:19
  72.9 15.2 %collective-permute-done.33 = bf16[384,1024]{1,0:T(8,128)(2,1)S(1)} collective-permute-done((bf16[384,1024]{1,0:T(8,128)(2,1)}, bf16[384,1024]{1,0:T(8,128)(2,1)S(1)}, u32[]{:S(2)}, u32[]{:S(2)}) %collective-permute-start.33) | collective-permute-done | bytes 786464 | tf_op jit(solution)/shard_map/ppermute | solution.py:162
  89.8 3.5 %collective-permute-done.1.refs_0_ = bf16[384,2048]{1,0:T(8,128)(2,1)S(1)} collective-permute-done((bf16[384,2048]{1,0:T(8,128)(2,1)S(1)}, bf16[384,2048]{1,0:T(8,128)(2,1)S(1)}, u32[]{:S(2)}, u32[]{:S(2)}) %collective-permute-start.1) | collective-permute-done | bytes 1572896 | tf_op jit(solution)/shard_map/ppermute | solution.py:19
  96.3 10.1 %collective-permute-done.17 = f32[16,1024]{1,0:T(8,128)S(1)} collective-permute-done((f32[16,1024]{1,0:T(8,128)S(1)}, f32[16,1024]{1,0:T(8,128)S(1)}, u32[]{:S(2)}, u32[]{:S(2)}) %collective-permute-start.17) | collective-permute-done | bytes 65568 | tf_op jit(solution)/shard_map/ppermute | solution.py:162
  108.0 2.1 collective-permute-start.19
  121.4 12.3 %collective-permute-done.36 = bf16[384,1024]{1,0:T(8,128)(2,1)} collective-permute-done((bf16[384,1024]{1,0:T(8,128)(2,1)}, bf16[384,1024]{1,0:T(8,128)(2,1)}, u32[]{:S(2)}, u32[]{:S(2)}) %collective-permute-start.36) | collective-permute-done | bytes 786464 | tf_op jit(solution)/shard_map/ppermute | solution.py:162
  135.0 3.8 %collective-permute-start.5 = (bf16[384,2048]{1,0:T(8,128)(2,1)}, bf16[384,2048]{1,0:T(8,128)(2,1)S(1)}, u32[]{:S(2)}, u32[]{:S(2)}) collective-permute-start(bf16[384,2048]{1,0:T(8,128)(2,1)} %collective-permute-done.4.refs_1_), channel_id=1, source_target_pairs={{0,4},{4,0},{8,12},{12,8},{16,20},{20,16},{24,28},{28,24},{1,5},{5... | collective-permute-start | bytes 4718600 | tf_op jit(solution)/shard_map/ppermute | solution.py:19
  140.0 10.4 %collective-permute-done.27 = bf16[384,1024]{1,0:T(8,128)(2,1)S(1)} collective-permute-done((bf16[384,1024]{1,0:T(8,128)(2,1)}, bf16[384,1024]{1,0:T(8,128)(2,1)S(1)}, u32[]{:S(2)}, u32[]{:S(2)}) %collective-permute-start.27) | collective-permute-done | bytes 786464 | tf_op jit(solution)/shard_map/ppermute | solution.py:162
  153.9 13.4 %collective-permute-done.21 = bf16[384,1024]{1,0:T(8,128)(2,1)S(1)} collective-permute-done((bf16[384,1024]{1,0:T(8,128)(2,1)}, bf16[384,1024]{1,0:T(8,128)(2,1)S(1)}, u32[]{:S(2)}, u32[]{:S(2)}) %collective-permute-start.21) | collective-permute-done | bytes 786464 | tf_op jit(solution)/shard_map/ppermute | solution.py:162
  175.9 8.8 %collective-permute-done.28 = bf16[384,1024]{1,0:T(8,128)(2,1)S(1)} collective-permute-done((bf16[384,1024]{1,0:T(8,128)(2,1)S(1)}, bf16[384,1024]{1,0:T(8,128)(2,1)S(1)}, u32[]{:S(2)}, u32[]{:S(2)}) %collective-permute-start.28) | collective-permute-done | bytes 786464 | tf_op jit(solution)/shard_map/ppermute | solution.py:162
  190.0 4.7 %collective-permute-start.31 = (bf16[384,1024]{1,0:T(8,128)(2,1)}, bf16[384,1024]{1,0:T(8,128)(2,1)}, u32[]{:S(2)}, u32[]{:S(2)}) collective-permute-start(bf16[384,1024]{1,0:T(8,128)(2,1)} %collective-permute-done.30), channel_id=1, source_target_pairs={{2,3},{6,7},{10,11},{14,15},{17,16},{21,20},{25,24},{29,28}} | collective-permute-start | bytes 2359304 | tf_op jit(solution)/shard_map/ppermute | solution.py:162
  195.3 11.6 %collective-permute-done.24 = bf16[384,1024]{1,0:T(8,128)(2,1)} collective-permute-done((bf16[384,1024]{1,0:T(8,128)(2,1)S(1)}, bf16[384,1024]{1,0:T(8,128)(2,1)}, u32[]{:S(2)}, u32[]{:S(2)}) %collective-permute-start.24) | collective-permute-done | bytes 786464 | tf_op jit(solution)/shard_map/ppermute | solution.py:162
  206.9 2.2 collective-permute-start.25
  211.2 9.1 %shard_map.56.refs_10_ = f32[1024,2048]{1,0:T(8,128)} custom-call(bf16[384,2048]{1,0:T(8,128)(2,1)S(1)} %slice_select_fusion.refs_0_, bf16[384,2048]{1,0:T(8,128)(2,1)} %collective-permute-done.3.refs_1_, bf16[384,1024]{1,0:T(8,128)(2,1)S(1)} %select_select_fusion.1.refs_2_, bf16[384,1024]{1,0:T(8,128)(2,1)S(1)} %select_select_fusion.refs_3_, ...), custom_call_target="tpu_custom_call" | custom-call | flops 3221225472 | bytes 21495808 | tf_op jit(solution)/shard_map/pallas_call | solution.py:123
  220.3 3.4 %collective-permute-done.7 = bf16[384,1024]{1,0:T(8,128)(2,1)} collective-permute-done((bf16[384,1024]{1,0:T(8,128)(2,1)}, bf16[384,1024]{1,0:T(8,128)(2,1)}, u32[]{:S(2)}, u32[]{:S(2)}) %collective-permute-start.7) | collective-permute-done | bytes 786464 | tf_op jit(solution)/shard_map/ppermute | solution.py:162
  227.1 8.3 %collective-permute-done.25 = bf16[384,1024]{1,0:T(8,128)(2,1)} collective-permute-done((bf16[384,1024]{1,0:T(8,128)(2,1)}, bf16[384,1024]{1,0:T(8,128)(2,1)}, u32[]{:S(2)}, u32[]{:S(2)}) %collective-permute-start.25) | collective-permute-done | bytes 786464 | tf_op jit(solution)/shard_map/ppermute | solution.py:162
  237.4 3.2 %collective-permute-done.10 = bf16[384,1024]{1,0:T(8,128)(2,1)} collective-permute-done((bf16[384,1024]{1,0:T(8,128)(2,1)}, bf16[384,1024]{1,0:T(8,128)(2,1)}, u32[]{:S(2)}, u32[]{:S(2)}) %collective-permute-start.10) | collective-permute-done | bytes 786464 | tf_op jit(solution)/shard_map/ppermute | solution.py:162
  241.9 11.1 %shard_map.57.refs_10_ = f32[1024,2048]{1,0:T(8,128)} custom-call(bf16[384,2048]{1,0:T(8,128)(2,1)S(1)} %collective-permute-done.1.refs_0_, bf16[384,2048]{1,0:T(8,128)(2,1)} %collective-permute-done.4.refs_1_, bf16[384,1024]{1,0:T(8,128)(2,1)S(1)} %select_select_fusion.3.refs_2_, ...), custom_call_target="tpu_custom_call", output_to_operand_aliasing={{}: (10, {})} | custom-call | flops 3221225472 | bytes 21495808 | tf_op jit(solution)/shard_map/pallas_call | solution.py:123
  253.0 11.0 %shard_map.58.refs_10_ = f32[1024,2048]{1,0:T(8,128)} custom-call(bf16[384,2048]{1,0:T(8,128)(2,1)S(1)} %copy-done.3, bf16[384,2048]{1,0:T(8,128)(2,1)} %collective-permute-done.19.refs_1_, bf16[384,1024]{1,0:T(8,128)(2,1)S(1)} %select_select_fusion.5.refs_2_, bf16[384,1024]{1,0:T(8,128)(2,1)S(1)} %select_select_fusion.4.refs_3_, ...), custom_call_target="tpu_custom_call", output_to_operand_aliasing={{}: (10, {})} | custom-call | flops 3221225472 | bytes 21495808 | tf_op jit(solution)/shard_map/pallas_call | solution.py:123
  265.8 3.3 %collective-permute-done.11 = bf16[384,1024]{1,0:T(8,128)(2,1)S(1)} collective-permute-done((bf16[384,1024]{1,0:T(8,128)(2,1)}, bf16[384,1024]{1,0:T(8,128)(2,1)S(1)}, u32[]{:S(2)}, u32[]{:S(2)}) %collective-permute-start.11) | collective-permute-done | bytes 786464 | tf_op jit(solution)/shard_map/ppermute | solution.py:162
  270.8 11.1 %shard_map.59 = f32[1024,2048]{1,0:T(8,128)} custom-call(bf16[384,2048]{1,0:T(8,128)(2,1)S(1)} %collective-permute-done.2.refs_0_, bf16[384,2048]{1,0:T(8,128)(2,1)} %copy-done.4, bf16[384,1024]{1,0:T(8,128)(2,1)S(1)} %select_select_fusion.7.refs_2_, bf16[384,1024]{1,0:T(8,128)(2,1)S(1)} %select_select_fusion.6.refs_3_, ...), custom_call_target="tpu_custom_call", output_to_operand_aliasing={{}: (10, {})} | custom-call | flops 3221225472 | bytes 21495808 | tf_op jit(solution)/shard_map/pallas_call | solution.py:123
  (148 shorter events, 71.6 us)
Async XLA Ops:
  1.4 30.3 %collective-permute-start = (bf16[288,2048]{1,0:T(8,128)(2,1)S(1)}, bf16[288,2048]{1,0:T(8,128)(2,1)S(1)}, u32[]{:S(2)}, u32[]{:S(2)}) collective-permute-start(bf16[288,2048]{1,0:T(8,128)(2,1)S(1)} %slice.32), channel_id=1, source_target_pairs={{0,16},{4,20},{8,24},{12,28},{16,0},{20,4},{24,8},{28,12},{1,17},{... | collective-permute-start | bytes 3538952 | tf_op jit(solution)/shard_map/ppermute | solution.py:19
  6.3 50.1 %collective-permute-start.12 = (f32[16,2048]{1,0:T(8,128)S(1)}, f32[16,2048]{1,0:T(8,128)S(1)}, u32[]{:S(2)}, u32[]{:S(2)}) collective-permute-start(f32[16,2048]{1,0:T(8,128)S(1)} %shard_map.55), channel_id=1, source_target_pairs={{0,16},{4,20},{8,24},{12,28},{16,0},{20,4},{24,8},{28,12},{1,17},{... | collective-permute-start | bytes 393224 | tf_op jit(solution)/shard_map/ppermute | solution.py:19
  33.7 36.5 %collective-permute-start.3 = (bf16[384,2048]{1,0:T(8,128)(2,1)S(1)}, bf16[384,2048]{1,0:T(8,128)(2,1)}, u32[]{:S(2)}, u32[]{:S(2)}) collective-permute-start(bf16[384,2048]{1,0:T(8,128)(2,1)S(1)} %slice_select_fusion.refs_0_), channel_id=1, source_target_pairs={{0,16},{4,20},{8,24},{12,28},{16,0},{20,4},{24,8},{28,12},{1,17},{... | collective-permute-start | bytes 4718600 | tf_op jit(solution)/shard_map/ppermute | solution.py:19
  34.9 30.0 %collective-permute-start.32 = (bf16[384,1024]{1,0:T(8,128)(2,1)}, bf16[384,1024]{1,0:T(8,128)(2,1)}, u32[]{:S(2)}, u32[]{:S(2)}) collective-permute-start(bf16[384,1024]{1,0:T(8,128)(2,1)} %constant_dynamic-slice_fusion.3), channel_id=1, source_target_pairs={{0,1},{4,5},{9,8},{13,12},{18,19},{22,23},{27,26},{31,30}} | collective-permute-start | bytes 2359304 | tf_op jit(solution)/shard_map/ppermute | solution.py:162
  56.5 36.8 %collective-permute-start.1 = (bf16[384,2048]{1,0:T(8,128)(2,1)S(1)}, bf16[384,2048]{1,0:T(8,128)(2,1)S(1)}, u32[]{:S(2)}, u32[]{:S(2)}) collective-permute-start(bf16[384,2048]{1,0:T(8,128)(2,1)S(1)} %slice_select_fusion.refs_0_), channel_id=1, source_target_pairs={{0,8},{4,12},{8,0},{12,4},{16,24},{20,28},{24,16},{28,20},{1,9},{5... | collective-permute-start | bytes 4718600 | tf_op jit(solution)/shard_map/ppermute | solution.py:19
  64.9 43.1 %collective-permute-start.18 = (bf16[384,2048]{1,0:T(8,128)(2,1)S(1)}, bf16[384,2048]{1,0:T(8,128)(2,1)S(1)}, u32[]{:S(2)}, u32[]{:S(2)}) collective-permute-start(bf16[384,2048]{1,0:T(8,128)(2,1)S(1)} %slice_select_fusion.refs_0_), channel_id=1, source_target_pairs={{0,4},{4,0},{8,12},{12,8},{16,20},{20,16},{24,28},{28,24},{1,5},{5... | collective-permute-start | bytes 4718600 | tf_op jit(solution)/shard_map/ppermute | solution.py:19
  65.0 23.1 %collective-permute-start.33 = (bf16[384,1024]{1,0:T(8,128)(2,1)}, bf16[384,1024]{1,0:T(8,128)(2,1)S(1)}, u32[]{:S(2)}, u32[]{:S(2)}) collective-permute-start(bf16[384,1024]{1,0:T(8,128)(2,1)} %collective-permute-done.32), channel_id=1, source_target_pairs={{1,2},{5,6},{8,10},{12,14},{19,17},{23,21},{26,25},{30,29}} | collective-permute-start | bytes 2359304 | tf_op jit(solution)/shard_map/ppermute | solution.py:162
  71.3 39.8 %collective-permute-start.35 = (bf16[384,1024]{1,0:T(8,128)(2,1)S(1)}, bf16[384,1024]{1,0:T(8,128)(2,1)}, u32[]{:S(2)}, u32[]{:S(2)}) collective-permute-start(bf16[384,1024]{1,0:T(8,128)(2,1)S(1)} %constant_dynamic-slice_fusion.2), channel_id=1, source_target_pairs={{0,1},{4,5},{9,8},{13,12},{18,19},{22,23},{27,26},{31,30}} | collective-permute-start | bytes 2359304 | tf_op jit(solution)/shard_map/ppermute | solution.py:162
  88.1 24.6 %collective-permute-start.34 = (bf16[384,1024]{1,0:T(8,128)(2,1)S(1)}, bf16[384,1024]{1,0:T(8,128)(2,1)S(1)}, u32[]{:S(2)}, u32[]{:S(2)}) collective-permute-start(bf16[384,1024]{1,0:T(8,128)(2,1)S(1)} %collective-permute-done.33), channel_id=1, source_target_pairs={{2,3},{6,7},{10,11},{14,15},{17,16},{21,20},{25,24},{29,28}} | collective-permute-start | bytes 2359304 | tf_op jit(solution)/shard_map/ppermute | solution.py:162
  89.5 45.5 %collective-permute-start.4 = (bf16[384,2048]{1,0:T(8,128)(2,1)}, bf16[384,2048]{1,0:T(8,128)(2,1)}, u32[]{:S(2)}, u32[]{:S(2)}) collective-permute-start(bf16[384,2048]{1,0:T(8,128)(2,1)} %collective-permute-done.3.refs_1_), channel_id=1, source_target_pairs={{0,8},{4,12},{8,0},{12,4},{16,24},{20,28},{24,16},{28,20},{1,9},{5... | collective-permute-start | bytes 4718600 | tf_op jit(solution)/shard_map/ppermute | solution.py:19
  108.0 43.2 %collective-permute-start.19 = (bf16[384,2048]{1,0:T(8,128)(2,1)}, bf16[384,2048]{1,0:T(8,128)(2,1)}, u32[]{:S(2)}, u32[]{:S(2)}) collective-permute-start(bf16[384,2048]{1,0:T(8,128)(2,1)} %collective-permute-done.3.refs_1_), channel_id=1, source_target_pairs={{0,4},{4,0},{8,12},{12,8},{16,20},{20,16},{24,28},{28,24},{1,5},{5... | collective-permute-start | bytes 4718600 | tf_op jit(solution)/shard_map/ppermute | solution.py:19
  118.2 32.2 %collective-permute-start.27 = (bf16[384,1024]{1,0:T(8,128)(2,1)}, bf16[384,1024]{1,0:T(8,128)(2,1)S(1)}, u32[]{:S(2)}, u32[]{:S(2)}) collective-permute-start(bf16[384,1024]{1,0:T(8,128)(2,1)} %collective-permute-done.26), channel_id=1, source_target_pairs={{1,2},{5,6},{8,10},{12,14},{19,17},{23,21},{26,25},{30,29}} | collective-permute-start | bytes 2359304 | tf_op jit(solution)/shard_map/ppermute | solution.py:162
  120.2 47.9 %collective-permute-start.2 = (bf16[384,2048]{1,0:T(8,128)(2,1)S(1)}, bf16[384,2048]{1,0:T(8,128)(2,1)S(1)}, u32[]{:S(2)}, u32[]{:S(2)}) collective-permute-start(bf16[384,2048]{1,0:T(8,128)(2,1)S(1)} %collective-permute-done.1.refs_0_), channel_id=1, source_target_pairs={{0,4},{4,0},{8,12},{12,8},{16,20},{20,16},{24,28},{28,24},{1,5},{5... | collective-permute-start | bytes 4718600 | tf_op jit(solution)/shard_map/ppermute | solution.py:19
  133.7 33.6 %collective-permute-start.21 = (bf16[384,1024]{1,0:T(8,128)(2,1)}, bf16[384,1024]{1,0:T(8,128)(2,1)S(1)}, u32[]{:S(2)}, u32[]{:S(2)}) collective-permute-start(bf16[384,1024]{1,0:T(8,128)(2,1)} %collective-permute-done.20), channel_id=1, source_target_pairs={{1,2},{5,6},{8,10},{12,14},{19,17},{23,21},{26,25},{30,29}} | collective-permute-start | bytes 2359304 | tf_op jit(solution)/shard_map/ppermute | solution.py:162
  135.0 38.8 %collective-permute-start.5 = (bf16[384,2048]{1,0:T(8,128)(2,1)}, bf16[384,2048]{1,0:T(8,128)(2,1)S(1)}, u32[]{:S(2)}, u32[]{:S(2)}) collective-permute-start(bf16[384,2048]{1,0:T(8,128)(2,1)} %collective-permute-done.4.refs_1_), channel_id=1, source_target_pairs={{0,4},{4,0},{8,12},{12,8},{16,20},{20,16},{24,28},{28,24},{1,5},{5... | collective-permute-start | bytes 4718600 | tf_op jit(solution)/shard_map/ppermute | solution.py:19
  172.5 36.6 %collective-permute-start.22 = (bf16[384,1024]{1,0:T(8,128)(2,1)S(1)}, bf16[384,1024]{1,0:T(8,128)(2,1)S(1)}, u32[]{:S(2)}, u32[]{:S(2)}) collective-permute-start(bf16[384,1024]{1,0:T(8,128)(2,1)S(1)} %collective-permute-done.21), channel_id=1, source_target_pairs={{2,3},{6,7},{10,11},{14,15},{17,16},{21,20},{25,24},{29,28}} | collective-permute-start | bytes 2359304 | tf_op jit(solution)/shard_map/ppermute | solution.py:162
  173.8 33.0 %collective-permute-start.24 = (bf16[384,1024]{1,0:T(8,128)(2,1)S(1)}, bf16[384,1024]{1,0:T(8,128)(2,1)}, u32[]{:S(2)}, u32[]{:S(2)}) collective-permute-start(bf16[384,1024]{1,0:T(8,128)(2,1)S(1)} %collective-permute-done.23), channel_id=1, source_target_pairs={{1,2},{5,6},{8,10},{12,14},{19,17},{23,21},{26,25},{30,29}} | collective-permute-start | bytes 2359304 | tf_op jit(solution)/shard_map/ppermute | solution.py:162
  184.7 25.0 %collective-permute-start.9 = (bf16[384,1024]{1,0:T(8,128)(2,1)S(1)}, bf16[384,1024]{1,0:T(8,128)(2,1)}, u32[]{:S(2)}, u32[]{:S(2)}) collective-permute-start(bf16[384,1024]{1,0:T(8,128)(2,1)S(1)} %constant_dynamic-slice_fusion.14), channel_id=1, source_target_pairs={{0,1},{4,5},{9,8},{13,12},{18,19},{22,23},{27,26},{31,30}} | collective-permute-start | bytes 2359304 | tf_op jit(solution)/shard_map/ppermute | solution.py:162
  188.2 35.5 %collective-permute-start.7 = (bf16[384,1024]{1,0:T(8,128)(2,1)}, bf16[384,1024]{1,0:T(8,128)(2,1)}, u32[]{:S(2)}, u32[]{:S(2)}) collective-permute-start(bf16[384,1024]{1,0:T(8,128)(2,1)} %collective-permute-done.6), channel_id=1, source_target_pairs={{1,2},{5,6},{8,10},{12,14},{19,17},{23,21},{26,25},{30,29}} | collective-permute-start | bytes 2359304 | tf_op jit(solution)/shard_map/ppermute | solution.py:162
  190.0 35.0 %collective-permute-start.31 = (bf16[384,1024]{1,0:T(8,128)(2,1)}, bf16[384,1024]{1,0:T(8,128)(2,1)}, u32[]{:S(2)}, u32[]{:S(2)}) collective-permute-start(bf16[384,1024]{1,0:T(8,128)(2,1)} %collective-permute-done.30), channel_id=1, source_target_pairs={{2,3},{6,7},{10,11},{14,15},{17,16},{21,20},{25,24},{29,28}} | collective-permute-start | bytes 2359304 | tf_op jit(solution)/shard_map/ppermute | solution.py:162
  206.9 28.5 %collective-permute-start.25 = (bf16[384,1024]{1,0:T(8,128)(2,1)}, bf16[384,1024]{1,0:T(8,128)(2,1)}, u32[]{:S(2)}, u32[]{:S(2)}) collective-permute-start(bf16[384,1024]{1,0:T(8,128)(2,1)} %collective-permute-done.24), channel_id=1, source_target_pairs={{2,3},{6,7},{10,11},{14,15},{17,16},{21,20},{25,24},{29,28}} | collective-permute-start | bytes 2359304 | tf_op jit(solution)/shard_map/ppermute | solution.py:162
  209.7 30.9 %collective-permute-start.10 = (bf16[384,1024]{1,0:T(8,128)(2,1)}, bf16[384,1024]{1,0:T(8,128)(2,1)}, u32[]{:S(2)}, u32[]{:S(2)}) collective-permute-start(bf16[384,1024]{1,0:T(8,128)(2,1)} %collective-permute-done.9), channel_id=1, source_target_pairs={{1,2},{5,6},{8,10},{12,14},{19,17},{23,21},{26,25},{30,29}} | collective-permute-start | bytes 2359304 | tf_op jit(solution)/shard_map/ppermute | solution.py:162
  223.7 40.3 %collective-permute-start.8 = (bf16[384,1024]{1,0:T(8,128)(2,1)}, bf16[384,1024]{1,0:T(8,128)(2,1)S(1)}, u32[]{:S(2)}, u32[]{:S(2)}) collective-permute-start(bf16[384,1024]{1,0:T(8,128)(2,1)} %collective-permute-done.7), channel_id=1, source_target_pairs={{2,3},{6,7},{10,11},{14,15},{17,16},{21,20},{25,24},{29,28}} | collective-permute-start | bytes 2359304 | tf_op jit(solution)/shard_map/ppermute | solution.py:162
  240.6 28.5 %collective-permute-start.11 = (bf16[384,1024]{1,0:T(8,128)(2,1)}, bf16[384,1024]{1,0:T(8,128)(2,1)S(1)}, u32[]{:S(2)}, u32[]{:S(2)}) collective-permute-start(bf16[384,1024]{1,0:T(8,128)(2,1)} %collective-permute-done.10), channel_id=1, source_target_pairs={{2,3},{6,7},{10,11},{14,15},{17,16},{21,20},{25,24},{29,28}} | collective-permute-start | bytes 2359304 | tf_op jit(solution)/shard_map/ppermute | solution.py:162
  (30 other events, 455.8 us)

commit v2 on v1

v2 whole, which is shorter than its diff:
```python
import functools

import jax
import jax.numpy as jnp
from jax import lax
from jax.experimental import pallas as pl
from jax.experimental.pallas import tpu as pltpu
from jax.sharding import PartitionSpec as P

COHORTS = 8
BLOCK = 96
HALF = 4
EPSILON = 1e-05
PARTS = 3
TABLE = 128


def swapped(block, distance):
    return lax.ppermute(
        block, "samp", [(i, i ^ distance) for i in range(lax.axis_size("samp"))]
    )


def hops(owner, count):
    if count == 4:
        low = owner < 2
        middle = 2 if low else 1
        ends = [p for p in range(4) if p not in (owner, middle)]
        ends.sort(reverse=low)
        return [(0, owner, middle)] + [(i + 1, middle, e) for i, e in enumerate(ends)]
    down, up = list(range(owner - 1, -1, -1)), list(range(owner + 1, count))
    visited = [owner] + (down + up if owner < count // 2 else up + down)
    return [(i, visited[i], visited[i + 1]) for i in range(count - 1)]


def split_parts(table):
    parts, rest = [], table
    for _ in range(PARTS):
        part = lax.reduce_precision(rest, exponent_bits=8, mantissa_bits=7)
        parts.append(part.astype(jnp.bfloat16))
        rest = rest - part
    used = PARTS * COHORTS
    parts.append(jnp.zeros((TABLE - used, table.shape[1]), jnp.bfloat16))
    return jnp.concatenate(parts, 0)


def sums_kernel(member_ref, dose_ref, sums_ref):
    member = member_ref[...]
    dose = dose_ref[...]
    wide = dose.astype(jnp.float32)
    square = wide * wide
    high = square.astype(jnp.bfloat16)
    low = (square - high.astype(jnp.float32)).astype(jnp.bfloat16)
    dot = functools.partial(jnp.dot, preferred_element_type=jnp.float32)
    sums_ref[:COHORTS, :] = dot(member, dose)[:COHORTS]
    sums_ref[COHORTS:, :] = (dot(member, high) + dot(member, low))[:COHORTS]


def cohort_sums(member, dose):
    rows, columns = dose.shape
    tile = min(512, columns)
    return pl.pallas_call(
        sums_kernel,
        grid=(columns // tile,),
        in_specs=[
            pl.BlockSpec((16, rows), lambda j: (0, 0)),
            pl.BlockSpec((rows, tile), lambda j: (0, j)),
        ],
        out_specs=pl.BlockSpec((2 * COHORTS, tile), lambda j: (0, j)),
        out_shape=jax.ShapeDtypeStruct((2 * COHORTS, columns), jnp.float32),
        cost_estimate=pl.CostEstimate(
            flops=6 * 16 * rows * columns, bytes_accessed=2 * rows * columns, transcendentals=0
        ),
        compiler_params=pltpu.CompilerParams(vmem_limit_bytes=24 * 2**20),
    )(member, dose)


def standardize_kernel(dose_ref, code_ref, mean_ref, scale_ref, out_ref):
    code = code_ref[...].astype(jnp.float32)
    lane = lax.broadcasted_iota(jnp.int32, code.shape, 1)
    cohort = jnp.where(lane < PARTS * COHORTS, lane % COHORTS, -1)
    hot = (code == cohort.astype(jnp.float32)).astype(jnp.float32).astype(jnp.bfloat16)
    dot = functools.partial(jnp.dot, preferred_element_type=jnp.float32)
    centered = dose_ref[...].astype(jnp.float32) - dot(hot, mean_ref[...])
    out_ref[...] = (centered * dot(hot, scale_ref[...])).astype(jnp.bfloat16)


def standardized(coded, tables):
    rows, width = coded.shape[0], coded.shape[1] - TABLE
    tile = min(512, width)
    by_tile = lambda height: pl.BlockSpec((height, tile), lambda j: (0, j))
    return pl.pallas_call(
        standardize_kernel,
        grid=(width // tile,),
        in_specs=[
            by_tile(rows),
            pl.BlockSpec((rows, TABLE), lambda j: (0, width // TABLE)),
            by_tile(TABLE),
            by_tile(TABLE),
        ],
        out_specs=by_tile(rows),
        out_shape=jax.ShapeDtypeStruct((rows, width), jnp.bfloat16),
        cost_estimate=pl.CostEstimate(
            flops=4 * TABLE * rows * width, bytes_accessed=4 * rows * width, transcendentals=0
        ),
        compiler_params=pltpu.CompilerParams(vmem_limit_bytes=24 * 2**20),
    )(coded, coded, *tables)


def gram_kernel(takes, row_sizes, row_counts, has_total, *refs):
    n = len(takes)
    role, cols, refs = refs[0][0], refs[1 : n + 1], refs[n + 1 :]
    rows = []
    for count in row_counts:
        rows.append(refs[:count])
        refs = refs[count:]
    total = refs[0] if has_total else None
    out, row_dose, row_ready, col_ready, sems = refs[-5:]
    depth = sum(row_sizes)

    @pl.when(pl.program_id(0) == 0)
    def _():
        at, waits = 0, []
        for j, (places, size) in enumerate(zip(rows, row_sizes)):
            to = row_dose.at[pl.ds(at, size), :]
            for i, place in enumerate(places):
                here = role == i if i < len(places) - 1 else role >= i

                @pl.when(here)
                def _():
                    pltpu.make_async_copy(place, to, sems.at[j]).start()

            waits.append(pltpu.make_async_copy(places[0], to, sems.at[j]))
            at += size
        for wait in waits:
            wait.wait()
        step = 128 if depth % 128 == 0 else depth
        for at in range(0, depth, step):
            row_ready[:, at : at + step] = row_dose[at : at + step, :].T

    at = 0
    for j, (start, size) in enumerate(takes):
        col_ready[at : at + size, :] = cols[j][start : start + size, :]
        at += size
    product = jnp.dot(row_ready[...], col_ready[...], preferred_element_type=jnp.float32)
    if has_total:
        product += total[...]
    out[...] = product


def gram(total, role, cols, rows):
    takes = tuple((start, size) for _, start, size in cols)
    blocks = [block for block, _, _ in cols]
    row_sizes = tuple(r[0].shape[0] for r in rows)
    depth, width, height = sum(row_sizes), blocks[0].shape[1], rows[0][0].shape[1]
    tile = min(512, width)
    by_tile = lambda height: pl.BlockSpec((height, tile), lambda j: (0, j))
    in_specs = (
        [pl.BlockSpec(memory_space=pltpu.SMEM)]
        + [by_tile(start + size) for start, size in takes]
        + [pl.BlockSpec(memory_space=pl.ANY) for r in rows for _ in r]
    )
    operands = [role, *blocks, *(part for r in rows for part in r)]
    aliases = {}
    if total is not None:
        aliases = {len(operands): 0}
        operands.append(total)
        in_specs.append(by_tile(height))
    return pl.pallas_call(
        functools.partial(
            gram_kernel, takes, row_sizes, tuple(len(r) for r in rows), total is not None
        ),
        grid=(width // tile,),
        in_specs=in_specs,
        out_specs=by_tile(height),
        out_shape=jax.ShapeDtypeStruct((height, width), jnp.float32),
        scratch_shapes=[
            pltpu.VMEM((depth, height), jnp.bfloat16),
            pltpu.VMEM((height, depth), jnp.bfloat16),
            pltpu.VMEM((depth, tile), jnp.bfloat16),
            pltpu.SemaphoreType.DMA((len(rows),)),
        ],
        input_output_aliases=aliases,
        cost_estimate=pl.CostEstimate(
            flops=2 * depth * height * width,
            bytes_accessed=8 * height * width + 2 * depth * (height + width),
            transcendentals=0,
        ),
        compiler_params=pltpu.CompilerParams(vmem_limit_bytes=48 * 2**20),
    )(*operands)


def gram_of(groups, role, at_once):
    total = None
    for at in range(0, len(groups), at_once):
        part = groups[at : at + at_once]
        cols = [c for g in part for c in g[0]]
        total = gram(total, role, cols, [r for g in part for r in g[1]])
    return total


def after(block, *done):
    return lax.optimization_barrier((block, *done))[0]


def shards(dosage, cohort, live_blocks, weight_counts):
    n_samp, n_var = lax.axis_size("samp"), lax.axis_size("var")
    samp, var = lax.axis_index("samp"), lax.axis_index("var")
    slots, width = dosage.shape
    height = width * n_var // n_samp
    kept = HALF * BLOCK
    owner = [i * height // width for i in range(n_samp)]
    owns_rows = samp * height // width == var
    lines = [hops(o, n_var) for o in owner]
    reached = [[0] * n_var for _ in range(n_samp)]
    for s, line in enumerate(lines):
        for step, _, end in line:
            reached[s][end] = step + 1
    here = (jnp.arange(n_samp)[:, None] == samp) & (jnp.arange(n_var)[None, :] == var)
    role = jnp.sum(jnp.where(here, jnp.asarray(reached, jnp.int32), 0)).reshape(1)
    row_start = samp * height % width
    early = BLOCK if (n_samp, n_var) == (8, 4) else 0
    bits = [n_samp >> (b + 1) for b in range(n_samp.bit_length() - 1)]
    def hop(block, step):
        pairs = [
            (s * n_var + line[step][1], s * n_var + line[step][2]) for s, line in enumerate(lines)
        ]
        return lax.ppermute(block, ("samp", "var"), pairs)

    def along_line(block, *done):
        got = []
        for step in range(n_var - 1):
            source = [k for k in range(step) if lines[0][k][2] == lines[0][step][1]]
            moving = got[source[0]] if source else block
            got.append(hop(after(moving, *done) if source and done else moving, step))
        return [block, *got]

    def along_var(block, shift):
        pairs = [(v, v + shift) for v in range(n_var) if 0 <= v + shift < n_var]
        return lax.ppermute(block, "var", pairs)

    def row_part(block, start, size):
        return lax.dynamic_slice(block, (start, row_start), (size, height))

    own_live = live_blocks[0]
    code = cohort.astype(jnp.bfloat16)
    coded = jnp.concatenate([dosage, jnp.broadcast_to(code[:, None], (slots, TABLE))], 1)

    position = lax.broadcasted_iota(jnp.int32, (16, slots), 1)
    label = lax.broadcasted_iota(jnp.int32, (16, slots), 0)
    member = (cohort[None, :] == label) & (position < own_live * BLOCK)
    counts = jnp.sum(member.astype(jnp.float32), axis=1, keepdims=True)
    sums = cohort_sums(member.astype(jnp.bfloat16), dosage)
    extra = [jnp.broadcast_to(counts, (2 * COHORTS, TABLE))]
    if early:
        row = lax.broadcasted_iota(jnp.int32, (2 * COHORTS, early), 0)
        slot_codes = jnp.where(row == samp, cohort[None, :early].astype(jnp.float32), 0.0)
        extra.append(jnp.pad(slot_codes, ((0, 0), (0, TABLE - early))))
    sums = jnp.concatenate([sums, *extra], 1)
    surplus = swapped(coded[kept:], bits[0])
    for bit in bits[1:]:
        sums = sums + swapped(sums, bit)
    sums = sums + swapped(after(sums, surplus), bits[0])
    below, above = [dosage[:early]], [dosage[:early]]
    if early:
        for _ in range(n_var - 1):
            below.append(along_var(below[-1], 1))
            above.append(along_var(above[-1], -1))

    sum_one, sum_two = sums[:COHORTS, :width], sums[COHORTS:, :width]
    cohort_size = sums[:COHORTS, width]
    cohort_mean = sum_one / cohort_size[:, None]
    cohort_var = sum_two / cohort_size[:, None] - cohort_mean * cohort_mean
    inv_spread = lax.rsqrt(cohort_var + EPSILON)
    counts_float = weight_counts.astype(jnp.float32)
    cohort_share = counts_float / jnp.sum(counts_float)
    multiplier = inv_spread * jnp.sqrt(cohort_share / cohort_size)[:, None]
    tables = [split_parts(cohort_mean), split_parts(multiplier)]

    offset = own_live * BLOCK
    placed = lax.dynamic_update_slice_in_dim(jnp.zeros_like(coded), surplus, offset, 0)
    row_index = lax.broadcasted_iota(jnp.int32, (kept, 1), 0)
    balanced = jnp.where(row_index < offset, coded[:kept], placed[:kept])
    if early:
        balanced = after(balanced, below[2], above[2])
    base = standardized(balanced, tables)
    if not early:
        pieces = {0: base}
        for bit in bits:
            pieces |= {m ^ bit: swapped(block, bit) for m, block in pieces.items()}
        groups = []
        for m in range(0, n_samp, 2):
            cols = [(pieces[i], 0, kept) for i in (m, m + 1)]
            rows = along_line(jnp.concatenate([row_part(p, 0, kept) for p, _, _ in cols], 0))
            if n_var > 4:
                rows = [rows[0], sum(rows[2:], rows[1])]
            groups.append((cols, [rows]))
        return gram_of(groups, role, 3)

    def of_panel(panel):
        chosen = jnp.zeros_like(below[0])
        for h in range(1, n_var):
            chosen += jnp.where(panel == var - h, below[h], jnp.zeros_like(below[h]))
            chosen += jnp.where(panel == var + h, above[h], jnp.zeros_like(above[h]))
        return chosen

    chip = samp // 2
    far, near, both = 4, 2, 6
    size, used = kept - early, PARTS * COHORTS
    rest = lambda m: pieces[m][early:]
    panel = lambda got: jnp.where(owns_rows, got[0], sum(got[2:], got[1]))
    other_half = lambda block: lax.dynamic_slice_in_dim(block, height - row_start, height, 1)
    my_half = lambda block: row_part(block, 0, block.shape[0])

    pieces = {0: base}
    pieces[far], pieces[near] = swapped(base, far), swapped(base, near)
    first = jnp.concatenate([rest(0), *(t[:used] for t in tables)], 0)
    legs = [along_line(first)]
    pieces[1] = swapped(base, 1)
    legs.append(along_line(after(rest(near), pieces[1], below[3], above[3])))
    pieces[both] = swapped(after(pieces[far], pieces[near], legs[0][1]), near)
    legs.append(along_line(after(rest(far), legs[0][1])))
    up = jnp.concatenate([of_panel(chip ^ 2), of_panel(chip ^ 3)], 0)
    up = swapped(after(up, legs[1][1]), far)
    pieces[both + 1] = swapped(after(pieces[both], *legs[0][2:], legs[1][1]), 1)
    done = (legs[2][1], *legs[1][2:])
    tail = [row_part(pieces[m], early, size) for m in (both, both + 1)]
    legs.append(along_line(after(tail[0], *done), *legs[2][2:]))
    legs.append(along_line(after(tail[1], *done), *legs[2][2:], *legs[3][2:]))
    aside = jnp.concatenate([of_panel(chip ^ 1), up[early:]], 0)
    aside = swapped(after(aside, *done), near)
    brought = jnp.concatenate([of_panel(chip), aside[:early], up[:early], aside[early:]], 0)
    other = swapped(brought, 1)
    pieces[far + 1] = swapped(after(pieces[far], pieces[both + 1]), 1)
    pieces[near + 1] = swapped(after(pieces[near], pieces[far + 1]), 1)
    whole = [panel([part[:size] for part in leg]) for leg in legs[:3]]
    others = [swapped(other_half(block), 1) for block in whole]

    row_tables = my_half(panel([part[size:] for part in legs[0]]))
    pad = jnp.zeros((TABLE - used, height), jnp.bfloat16)
    row_tables = [jnp.concatenate([row_tables[i : i + used], pad], 0) for i in (0, used)]
    order = [*range(0, n_samp, 2), *range(1, n_samp, 2)]
    source = samp ^ jnp.asarray(order, jnp.int32)
    pick = (source[:, None] == jnp.arange(n_samp)[None, :]).astype(jnp.float32)
    early_codes = jnp.dot(pick, sums[:n_samp, width + TABLE : width + TABLE + early])
    lanes = jnp.broadcast_to(early_codes.reshape(-1, 1), (n_samp * early, TABLE))
    brought = jnp.concatenate([my_half(brought), my_half(other)], 0)
    brought = standardized(jnp.concatenate([brought, lanes.astype(jnp.bfloat16)], 1), row_tables)
    own = jnp.concatenate([row_part(pieces[m], 0, early) for m in order], 0)

    cols = lambda *ms: [(pieces[m], early, size) for m in ms]
    groups = [([(pieces[m], 0, early) for m in order], [[own, brought]])]
    groups += [
        (cols(i, i + 1), [[my_half(block)], [other]])
        for i, block, other in zip((0, near, far), whole, others)
    ]
    groups.append((cols(both, both + 1), legs[3:]))
    return gram_of(groups, role, 3)


def solution(mesh):
    placed = (P("samp", "var"), P("samp"), P("samp"), P())
    return jax.shard_map(
        shards, mesh=mesh, in_specs=placed, out_specs=P("samp", "var"), check_vma=False
    )
```

time: 287 us -> 233 us (0.81); the launches traced: 282 us -> 232 us
  waiting for transfers between devices: 107 us -> 76.9 us
  starting transfers between devices: 55.3 us -> 80.3 us
  blocking collectives: 22.3 us -> 0 us
  local copies, waits for them, and re-layouts: 34.4 us -> 21.8 us
  Pallas kernels: 44.4 us -> 34.7 us
    ppermute x27 -> x21, waiting for transfers between devices: 100 us -> 63.4 us  [the longest x15 58.1 us: hop(): return lax.ppermute(block, ('samp', 'var'), pairs)]
    ppermute x11 -> x17, starting transfers between devices: 15 us -> 38.4 us  [swapped(): lax.ppermute(block, 'samp', [(i, i ^ distance) for i in range(lax.axis_si...]
    unnamed x1 -> x0, blocking collectives: 22.3 us -> none
    gather x4 -> x0, local copies, waits for them, and re-layouts: 19.7 us -> none  [the longest x3 19.1 us: shards(): jnp.take_along_axis(partner, jnp.clip(moved_from, 0, slots - 1), axis=1)]
    pallas_call x4, Pallas kernels: 42.3 us -> 32.6 us  [the longest x2 29.2 us: gram(): pl.pallas_call(functools.partial(gram_kernel, takes, row_sizes, tuple((le...]
    ppermute x11 -> x17, waiting for transfers between devices: 6.54 us -> 13.5 us  [swapped(): lax.ppermute(block, 'samp', [(i, i ^ distance) for i in range(lax.axis_si...]
    select_n x12 -> x5, other arithmetic: 11.7 us -> 5.04 us  [the longest x3 4.51 us: shards(): panel = lambda got: jnp.where(owns_rows, got[0], sum(got[2:], got[1]))]
    dynamic_slice x10 -> x7, local copies, waits for them, and re-layouts: 7.94 us -> 1.58 us  [the longest x4 1.3 us: row_part(): return lax.dynamic_slice(block, (start, row_start), (size, height))]
  transfers between devices with their start and end apart: 38 -> 38, of which waited for: 16 -> 14; matrix products, arithmetic and copies ran while one was open for 15% -> 11% of each run, Pallas kernels for 12% -> 8%
where the time goes in v2:
time: 233 us; the launch traced here: 232 us
  starting transfers between devices  80.3 us (34%)
  waiting for transfers between devices  76.9 us (33%)
  Pallas kernels  34.7 us (15%)
  local copies, waits for them, and re-layouts  21.8 us (9%)
  other arithmetic  15.5 us (7%)
    ppermute x15, waiting for transfers between devices, hop(): return lax.ppermute(block, ('samp', 'var'), pairs)  58.1 us
    ppermute x17, starting transfers between devices, swapped(): lax.ppermute(block, 'samp', [(i, i ^ distance) for i in range(lax.axis_si...  38.4 us
    pallas_call x2, Pallas kernels, gram(): pl.pallas_call(functools.partial(gram_kernel, takes, row_sizes, tuple((le...  29.2 us
    ppermute x15, starting transfers between devices, hop(): return lax.ppermute(block, ('samp', 'var'), pairs)  25.7 us
    ppermute x6, starting transfers between devices, along_var(): return lax.ppermute(block, 'var', pairs)  16.2 us
    ppermute x17, waiting for transfers between devices, swapped(): lax.ppermute(block, 'samp', [(i, i ^ distance) for i in range(lax.axis_si...  13.5 us
    unnamed x65, local copies, waits for them, and re-layouts  9.73 us
    ppermute x6, waiting for transfers between devices, along_var(): return lax.ppermute(block, 'var', pairs)  5.29 us
  transfers between devices with their start and end apart: 38, of which 14 were waited for; matrix products, arithmetic and copies ran while one was open for 11% of the time, Pallas kernels for 8%

profile of v2, /device:TPU:15, one launch (start us, length us, event | category | flops | bytes accessed | tf_op | source)
XLA Modules:
  0.0 231.8 jit_solution(5274737220551090471)
XLA Ops:
  0.9 2.6 %pad_maximum_fusion.2 = bf16[288,2176]{1,0:T(8,128)(2,1)} fusion(bf16[672,128]{1,0:T(8,128)(2,1)S(1)} %broadcast_in_dim.34, bf16[672,2048]{1,0:T(8,128)(2,1)} %dose_ref.1), kind=kLoop, calls=%fused_computation.6 | loop fusion | flops 2506752 | bytes 4177920 | tf_op jit(solution)/shard_map/concatenate | solution.py:247
  9.9 3.4 %collective-permute-start.1 = (bf16[96,2048]{1,0:T(8,128)(2,1)}, bf16[96,2048]{1,0:T(8,128)(2,1)S(1)}, u32[]{:S(2)}, u32[]{:S(2)}) collective-permute-start(bf16[96,2048]{1,0:T(8,128)(2,1)} %slice.82), channel_id=1, source_target_pairs={{0,1},{1,2},{2,3},{4,5},{5,6},{6,7},{8,9},{9,10},{10,11},{12,13},{... | collective-permute-start | bytes 1179656 | tf_op jit(solution)/shard_map/ppermute | solution.py:240
  21.8 3.1 %collective-permute-start.2 = (bf16[96,2048]{1,0:T(8,128)(2,1)S(1)}, bf16[96,2048]{1,0:T(8,128)(2,1)S(1)}, u32[]{:S(2)}, u32[]{:S(2)}) collective-permute-start(bf16[96,2048]{1,0:T(8,128)(2,1)S(1)} %collective-permute-done.1), channel_id=1, source_target_pairs={{0,1},{1,2},{2,3},{4,5},{5,6},{6,7},{8,9},{9,10},{10,11},{12,13},{... | collective-permute-start | bytes 1179656 | tf_op jit(solution)/shard_map/ppermute | solution.py:240
  24.8 7.3 %collective-permute-done = bf16[288,2176]{1,0:T(8,128)(2,1)} collective-permute-done((bf16[288,2176]{1,0:T(8,128)(2,1)}, bf16[288,2176]{1,0:T(8,128)(2,1)}, u32[]{:S(2)}, u32[]{:S(2)}) %collective-permute-start) | collective-permute-done | bytes 1253408 | tf_op jit(solution)/shard_map/ppermute | solution.py:19
  46.0 3.0 %collective-permute-start.14 = (bf16[384,2048]{1,0:T(8,128)(2,1)S(1)}, bf16[384,2048]{1,0:T(8,128)(2,1)}, u32[]{:S(2)}, u32[]{:S(2)}) collective-permute-start(bf16[384,2048]{1,0:T(8,128)(2,1)S(1)} %shard_map.65.refs_1_.refs_9_), channel_id=1, source_target_pairs={{0,4},{4,0},{8,12},{12,8},{16,20},{20,16},{24,28},{28,24},{1,5},{5... | collective-permute-start | bytes 4718600 | tf_op jit(solution)/shard_map/ppermute | solution.py:19
  49.0 2.9 %collective-permute-start.8 = (bf16[384,2048]{1,0:T(8,128)(2,1)S(1)}, bf16[384,2048]{1,0:T(8,128)(2,1)}, u32[]{:S(2)}, u32[]{:S(2)}) collective-permute-start(bf16[384,2048]{1,0:T(8,128)(2,1)S(1)} %shard_map.65.refs_1_.refs_9_), channel_id=1, source_target_pairs={{0,16},{4,20},{8,24},{12,28},{16,0},{20,4},{24,8},{28,12},{1,17},{... | collective-permute-start | bytes 4718600 | tf_op jit(solution)/shard_map/ppermute | solution.py:19
  51.9 3.7 %collective-permute-start.16 = (bf16[96,2048]{1,0:T(8,128)(2,1)}, bf16[96,2048]{1,0:T(8,128)(2,1)S(1)}, u32[]{:S(2)}, u32[]{:S(2)}) collective-permute-start(bf16[96,2048]{1,0:T(8,128)(2,1)} %copy-done.13), channel_id=1, source_target_pairs={{1,0},{2,1},{3,2},{5,4},{6,5},{7,6},{9,8},{10,9},{11,10},{13,12},{... | collective-permute-start | bytes 1179656 | tf_op jit(solution)/shard_map/ppermute | solution.py:240
  55.7 20.9 %collective-permute-done.10 = bf16[336,2048]{1,0:T(8,128)(2,1)} collective-permute-done((bf16[336,2048]{1,0:T(8,128)(2,1)}, bf16[336,2048]{1,0:T(8,128)(2,1)}, u32[]{:S(2)}, u32[]{:S(2)}) %collective-permute-start.10) | collective-permute-done | bytes 1376288 | tf_op jit(solution)/shard_map/ppermute | solution.py:228
  79.0 4.9 %collective-permute-start.13 = (bf16[336,2048]{1,0:T(8,128)(2,1)}, bf16[336,2048]{1,0:T(8,128)(2,1)}, u32[]{:S(2)}, u32[]{:S(2)}) collective-permute-start(bf16[336,2048]{1,0:T(8,128)(2,1)} %collective-permute-done.10), channel_id=1, source_target_pairs={{2,1},{6,5},{10,8},{14,12},{17,19},{21,23},{25,26},{29,30}} | collective-permute-start | bytes 4128776 | tf_op jit(solution)/shard_map/ppermute | solution.py:228
  84.1 3.8 %collective-permute-done.16 = bf16[96,2048]{1,0:T(8,128)(2,1)S(1)} collective-permute-done((bf16[96,2048]{1,0:T(8,128)(2,1)}, bf16[96,2048]{1,0:T(8,128)(2,1)S(1)}, u32[]{:S(2)}, u32[]{:S(2)}) %collective-permute-start.16) | collective-permute-done | bytes 393248 | tf_op jit(solution)/shard_map/ppermute | solution.py:240
  88.0 2.4 %collective-permute-start.12 = (bf16[336,2048]{1,0:T(8,128)(2,1)}, bf16[336,2048]{1,0:T(8,128)(2,1)}, u32[]{:S(2)}, u32[]{:S(2)}) collective-permute-start(bf16[336,2048]{1,0:T(8,128)(2,1)} %collective-permute-done.10), channel_id=1, source_target_pairs={{2,3},{6,7},{10,11},{14,15},{17,16},{21,20},{25,24},{29,28}} | collective-permute-start | bytes 4128776 | tf_op jit(solution)/shard_map/ppermute | solution.py:228
  92.9 2.5 %slice.111 = bf16[288,2048]{1,0:T(8,128)(2,1)} slice(bf16[384,2048]{1,0:T(8,128)(2,1)} %collective-permute-done.8.refs_3_.refs_1_), slice={[96:384], [0:2048]} | slice | bytes 2359296 | tf_op jit(solution)/shard_map/slice | solution.py:310
  97.9 18.1 %collective-permute-done.17 = bf16[288,2048]{1,0:T(8,128)(2,1)} collective-permute-done((bf16[288,2048]{1,0:T(8,128)(2,1)S(1)}, bf16[288,2048]{1,0:T(8,128)(2,1)}, u32[]{:S(2)}, u32[]{:S(2)}) %collective-permute-start.17) | collective-permute-done | bytes 1179680 | tf_op jit(solution)/shard_map/ppermute | solution.py:228
  123.2 9.4 %collective-permute-start.18 = (bf16[384,2048]{1,0:T(8,128)(2,1)}, bf16[384,2048]{1,0:T(8,128)(2,1)S(1)}, u32[]{:S(2)}, u32[]{:S(2)}) collective-permute-start(bf16[384,2048]{1,0:T(8,128)(2,1)} %collective-permute-done.11.refs_4_.refs_3_), channel_id=1, source_target_pairs={{0,4},{4,0},{8,12},{12,8},{16,20},{20,16},{24,28},{28,24},{1,5},{5... | collective-permute-start | bytes 4718600 | tf_op jit(solution)/shard_map/ppermute | solution.py:19
  133.6 7.6 %collective-permute-done.20 = bf16[288,2048]{1,0:T(8,128)(2,1)} collective-permute-done((bf16[288,2048]{1,0:T(8,128)(2,1)}, bf16[288,2048]{1,0:T(8,128)(2,1)}, u32[]{:S(2)}, u32[]{:S(2)}) %collective-permute-start.20) | collective-permute-done | bytes 1179680 | tf_op jit(solution)/shard_map/ppermute | solution.py:228
  149.6 6.0 %collective-permute-start.19 = (bf16[384,2048]{1,0:T(8,128)(2,1)}, bf16[384,2048]{1,0:T(8,128)(2,1)S(1)}, u32[]{:S(2)}, u32[]{:S(2)}) collective-permute-start(bf16[384,2048]{1,0:T(8,128)(2,1)} %collective-permute-done.8.refs_3_.refs_1_), channel_id=1, source_target_pairs={{0,4},{4,0},{8,12},{12,8},{16,20},{20,16},{24,28},{28,24},{1,5},{5... | collective-permute-start | bytes 4718600 | tf_op jit(solution)/shard_map/ppermute | solution.py:19
  158.0 2.7 %collective-permute-done.34 = bf16[192,2048]{1,0:T(8,128)(2,1)S(1)} collective-permute-done((bf16[192,2048]{1,0:T(8,128)(2,1)S(1)}, bf16[192,2048]{1,0:T(8,128)(2,1)S(1)}, u32[]{:S(2)}, u32[]{:S(2)}) %collective-permute-start.34) | collective-permute-done | bytes 786464 | tf_op jit(solution)/shard_map/ppermute | solution.py:19
  161.0 6.7 %collective-permute-start.35 = (bf16[384,2048]{1,0:T(8,128)(2,1)S(1)}, bf16[384,2048]{1,0:T(8,128)(2,1)S(1)}, u32[]{:S(2)}, u32[]{:S(2)}) collective-permute-start(bf16[384,2048]{1,0:T(8,128)(2,1)S(1)} %pad_maximum_fusion.1), channel_id=1, source_target_pairs={{0,4},{4,0},{8,12},{12,8},{16,20},{20,16},{24,28},{28,24},{1,5},{5... | collective-permute-start | bytes 4718600 | tf_op jit(solution)/shard_map/ppermute | solution.py:19
  169.8 4.2 %collective-permute-done.26.refs_8_ = bf16[288,1024]{1,0:T(8,128)(2,1)S(1)} collective-permute-done((bf16[288,1024]{1,0:T(8,128)(2,1)S(1)}, bf16[288,1024]{1,0:T(8,128)(2,1)S(1)}, u32[]{:S(2)}, u32[]{:S(2)}) %collective-permute-start.26) | collective-permute-done | bytes 589856 | tf_op jit(solution)/shard_map/ppermute | solution.py:228
  182.2 4.7 %collective-permute-done.28.refs_10_ = bf16[288,1024]{1,0:T(8,128)(2,1)S(1)} collective-permute-done((bf16[288,1024]{1,0:T(8,128)(2,1)S(1)}, bf16[288,1024]{1,0:T(8,128)(2,1)S(1)}, u32[]{:S(2)}, u32[]{:S(2)}) %collective-permute-start.28) | collective-permute-done | bytes 589856 | tf_op jit(solution)/shard_map/ppermute | solution.py:228
  190.1 2.6 %collective-permute-done.29.refs_12_ = bf16[288,1024]{1,0:T(8,128)(2,1)S(1)} collective-permute-done((bf16[288,1024]{1,0:T(8,128)(2,1)S(1)}, bf16[288,1024]{1,0:T(8,128)(2,1)S(1)}, u32[]{:S(2)}, u32[]{:S(2)}) %collective-permute-start.29) | collective-permute-done | bytes 589856 | tf_op jit(solution)/shard_map/ppermute | solution.py:228
  192.8 2.5 %collective-permute-start.23 = (bf16[288,1024]{1,0:T(8,128)(2,1)S(1)}, bf16[288,1024]{1,0:T(8,128)(2,1)S(1)}, u32[]{:S(2)}, u32[]{:S(2)}) collective-permute-start(bf16[288,1024]{1,0:T(8,128)(2,1)S(1)} %get-tuple-element.54), channel_id=1, source_target_pairs={{0,4},{4,0},{8,12},{12,8},{16,20},{20,16},{24,28},{28,24},{1,5},{5... | collective-permute-start | bytes 1769480 | tf_op jit(solution)/shard_map/ppermute | solution.py:19
  202.5 15.6 %shard_map.67.refs_15_ = f32[1024,2048]{1,0:T(8,128)} custom-call(s32[1]{0:T(128)} %bitcast.refs_0_, bf16[384,2048]{1,0:T(8,128)(2,1)S(1)} %shard_map.65.refs_1_.refs_9_, bf16[384,2048]{1,0:T(8,128)(2,1)S(1)} %collective-permute-done.9.refs_2_.refs_11_, bf16[384,2048]{1,0:T(8,128)(2,1)} %collective-permute-done.8.refs_3_.refs_1_, ...), custom_call_target="tpu_custom_call" | custom-call | flops 8053063680 | bytes 28573696 | tf_op jit(solution)/shard_map/pallas_call | solution.py:169
  218.2 13.5 %shard_map.68 = f32[1024,2048]{1,0:T(8,128)} custom-call(s32[1]{0:T(128)} %bitcast.refs_0_, bf16[384,2048]{1,0:T(8,128)(2,1)} %collective-permute-done.8.refs_3_.refs_1_, bf16[384,2048]{1,0:T(8,128)(2,1)} %copy-done.4, bf16[384,2048]{1,0:T(8,128)(2,1)} %collective-permute-done.11.refs_4_.refs_3_, ...), custom_call_target="tpu_custom_call", output_to_operand_aliasing={{}: (15, {})} | custom-call | flops 4831838208 | bytes 23855104 | tf_op jit(solution)/shard_map/pallas_call | solution.py:169
  (188 shorter events, 75.9 us)
Async XLA Ops:
  3.5 28.7 %collective-permute-start = (bf16[288,2176]{1,0:T(8,128)(2,1)}, bf16[288,2176]{1,0:T(8,128)(2,1)}, u32[]{:S(2)}, u32[]{:S(2)}) collective-permute-start(bf16[288,2176]{1,0:T(8,128)(2,1)} %pad_maximum_fusion.2), channel_id=1, source_target_pairs={{0,16},{4,20},{8,24},{12,28},{16,0},{20,4},{24,8},{28,12},{1,17},{... | collective-permute-start | bytes 3760136 | tf_op jit(solution)/shard_map/ppermute | solution.py:19
  44.4 32.1 %collective-permute-start.10 = (bf16[336,2048]{1,0:T(8,128)(2,1)}, bf16[336,2048]{1,0:T(8,128)(2,1)}, u32[]{:S(2)}, u32[]{:S(2)}) collective-permute-start(bf16[336,2048]{1,0:T(8,128)(2,1)} %constant_dynamic-update-slice_fusion), channel_id=1, source_target_pairs={{0,2},{4,6},{9,10},{13,14},{18,17},{22,21},{27,25},{31,29}} | collective-permute-start | bytes 4128776 | tf_op jit(solution)/shard_map/ppermute | solution.py:228
  45.7 33.4 %collective-permute-start.9 = (bf16[384,2048]{1,0:T(8,128)(2,1)S(1)}, bf16[384,2048]{1,0:T(8,128)(2,1)S(1)}, u32[]{:S(2)}, u32[]{:S(2)}) collective-permute-start(bf16[384,2048]{1,0:T(8,128)(2,1)S(1)} %shard_map.65.refs_1_.refs_9_), channel_id=1, source_target_pairs={{0,8},{4,12},{8,0},{12,4},{16,24},{20,28},{24,16},{28,20},{1,9},{5... | collective-permute-start | bytes 4718600 | tf_op jit(solution)/shard_map/ppermute | solution.py:19
  46.0 44.4 %collective-permute-start.14 = (bf16[384,2048]{1,0:T(8,128)(2,1)S(1)}, bf16[384,2048]{1,0:T(8,128)(2,1)}, u32[]{:S(2)}, u32[]{:S(2)}) collective-permute-start(bf16[384,2048]{1,0:T(8,128)(2,1)S(1)} %shard_map.65.refs_1_.refs_9_), channel_id=1, source_target_pairs={{0,4},{4,0},{8,12},{12,8},{16,20},{20,16},{24,28},{28,24},{1,5},{5... | collective-permute-start | bytes 4718600 | tf_op jit(solution)/shard_map/ppermute | solution.py:19
  49.0 42.7 %collective-permute-start.8 = (bf16[384,2048]{1,0:T(8,128)(2,1)S(1)}, bf16[384,2048]{1,0:T(8,128)(2,1)}, u32[]{:S(2)}, u32[]{:S(2)}) collective-permute-start(bf16[384,2048]{1,0:T(8,128)(2,1)S(1)} %shard_map.65.refs_1_.refs_9_), channel_id=1, source_target_pairs={{0,16},{4,20},{8,24},{12,28},{16,0},{20,4},{24,8},{28,12},{1,17},{... | collective-permute-start | bytes 4718600 | tf_op jit(solution)/shard_map/ppermute | solution.py:19
  51.9 36.0 %collective-permute-start.16 = (bf16[96,2048]{1,0:T(8,128)(2,1)}, bf16[96,2048]{1,0:T(8,128)(2,1)S(1)}, u32[]{:S(2)}, u32[]{:S(2)}) collective-permute-start(bf16[96,2048]{1,0:T(8,128)(2,1)} %copy-done.13), channel_id=1, source_target_pairs={{1,0},{2,1},{3,2},{5,4},{6,5},{7,6},{9,8},{10,9},{11,10},{13,12},{... | collective-permute-start | bytes 1179656 | tf_op jit(solution)/shard_map/ppermute | solution.py:240
  79.0 38.7 %collective-permute-start.13 = (bf16[336,2048]{1,0:T(8,128)(2,1)}, bf16[336,2048]{1,0:T(8,128)(2,1)}, u32[]{:S(2)}, u32[]{:S(2)}) collective-permute-start(bf16[336,2048]{1,0:T(8,128)(2,1)} %collective-permute-done.10), channel_id=1, source_target_pairs={{2,1},{6,5},{10,8},{14,12},{17,19},{21,23},{25,26},{29,30}} | collective-permute-start | bytes 4128776 | tf_op jit(solution)/shard_map/ppermute | solution.py:228
  88.0 31.4 %collective-permute-start.12 = (bf16[336,2048]{1,0:T(8,128)(2,1)}, bf16[336,2048]{1,0:T(8,128)(2,1)}, u32[]{:S(2)}, u32[]{:S(2)}) collective-permute-start(bf16[336,2048]{1,0:T(8,128)(2,1)} %collective-permute-done.10), channel_id=1, source_target_pairs={{2,3},{6,7},{10,11},{14,15},{17,16},{21,20},{25,24},{29,28}} | collective-permute-start | bytes 4128776 | tf_op jit(solution)/shard_map/ppermute | solution.py:228
  90.4 25.6 %collective-permute-start.17 = (bf16[288,2048]{1,0:T(8,128)(2,1)S(1)}, bf16[288,2048]{1,0:T(8,128)(2,1)}, u32[]{:S(2)}, u32[]{:S(2)}) collective-permute-start(bf16[288,2048]{1,0:T(8,128)(2,1)S(1)} %slice.110), channel_id=1, source_target_pairs={{0,2},{4,6},{9,10},{13,14},{18,17},{22,21},{27,25},{31,29}} | collective-permute-start | bytes 3538952 | tf_op jit(solution)/shard_map/ppermute | solution.py:228
  91.7 31.5 %collective-permute-start.11 = (bf16[384,2048]{1,0:T(8,128)(2,1)}, bf16[384,2048]{1,0:T(8,128)(2,1)}, u32[]{:S(2)}, u32[]{:S(2)}) collective-permute-start(bf16[384,2048]{1,0:T(8,128)(2,1)} %collective-permute-done.8.refs_3_.refs_1_), channel_id=1, source_target_pairs={{0,8},{4,12},{8,0},{12,4},{16,24},{20,28},{24,16},{28,20},{1,9},{5... | collective-permute-start | bytes 4718600 | tf_op jit(solution)/shard_map/ppermute | solution.py:19
  95.3 45.9 %collective-permute-start.20 = (bf16[288,2048]{1,0:T(8,128)(2,1)}, bf16[288,2048]{1,0:T(8,128)(2,1)}, u32[]{:S(2)}, u32[]{:S(2)}) collective-permute-start(bf16[288,2048]{1,0:T(8,128)(2,1)} %slice.111), channel_id=1, source_target_pairs={{0,2},{4,6},{9,10},{13,14},{18,17},{22,21},{27,25},{31,29}} | collective-permute-start | bytes 3538952 | tf_op jit(solution)/shard_map/ppermute | solution.py:228
  116.0 28.6 %collective-permute-start.33 = (bf16[192,2048]{1,0:T(8,128)(2,1)}, bf16[192,2048]{1,0:T(8,128)(2,1)}, u32[]{:S(2)}, u32[]{:S(2)}) collective-permute-start(bf16[192,2048]{1,0:T(8,128)(2,1)} %pad_maximum_fusion.3), channel_id=1, source_target_pairs={{0,16},{4,20},{8,24},{12,28},{16,0},{20,4},{24,8},{28,12},{1,17},{... | collective-permute-start | bytes 2359304 | tf_op jit(solution)/shard_map/ppermute | solution.py:19
  117.7 29.5 %collective-permute-start.25 = (bf16[288,2048]{1,0:T(8,128)(2,1)}, bf16[288,2048]{1,0:T(8,128)(2,1)S(1)}, u32[]{:S(2)}, u32[]{:S(2)}) collective-permute-start(bf16[288,2048]{1,0:T(8,128)(2,1)} %collective-permute-done.17), channel_id=1, source_target_pairs={{2,1},{6,5},{10,8},{14,12},{17,19},{21,23},{25,26},{29,30}} | collective-permute-start | bytes 3538952 | tf_op jit(solution)/shard_map/ppermute | solution.py:228
  119.4 27.9 %collective-permute-start.24 = (bf16[288,2048]{1,0:T(8,128)(2,1)}, bf16[288,2048]{1,0:T(8,128)(2,1)S(1)}, u32[]{:S(2)}, u32[]{:S(2)}) collective-permute-start(bf16[288,2048]{1,0:T(8,128)(2,1)} %collective-permute-done.17), channel_id=1, source_target_pairs={{2,3},{6,7},{10,11},{14,15},{17,16},{21,20},{25,24},{29,28}} | collective-permute-start | bytes 3538952 | tf_op jit(solution)/shard_map/ppermute | solution.py:228
  123.2 26.4 %collective-permute-start.18 = (bf16[384,2048]{1,0:T(8,128)(2,1)}, bf16[384,2048]{1,0:T(8,128)(2,1)S(1)}, u32[]{:S(2)}, u32[]{:S(2)}) collective-permute-start(bf16[384,2048]{1,0:T(8,128)(2,1)} %collective-permute-done.11.refs_4_.refs_3_), channel_id=1, source_target_pairs={{0,4},{4,0},{8,12},{12,8},{16,20},{20,16},{24,28},{28,24},{1,5},{5... | collective-permute-start | bytes 4718600 | tf_op jit(solution)/shard_map/ppermute | solution.py:19
  141.3 28.5 %collective-permute-start.22 = (bf16[288,2048]{1,0:T(8,128)(2,1)}, bf16[288,2048]{1,0:T(8,128)(2,1)S(1)}, u32[]{:S(2)}, u32[]{:S(2)}) collective-permute-start(bf16[288,2048]{1,0:T(8,128)(2,1)} %collective-permute-done.20), channel_id=1, source_target_pairs={{2,1},{6,5},{10,8},{14,12},{17,19},{21,23},{25,26},{29,30}} | collective-permute-start | bytes 3538952 | tf_op jit(solution)/shard_map/ppermute | solution.py:228
  144.6 25.2 %collective-permute-start.21 = (bf16[288,2048]{1,0:T(8,128)(2,1)}, bf16[288,2048]{1,0:T(8,128)(2,1)S(1)}, u32[]{:S(2)}, u32[]{:S(2)}) collective-permute-start(bf16[288,2048]{1,0:T(8,128)(2,1)} %collective-permute-done.20), channel_id=1, source_target_pairs={{2,3},{6,7},{10,11},{14,15},{17,16},{21,20},{25,24},{29,28}} | collective-permute-start | bytes 3538952 | tf_op jit(solution)/shard_map/ppermute | solution.py:228
  149.6 28.4 %collective-permute-start.19 = (bf16[384,2048]{1,0:T(8,128)(2,1)}, bf16[384,2048]{1,0:T(8,128)(2,1)S(1)}, u32[]{:S(2)}, u32[]{:S(2)}) collective-permute-start(bf16[384,2048]{1,0:T(8,128)(2,1)} %collective-permute-done.8.refs_3_.refs_1_), channel_id=1, source_target_pairs={{0,4},{4,0},{8,12},{12,8},{16,20},{20,16},{24,28},{28,24},{1,5},{5... | collective-permute-start | bytes 4718600 | tf_op jit(solution)/shard_map/ppermute | solution.py:19
  156.7 17.3 %collective-permute-start.26 = (bf16[288,1024]{1,0:T(8,128)(2,1)S(1)}, bf16[288,1024]{1,0:T(8,128)(2,1)S(1)}, u32[]{:S(2)}, u32[]{:S(2)}) collective-permute-start(bf16[288,1024]{1,0:T(8,128)(2,1)S(1)} %constant_dynamic-slice_fusion.9.refs_7_), channel_id=1, source_target_pairs={{0,2},{4,6},{9,10},{13,14},{18,17},{22,21},{27,25},{31,29}} | collective-permute-start | bytes 1769480 | tf_op jit(solution)/shard_map/ppermute | solution.py:228
  161.0 34.3 %collective-permute-start.35 = (bf16[384,2048]{1,0:T(8,128)(2,1)S(1)}, bf16[384,2048]{1,0:T(8,128)(2,1)S(1)}, u32[]{:S(2)}, u32[]{:S(2)}) collective-permute-start(bf16[384,2048]{1,0:T(8,128)(2,1)S(1)} %pad_maximum_fusion.1), channel_id=1, source_target_pairs={{0,4},{4,0},{8,12},{12,8},{16,20},{20,16},{24,28},{28,24},{1,5},{5... | collective-permute-start | bytes 4718600 | tf_op jit(solution)/shard_map/ppermute | solution.py:19
  178.0 21.7 %collective-permute-start.32 = (bf16[384,2048]{1,0:T(8,128)(2,1)S(1)}, bf16[384,2048]{1,0:T(8,128)(2,1)S(1)}, u32[]{:S(2)}, u32[]{:S(2)}) collective-permute-start(bf16[384,2048]{1,0:T(8,128)(2,1)S(1)} %collective-permute-done.9.refs_2_.refs_11_), channel_id=1, source_target_pairs={{0,4},{4,0},{8,12},{12,8},{16,20},{20,16},{24,28},{28,24},{1,5},{5... | collective-permute-start | bytes 4718600 | tf_op jit(solution)/shard_map/ppermute | solution.py:19
  192.8 25.4 %collective-permute-start.23 = (bf16[288,1024]{1,0:T(8,128)(2,1)S(1)}, bf16[288,1024]{1,0:T(8,128)(2,1)S(1)}, u32[]{:S(2)}, u32[]{:S(2)}) collective-permute-start(bf16[288,1024]{1,0:T(8,128)(2,1)S(1)} %get-tuple-element.54), channel_id=1, source_target_pairs={{0,4},{4,0},{8,12},{12,8},{16,20},{20,16},{24,28},{28,24},{1,5},{5... | collective-permute-start | bytes 1769480 | tf_op jit(solution)/shard_map/ppermute | solution.py:19
  195.2 22.9 %collective-permute-start.31 = (bf16[288,1024]{1,0:T(8,128)(2,1)S(1)}, bf16[288,1024]{1,0:T(8,128)(2,1)S(1)}, u32[]{:S(2)}, u32[]{:S(2)}) collective-permute-start(bf16[288,1024]{1,0:T(8,128)(2,1)S(1)} %collective-permute-done.29.refs_12_), channel_id=1, source_target_pairs={{2,1},{6,5},{10,8},{14,12},{17,19},{21,23},{25,26},{29,30}} | collective-permute-start | bytes 1769480 | tf_op jit(solution)/shard_map/ppermute | solution.py:228
  199.7 18.4 %collective-permute-start.30 = (bf16[288,1024]{1,0:T(8,128)(2,1)S(1)}, bf16[288,1024]{1,0:T(8,128)(2,1)S(1)}, u32[]{:S(2)}, u32[]{:S(2)}) collective-permute-start(bf16[288,1024]{1,0:T(8,128)(2,1)S(1)} %collective-permute-done.29.refs_12_), channel_id=1, source_target_pairs={{2,3},{6,7},{10,11},{14,15},{17,16},{21,20},{25,24},{29,28}} | collective-permute-start | bytes 1769480 | tf_op jit(solution)/shard_map/ppermute | solution.py:228
  (40 other events, 601.3 us)

commit v3 on v2

--- a/solution.py
+++ b/solution.py
@@ -75,36 +75,47 @@
     )(member, dose)
 
 
-def standardize_kernel(dose_ref, code_ref, mean_ref, scale_ref, out_ref):
+def standardize_kernel(skip, dose_ref, code_ref, mean_ref, scale_ref, *refs):
     code = code_ref[...].astype(jnp.float32)
     lane = lax.broadcasted_iota(jnp.int32, code.shape, 1)
     cohort = jnp.where(lane < PARTS * COHORTS, lane % COHORTS, -1)
     hot = (code == cohort.astype(jnp.float32)).astype(jnp.float32).astype(jnp.bfloat16)
     dot = functools.partial(jnp.dot, preferred_element_type=jnp.float32)
     centered = dose_ref[...].astype(jnp.float32) - dot(hot, mean_ref[...])
-    out_ref[...] = (centered * dot(hot, scale_ref[...])).astype(jnp.bfloat16)
-
-
-def standardized(coded, tables):
+    ready = (centered * dot(hot, scale_ref[...])).astype(jnp.bfloat16)
+    if len(refs) == 1:
+        refs[0][...] = ready
+    else:
+        extra_ref, out_ref, rest_ref = refs
+        kept = ready.shape[0] - skip
+        out_ref[...] = ready
+        rest_ref[:kept, :] = ready[skip:]
+        rest_ref[kept:, :] = extra_ref[...]
+
+
+def standardized(coded, tables, extra=None, skip=0):
     rows, width = coded.shape[0], coded.shape[1] - TABLE
     tile = min(512, width)
     by_tile = lambda height: pl.BlockSpec((height, tile), lambda j: (0, j))
-    return pl.pallas_call(
-        standardize_kernel,
+    heights = [rows] if extra is None else [rows, rows - skip + extra.shape[0]]
+    out = pl.pallas_call(
+        functools.partial(standardize_kernel, skip),
         grid=(width // tile,),
         in_specs=[
             by_tile(rows),
             pl.BlockSpec((rows, TABLE), lambda j: (0, width // TABLE)),
             by_tile(TABLE),
             by_tile(TABLE),
-        ],
-        out_specs=by_tile(rows),
-        out_shape=jax.ShapeDtypeStruct((rows, width), jnp.bfloat16),
+        ]
+        + ([] if extra is None else [by_tile(extra.shape[0])]),
+        out_specs=[by_tile(h) for h in heights],
+        out_shape=[jax.ShapeDtypeStruct((h, width), jnp.bfloat16) for h in heights],
         cost_estimate=pl.CostEstimate(
             flops=4 * TABLE * rows * width, bytes_accessed=4 * rows * width, transcendentals=0
         ),
         compiler_params=pltpu.CompilerParams(vmem_limit_bytes=24 * 2**20),
-    )(coded, coded, *tables)
+    )(coded, coded, *tables, *([] if extra is None else [extra]))
+    return out[0] if extra is None else out
 
 
 def gram_kernel(takes, row_sizes, row_counts, has_total, *refs):
@@ -115,14 +126,13 @@
         rows.append(refs[:count])
         refs = refs[count:]
     total = refs[0] if has_total else None
-    out, row_dose, row_ready, col_ready, sems = refs[-5:]
-    depth = sum(row_sizes)
+    out, row_ready, col_ready, sems = refs[-4:]
 
     @pl.when(pl.program_id(0) == 0)
     def _():
         at, waits = 0, []
         for j, (places, size) in enumerate(zip(rows, row_sizes)):
-            to = row_dose.at[pl.ds(at, size), :]
+            to = row_ready.at[pl.ds(at, size), :]
             for i, place in enumerate(places):
                 here = role == i if i < len(places) - 1 else role >= i
 
@@ -134,15 +144,17 @@
             at += size
         for wait in waits:
             wait.wait()
-        step = 128 if depth % 128 == 0 else depth
-        for at in range(0, depth, step):
-            row_ready[:, at : at + step] = row_dose[at : at + step, :].T
 
     at = 0
     for j, (start, size) in enumerate(takes):
         col_ready[at : at + size, :] = cols[j][start : start + size, :]
         at += size
-    product = jnp.dot(row_ready[...], col_ready[...], preferred_element_type=jnp.float32)
+    product = lax.dot_general(
+        row_ready[...],
+        col_ready[...],
+        (((0,), (0,)), ((), ())),
+        preferred_element_type=jnp.float32,
+    )
     if has_total:
         product += total[...]
     out[...] = product
@@ -176,7 +188,6 @@
         out_shape=jax.ShapeDtypeStruct((height, width), jnp.float32),
         scratch_shapes=[
             pltpu.VMEM((depth, height), jnp.bfloat16),
-            pltpu.VMEM((height, depth), jnp.bfloat16),
             pltpu.VMEM((depth, tile), jnp.bfloat16),
             pltpu.SemaphoreType.DMA((len(rows),)),
         ],
@@ -283,9 +294,8 @@
     balanced = jnp.where(row_index < offset, coded[:kept], placed[:kept])
     if early:
         balanced = after(balanced, below[2], above[2])
-    base = standardized(balanced, tables)
     if not early:
-        pieces = {0: base}
+        pieces = {0: standardized(balanced, tables)}
         for bit in bits:
             pieces |= {m ^ bit: swapped(block, bit) for m, block in pieces.items()}
         groups = []
@@ -312,12 +322,13 @@
     other_half = lambda block: lax.dynamic_slice_in_dim(block, height - row_start, height, 1)
     my_half = lambda block: row_part(block, 0, block.shape[0])
 
+    sent_tables = jnp.concatenate([t[:used] for t in tables], 0)
+    base, first = standardized(balanced, tables, sent_tables, early)
     pieces = {0: base}
     pieces[far], pieces[near] = swapped(base, far), swapped(base, near)
-    first = jnp.concatenate([rest(0), *(t[:used] for t in tables)], 0)
     legs = [along_line(first)]
     pieces[1] = swapped(base, 1)
-    legs.append(along_line(after(rest(near), pieces[1], below[3], above[3])))
+    legs.append(along_line(after(rest(near), pieces[1], below[3], above[3], legs[0][1], pieces[far])))
     pieces[both] = swapped(after(pieces[far], pieces[near], legs[0][1]), near)
     legs.append(along_line(after(rest(far), legs[0][1])))
     up = jnp.concatenate([of_panel(chip ^ 2), of_panel(chip ^ 3)], 0)
@@ -355,7 +366,7 @@
         for i, block, other in zip((0, near, far), whole, others)
     ]
     groups.append((cols(both, both + 1), legs[3:]))
-    return gram_of(groups, role, 3)
+    return gram_of(groups, role, 4)
 
 
 def solution(mesh):

time: 233 us -> 227 us (0.974)
  waiting for transfers between devices: 76.9 us -> 70.1 us
  starting transfers between devices: 80.3 us -> 83.1 us
    ppermute x15, waiting for transfers between devices: 58.1 us -> 52.4 us  [hop(): return lax.ppermute(block, ('samp', 'var'), pairs)]
    unnamed x65 -> x47, local copies, waits for them, and re-layouts: 9.73 us -> 6.39 us
  transfers between devices with their start and end apart: 38 -> 38, of which waited for: 14 -> 14; matrix products, arithmetic and copies ran while one was open for 11% -> 13% of each run, Pallas kernels for 8% -> 9%
where the time goes in v3:
time: 227 us; the launch traced here: 225 us
  starting transfers between devices  83.1 us (37%)
  waiting for transfers between devices  70.1 us (31%)
  Pallas kernels  33.9 us (15%)
  local copies, waits for them, and re-layouts  19.8 us (9%)
  other arithmetic  16.8 us (7%)
    ppermute x15, waiting for transfers between devices, hop(): return lax.ppermute(block, ('samp', 'var'), pairs)  52.4 us
    ppermute x17, starting transfers between devices, swapped(): lax.ppermute(block, 'samp', [(i, i ^ distance) for i in range(lax.axis_si...  40.5 us
    pallas_call x2, Pallas kernels, gram(): pl.pallas_call(functools.partial(gram_kernel, takes, row_sizes, tuple((le...  28.1 us
    ppermute x15, starting transfers between devices, hop(): return lax.ppermute(block, ('samp', 'var'), pairs)  26.4 us
    ppermute x6, starting transfers between devices, along_var(): return lax.ppermute(block, 'var', pairs)  16.2 us
    ppermute x17, waiting for transfers between devices, swapped(): lax.ppermute(block, 'samp', [(i, i ^ distance) for i in range(lax.axis_si...  13.1 us
    unnamed x47, local copies, waits for them, and re-layouts  6.39 us
    select_n x3, other arithmetic, shards(): panel = lambda got: jnp.where(owns_rows, got[0], sum(got[2:], got[1]))  4.61 us
  transfers between devices with their start and end apart: 38, of which 14 were waited for; matrix products, arithmetic and copies ran while one was open for 13% of the time, Pallas kernels for 9%

profile of v3, /device:TPU:15, one launch (start us, length us, event | category | flops | bytes accessed | tf_op | source)
XLA Modules:
  0.0 225.4 jit_solution(10950534840995222470)
XLA Ops:
  0.9 2.6 %pad_maximum_fusion.2 = bf16[288,2176]{1,0:T(8,128)(2,1)} fusion(bf16[672,128]{1,0:T(8,128)(2,1)S(1)} %broadcast_in_dim.34, bf16[672,2048]{1,0:T(8,128)(2,1)} %dose_ref.1), kind=kLoop, calls=%fused_computation.6 | loop fusion | flops 2506752 | bytes 4177920 | tf_op jit(solution)/shard_map/concatenate | solution.py:258
  9.9 3.4 %collective-permute-start.1 = (bf16[96,2048]{1,0:T(8,128)(2,1)}, bf16[96,2048]{1,0:T(8,128)(2,1)}, u32[]{:S(2)}, u32[]{:S(2)}) collective-permute-start(bf16[96,2048]{1,0:T(8,128)(2,1)} %slice.83), channel_id=1, source_target_pairs={{0,1},{1,2},{2,3},{4,5},{5,6},{6,7},{8,9},{9,10},{10,11},{12,13},{... | collective-permute-start | bytes 1179656 | tf_op jit(solution)/shard_map/ppermute | solution.py:251
  21.7 3.1 %collective-permute-start.2 = (bf16[96,2048]{1,0:T(8,128)(2,1)}, bf16[96,2048]{1,0:T(8,128)(2,1)S(1)}, u32[]{:S(2)}, u32[]{:S(2)}) collective-permute-start(bf16[96,2048]{1,0:T(8,128)(2,1)} %collective-permute-done.1), channel_id=1, source_target_pairs={{0,1},{1,2},{2,3},{4,5},{5,6},{6,7},{8,9},{9,10},{10,11},{12,13},{... | collective-permute-start | bytes 1179656 | tf_op jit(solution)/shard_map/ppermute | solution.py:251
  24.8 7.4 %collective-permute-done = bf16[288,2176]{1,0:T(8,128)(2,1)} collective-permute-done((bf16[288,2176]{1,0:T(8,128)(2,1)}, bf16[288,2176]{1,0:T(8,128)(2,1)}, u32[]{:S(2)}, u32[]{:S(2)}) %collective-permute-start) | collective-permute-done | bytes 1253408 | tf_op jit(solution)/shard_map/ppermute | solution.py:19
  41.2 3.0 %collective-permute-start.14 = (bf16[384,2048]{1,0:T(8,128)(2,1)S(1)}, bf16[384,2048]{1,0:T(8,128)(2,1)}, u32[]{:S(2)}, u32[]{:S(2)}) collective-permute-start(bf16[384,2048]{1,0:T(8,128)(2,1)S(1)} %get-tuple-element.23.refs_1_.refs_9_), channel_id=1, source_target_pairs={{0,4},{4,0},{8,12},{12,8},{16,20},{20,16},{24,28},{28,24},{1,5},{5... | collective-permute-start | bytes 4718600 | tf_op jit(solution)/shard_map/ppermute | solution.py:19
  44.2 3.0 %collective-permute-start.8 = (bf16[384,2048]{1,0:T(8,128)(2,1)S(1)}, bf16[384,2048]{1,0:T(8,128)(2,1)}, u32[]{:S(2)}, u32[]{:S(2)}) collective-permute-start(bf16[384,2048]{1,0:T(8,128)(2,1)S(1)} %get-tuple-element.23.refs_1_.refs_9_), channel_id=1, source_target_pairs={{0,16},{4,20},{8,24},{12,28},{16,0},{20,4},{24,8},{28,12},{1,17},{... | collective-permute-start | bytes 4718600 | tf_op jit(solution)/shard_map/ppermute | solution.py:19
  47.2 3.7 %collective-permute-start.16 = (bf16[96,2048]{1,0:T(8,128)(2,1)}, bf16[96,2048]{1,0:T(8,128)(2,1)S(1)}, u32[]{:S(2)}, u32[]{:S(2)}) collective-permute-start(bf16[96,2048]{1,0:T(8,128)(2,1)} %copy-done.8), channel_id=1, source_target_pairs={{1,0},{2,1},{3,2},{5,4},{6,5},{7,6},{9,8},{10,9},{11,10},{13,12},{... | collective-permute-start | bytes 1179656 | tf_op jit(solution)/shard_map/ppermute | solution.py:251
  50.9 20.6 %collective-permute-done.10 = bf16[336,2048]{1,0:T(8,128)(2,1)} collective-permute-done((bf16[336,2048]{1,0:T(8,128)(2,1)S(1)}, bf16[336,2048]{1,0:T(8,128)(2,1)}, u32[]{:S(2)}, u32[]{:S(2)}) %collective-permute-start.10) | collective-permute-done | bytes 1376288 | tf_op jit(solution)/shard_map/ppermute | solution.py:239
  74.3 5.0 %collective-permute-start.13 = (bf16[336,2048]{1,0:T(8,128)(2,1)}, bf16[336,2048]{1,0:T(8,128)(2,1)}, u32[]{:S(2)}, u32[]{:S(2)}) collective-permute-start(bf16[336,2048]{1,0:T(8,128)(2,1)} %collective-permute-done.10), channel_id=1, source_target_pairs={{2,1},{6,5},{10,8},{14,12},{17,19},{21,23},{25,26},{29,30}} | collective-permute-start | bytes 4128776 | tf_op jit(solution)/shard_map/ppermute | solution.py:239
  83.0 2.4 %collective-permute-start.12 = (bf16[336,2048]{1,0:T(8,128)(2,1)}, bf16[336,2048]{1,0:T(8,128)(2,1)}, u32[]{:S(2)}, u32[]{:S(2)}) collective-permute-start(bf16[336,2048]{1,0:T(8,128)(2,1)} %collective-permute-done.10), channel_id=1, source_target_pairs={{2,3},{6,7},{10,11},{14,15},{17,16},{21,20},{25,24},{29,28}} | collective-permute-start | bytes 4128776 | tf_op jit(solution)/shard_map/ppermute | solution.py:239
  88.8 2.5 %slice.112 = bf16[288,2048]{1,0:T(8,128)(2,1)} slice(bf16[384,2048]{1,0:T(8,128)(2,1)} %collective-permute-done.8.refs_3_.refs_13_), slice={[96:384], [0:2048]} | slice | bytes 2359296 | tf_op jit(solution)/shard_map/slice | solution.py:320
  94.9 16.0 %collective-permute-done.17 = bf16[288,2048]{1,0:T(8,128)(2,1)} collective-permute-done((bf16[288,2048]{1,0:T(8,128)(2,1)S(1)}, bf16[288,2048]{1,0:T(8,128)(2,1)}, u32[]{:S(2)}, u32[]{:S(2)}) %collective-permute-start.17) | collective-permute-done | bytes 1179680 | tf_op jit(solution)/shard_map/ppermute | solution.py:239
  112.6 3.0 %collective-permute-start.21 = (bf16[288,2048]{1,0:T(8,128)(2,1)}, bf16[288,2048]{1,0:T(8,128)(2,1)S(1)}, u32[]{:S(2)}, u32[]{:S(2)}) collective-permute-start(bf16[288,2048]{1,0:T(8,128)(2,1)} %collective-permute-done.17), channel_id=1, source_target_pairs={{2,1},{6,5},{10,8},{14,12},{17,19},{21,23},{25,26},{29,30}} | collective-permute-start | bytes 3538952 | tf_op jit(solution)/shard_map/ppermute | solution.py:239
  118.1 9.3 %collective-permute-start.18 = (bf16[384,2048]{1,0:T(8,128)(2,1)}, bf16[384,2048]{1,0:T(8,128)(2,1)S(1)}, u32[]{:S(2)}, u32[]{:S(2)}) collective-permute-start(bf16[384,2048]{1,0:T(8,128)(2,1)} %collective-permute-done.11.refs_4_.refs_1_), channel_id=1, source_target_pairs={{0,4},{4,0},{8,12},{12,8},{16,20},{20,16},{24,28},{28,24},{1,5},{5... | collective-permute-start | bytes 4718600 | tf_op jit(solution)/shard_map/ppermute | solution.py:19
  129.4 6.8 %collective-permute-done.19 = bf16[288,2048]{1,0:T(8,128)(2,1)} collective-permute-done((bf16[288,2048]{1,0:T(8,128)(2,1)}, bf16[288,2048]{1,0:T(8,128)(2,1)}, u32[]{:S(2)}, u32[]{:S(2)}) %collective-permute-start.19) | collective-permute-done | bytes 1179680 | tf_op jit(solution)/shard_map/ppermute | solution.py:239
  144.5 5.8 %collective-permute-start.30 = (bf16[384,2048]{1,0:T(8,128)(2,1)}, bf16[384,2048]{1,0:T(8,128)(2,1)S(1)}, u32[]{:S(2)}, u32[]{:S(2)}) collective-permute-start(bf16[384,2048]{1,0:T(8,128)(2,1)} %collective-permute-done.8.refs_3_.refs_13_), channel_id=1, source_target_pairs={{0,4},{4,0},{8,12},{12,8},{16,20},{20,16},{24,28},{28,24},{1,5},{5... | collective-permute-start | bytes 4718600 | tf_op jit(solution)/shard_map/ppermute | solution.py:19
  152.7 2.9 %collective-permute-done.33 = bf16[192,2048]{1,0:T(8,128)(2,1)S(1)} collective-permute-done((bf16[192,2048]{1,0:T(8,128)(2,1)S(1)}, bf16[192,2048]{1,0:T(8,128)(2,1)S(1)}, u32[]{:S(2)}, u32[]{:S(2)}) %collective-permute-start.33) | collective-permute-done | bytes 786464 | tf_op jit(solution)/shard_map/ppermute | solution.py:19
  155.8 6.7 %collective-permute-start.34 = (bf16[384,2048]{1,0:T(8,128)(2,1)S(1)}, bf16[384,2048]{1,0:T(8,128)(2,1)S(1)}, u32[]{:S(2)}, u32[]{:S(2)}) collective-permute-start(bf16[384,2048]{1,0:T(8,128)(2,1)S(1)} %pad_maximum_fusion.1), channel_id=1, source_target_pairs={{0,4},{4,0},{8,12},{12,8},{16,20},{20,16},{24,28},{28,24},{1,5},{5... | collective-permute-start | bytes 4718600 | tf_op jit(solution)/shard_map/ppermute | solution.py:19
  164.7 3.9 %collective-permute-done.22.refs_4_ = bf16[288,1024]{1,0:T(8,128)(2,1)S(1)} collective-permute-done((bf16[288,1024]{1,0:T(8,128)(2,1)S(1)}, bf16[288,1024]{1,0:T(8,128)(2,1)S(1)}, u32[]{:S(2)}, u32[]{:S(2)}) %collective-permute-start.22) | collective-permute-done | bytes 589856 | tf_op jit(solution)/shard_map/ppermute | solution.py:239
  172.7 2.5 %collective-permute-start.31 = (bf16[384,2048]{1,0:T(8,128)(2,1)}, bf16[384,2048]{1,0:T(8,128)(2,1)S(1)}, u32[]{:S(2)}, u32[]{:S(2)}) collective-permute-start(bf16[384,2048]{1,0:T(8,128)(2,1)} %collective-permute-done.9.refs_2_.refs_11_), channel_id=1, source_target_pairs={{0,4},{4,0},{8,12},{12,8},{16,20},{20,16},{24,28},{28,24},{1,5},{5... | collective-permute-start | bytes 4718600 | tf_op jit(solution)/shard_map/ppermute | solution.py:19
  177.8 3.3 %collective-permute-done.26.refs_6_ = bf16[288,1024]{1,0:T(8,128)(2,1)S(1)} collective-permute-done((bf16[288,1024]{1,0:T(8,128)(2,1)S(1)}, bf16[288,1024]{1,0:T(8,128)(2,1)S(1)}, u32[]{:S(2)}, u32[]{:S(2)}) %collective-permute-start.26) | collective-permute-done | bytes 589856 | tf_op jit(solution)/shard_map/ppermute | solution.py:239
  186.5 3.4 %collective-permute-start.36 = (bf16[288,1024]{1,0:T(8,128)(2,1)S(1)}, bf16[288,1024]{1,0:T(8,128)(2,1)S(1)}, u32[]{:S(2)}, u32[]{:S(2)}) collective-permute-start(bf16[288,1024]{1,0:T(8,128)(2,1)S(1)} %get-tuple-element.56), channel_id=1, source_target_pairs={{0,4},{4,0},{8,12},{12,8},{16,20},{20,16},{24,28},{28,24},{1,5},{5... | collective-permute-start | bytes 1769480 | tf_op jit(solution)/shard_map/ppermute | solution.py:19
  197.1 17.5 %shard_map.67.refs_11_ = f32[1024,2048]{1,0:T(8,128)} custom-call(s32[1]{0:T(128)} %bitcast.refs_0_, bf16[384,2048]{1,0:T(8,128)(2,1)S(1)} %get-tuple-element.23.refs_1_.refs_9_, bf16[384,2048]{1,0:T(8,128)(2,1)} %collective-permute-done.9.refs_2_.refs_11_, bf16[384,2048]{1,0:T(8,128)(2,1)} %collective-permute-done.8.refs_3_.refs_13_, ...), custom_call_target="tpu_custom_call" | custom-call | flops 10468982784 | bytes 32112640 | tf_op jit(solution)/shard_map/pallas_call | solution.py:181
  214.7 10.6 %shard_map.68 = f32[1024,2048]{1,0:T(8,128)} custom-call(s32[1]{0:T(128)} %bitcast.refs_0_, bf16[384,2048]{1,0:T(8,128)(2,1)} %collective-permute-done.11.refs_4_.refs_1_, bf16[384,2048]{1,0:T(8,128)(2,1)} %copy-done.4, bf16[288,1024]{1,0:T(8,128)(2,1)S(1)} %constant_dynamic-slice_fusion.9.refs_3_, ...), custom_call_target="tpu_custom_call", output_to_operand_aliasing={{}: (11, {})} | custom-call | flops 2415919104 | bytes 20316160 | tf_op jit(solution)/shard_map/pallas_call | solution.py:181
  (170 shorter events, 75.5 us)
Async XLA Ops:
  3.4 28.7 %collective-permute-start = (bf16[288,2176]{1,0:T(8,128)(2,1)}, bf16[288,2176]{1,0:T(8,128)(2,1)}, u32[]{:S(2)}, u32[]{:S(2)}) collective-permute-start(bf16[288,2176]{1,0:T(8,128)(2,1)} %pad_maximum_fusion.2), channel_id=1, source_target_pairs={{0,16},{4,20},{8,24},{12,28},{16,0},{20,4},{24,8},{28,12},{1,17},{... | collective-permute-start | bytes 3760136 | tf_op jit(solution)/shard_map/ppermute | solution.py:19
  39.6 31.9 %collective-permute-start.10 = (bf16[336,2048]{1,0:T(8,128)(2,1)S(1)}, bf16[336,2048]{1,0:T(8,128)(2,1)}, u32[]{:S(2)}, u32[]{:S(2)}) collective-permute-start(bf16[336,2048]{1,0:T(8,128)(2,1)S(1)} %get-tuple-element.24), channel_id=1, source_target_pairs={{0,2},{4,6},{9,10},{13,14},{18,17},{22,21},{27,25},{31,29}} | collective-permute-start | bytes 4128776 | tf_op jit(solution)/shard_map/ppermute | solution.py:239
  40.9 33.4 %collective-permute-start.9 = (bf16[384,2048]{1,0:T(8,128)(2,1)S(1)}, bf16[384,2048]{1,0:T(8,128)(2,1)}, u32[]{:S(2)}, u32[]{:S(2)}) collective-permute-start(bf16[384,2048]{1,0:T(8,128)(2,1)S(1)} %get-tuple-element.23.refs_1_.refs_9_), channel_id=1, source_target_pairs={{0,8},{4,12},{8,0},{12,4},{16,24},{20,28},{24,16},{28,20},{1,9},{5... | collective-permute-start | bytes 4718600 | tf_op jit(solution)/shard_map/ppermute | solution.py:19
  41.2 44.1 %collective-permute-start.14 = (bf16[384,2048]{1,0:T(8,128)(2,1)S(1)}, bf16[384,2048]{1,0:T(8,128)(2,1)}, u32[]{:S(2)}, u32[]{:S(2)}) collective-permute-start(bf16[384,2048]{1,0:T(8,128)(2,1)S(1)} %get-tuple-element.23.refs_1_.refs_9_), channel_id=1, source_target_pairs={{0,4},{4,0},{8,12},{12,8},{16,20},{20,16},{24,28},{28,24},{1,5},{5... | collective-permute-start | bytes 4718600 | tf_op jit(solution)/shard_map/ppermute | solution.py:19
  44.2 41.1 %collective-permute-start.8 = (bf16[384,2048]{1,0:T(8,128)(2,1)S(1)}, bf16[384,2048]{1,0:T(8,128)(2,1)}, u32[]{:S(2)}, u32[]{:S(2)}) collective-permute-start(bf16[384,2048]{1,0:T(8,128)(2,1)S(1)} %get-tuple-element.23.refs_1_.refs_9_), channel_id=1, source_target_pairs={{0,16},{4,20},{8,24},{12,28},{16,0},{20,4},{24,8},{28,12},{1,17},{... | collective-permute-start | bytes 4718600 | tf_op jit(solution)/shard_map/ppermute | solution.py:19
  47.2 35.8 %collective-permute-start.16 = (bf16[96,2048]{1,0:T(8,128)(2,1)}, bf16[96,2048]{1,0:T(8,128)(2,1)S(1)}, u32[]{:S(2)}, u32[]{:S(2)}) collective-permute-start(bf16[96,2048]{1,0:T(8,128)(2,1)} %copy-done.8), channel_id=1, source_target_pairs={{1,0},{2,1},{3,2},{5,4},{6,5},{7,6},{9,8},{10,9},{11,10},{13,12},{... | collective-permute-start | bytes 1179656 | tf_op jit(solution)/shard_map/ppermute | solution.py:251
  74.3 38.3 %collective-permute-start.13 = (bf16[336,2048]{1,0:T(8,128)(2,1)}, bf16[336,2048]{1,0:T(8,128)(2,1)}, u32[]{:S(2)}, u32[]{:S(2)}) collective-permute-start(bf16[336,2048]{1,0:T(8,128)(2,1)} %collective-permute-done.10), channel_id=1, source_target_pairs={{2,1},{6,5},{10,8},{14,12},{17,19},{21,23},{25,26},{29,30}} | collective-permute-start | bytes 4128776 | tf_op jit(solution)/shard_map/ppermute | solution.py:239
  83.0 32.7 %collective-permute-start.12 = (bf16[336,2048]{1,0:T(8,128)(2,1)}, bf16[336,2048]{1,0:T(8,128)(2,1)}, u32[]{:S(2)}, u32[]{:S(2)}) collective-permute-start(bf16[336,2048]{1,0:T(8,128)(2,1)} %collective-permute-done.10), channel_id=1, source_target_pairs={{2,3},{6,7},{10,11},{14,15},{17,16},{21,20},{25,24},{29,28}} | collective-permute-start | bytes 4128776 | tf_op jit(solution)/shard_map/ppermute | solution.py:239
  85.4 25.6 %collective-permute-start.17 = (bf16[288,2048]{1,0:T(8,128)(2,1)S(1)}, bf16[288,2048]{1,0:T(8,128)(2,1)}, u32[]{:S(2)}, u32[]{:S(2)}) collective-permute-start(bf16[288,2048]{1,0:T(8,128)(2,1)S(1)} %slice.111), channel_id=1, source_target_pairs={{0,2},{4,6},{9,10},{13,14},{18,17},{22,21},{27,25},{31,29}} | collective-permute-start | bytes 3538952 | tf_op jit(solution)/shard_map/ppermute | solution.py:239
  86.7 31.5 %collective-permute-start.11 = (bf16[384,2048]{1,0:T(8,128)(2,1)}, bf16[384,2048]{1,0:T(8,128)(2,1)}, u32[]{:S(2)}, u32[]{:S(2)}) collective-permute-start(bf16[384,2048]{1,0:T(8,128)(2,1)} %collective-permute-done.8.refs_3_.refs_13_), channel_id=1, source_target_pairs={{0,8},{4,12},{8,0},{12,4},{16,24},{20,28},{24,16},{28,20},{1,9},{5... | collective-permute-start | bytes 4718600 | tf_op jit(solution)/shard_map/ppermute | solution.py:19
  91.3 44.9 %collective-permute-start.19 = (bf16[288,2048]{1,0:T(8,128)(2,1)}, bf16[288,2048]{1,0:T(8,128)(2,1)}, u32[]{:S(2)}, u32[]{:S(2)}) collective-permute-start(bf16[288,2048]{1,0:T(8,128)(2,1)} %slice.112), channel_id=1, source_target_pairs={{0,2},{4,6},{9,10},{13,14},{18,17},{22,21},{27,25},{31,29}} | collective-permute-start | bytes 3538952 | tf_op jit(solution)/shard_map/ppermute | solution.py:239
  110.9 28.6 %collective-permute-start.32 = (bf16[192,2048]{1,0:T(8,128)(2,1)}, bf16[192,2048]{1,0:T(8,128)(2,1)}, u32[]{:S(2)}, u32[]{:S(2)}) collective-permute-start(bf16[192,2048]{1,0:T(8,128)(2,1)} %pad_maximum_fusion.3), channel_id=1, source_target_pairs={{0,16},{4,20},{8,24},{12,28},{16,0},{20,4},{24,8},{28,12},{1,17},{... | collective-permute-start | bytes 2359304 | tf_op jit(solution)/shard_map/ppermute | solution.py:19
  112.6 29.5 %collective-permute-start.21 = (bf16[288,2048]{1,0:T(8,128)(2,1)}, bf16[288,2048]{1,0:T(8,128)(2,1)S(1)}, u32[]{:S(2)}, u32[]{:S(2)}) collective-permute-start(bf16[288,2048]{1,0:T(8,128)(2,1)} %collective-permute-done.17), channel_id=1, source_target_pairs={{2,1},{6,5},{10,8},{14,12},{17,19},{21,23},{25,26},{29,30}} | collective-permute-start | bytes 3538952 | tf_op jit(solution)/shard_map/ppermute | solution.py:239
  115.7 26.5 %collective-permute-start.20 = (bf16[288,2048]{1,0:T(8,128)(2,1)}, bf16[288,2048]{1,0:T(8,128)(2,1)S(1)}, u32[]{:S(2)}, u32[]{:S(2)}) collective-permute-start(bf16[288,2048]{1,0:T(8,128)(2,1)} %collective-permute-done.17), channel_id=1, source_target_pairs={{2,3},{6,7},{10,11},{14,15},{17,16},{21,20},{25,24},{29,28}} | collective-permute-start | bytes 3538952 | tf_op jit(solution)/shard_map/ppermute | solution.py:239
  118.1 26.4 %collective-permute-start.18 = (bf16[384,2048]{1,0:T(8,128)(2,1)}, bf16[384,2048]{1,0:T(8,128)(2,1)S(1)}, u32[]{:S(2)}, u32[]{:S(2)}) collective-permute-start(bf16[384,2048]{1,0:T(8,128)(2,1)} %collective-permute-done.11.refs_4_.refs_1_), channel_id=1, source_target_pairs={{0,4},{4,0},{8,12},{12,8},{16,20},{20,16},{24,28},{28,24},{1,5},{5... | collective-permute-start | bytes 4718600 | tf_op jit(solution)/shard_map/ppermute | solution.py:19
  136.2 28.5 %collective-permute-start.24 = (bf16[288,2048]{1,0:T(8,128)(2,1)}, bf16[288,2048]{1,0:T(8,128)(2,1)S(1)}, u32[]{:S(2)}, u32[]{:S(2)}) collective-permute-start(bf16[288,2048]{1,0:T(8,128)(2,1)} %collective-permute-done.19), channel_id=1, source_target_pairs={{2,1},{6,5},{10,8},{14,12},{17,19},{21,23},{25,26},{29,30}} | collective-permute-start | bytes 3538952 | tf_op jit(solution)/shard_map/ppermute | solution.py:239
  139.5 25.1 %collective-permute-start.23 = (bf16[288,2048]{1,0:T(8,128)(2,1)}, bf16[288,2048]{1,0:T(8,128)(2,1)S(1)}, u32[]{:S(2)}, u32[]{:S(2)}) collective-permute-start(bf16[288,2048]{1,0:T(8,128)(2,1)} %collective-permute-done.19), channel_id=1, source_target_pairs={{2,3},{6,7},{10,11},{14,15},{17,16},{21,20},{25,24},{29,28}} | collective-permute-start | bytes 3538952 | tf_op jit(solution)/shard_map/ppermute | solution.py:239
  144.5 28.2 %collective-permute-start.30 = (bf16[384,2048]{1,0:T(8,128)(2,1)}, bf16[384,2048]{1,0:T(8,128)(2,1)S(1)}, u32[]{:S(2)}, u32[]{:S(2)}) collective-permute-start(bf16[384,2048]{1,0:T(8,128)(2,1)} %collective-permute-done.8.refs_3_.refs_13_), channel_id=1, source_target_pairs={{0,4},{4,0},{8,12},{12,8},{16,20},{20,16},{24,28},{28,24},{1,5},{5... | collective-permute-start | bytes 4718600 | tf_op jit(solution)/shard_map/ppermute | solution.py:19
  151.4 17.2 %collective-permute-start.22 = (bf16[288,1024]{1,0:T(8,128)(2,1)S(1)}, bf16[288,1024]{1,0:T(8,128)(2,1)S(1)}, u32[]{:S(2)}, u32[]{:S(2)}) collective-permute-start(bf16[288,1024]{1,0:T(8,128)(2,1)S(1)} %constant_dynamic-slice_fusion.9.refs_3_), channel_id=1, source_target_pairs={{0,2},{4,6},{9,10},{13,14},{18,17},{22,21},{27,25},{31,29}} | collective-permute-start | bytes 1769480 | tf_op jit(solution)/shard_map/ppermute | solution.py:239
  155.8 34.1 %collective-permute-start.34 = (bf16[384,2048]{1,0:T(8,128)(2,1)S(1)}, bf16[384,2048]{1,0:T(8,128)(2,1)S(1)}, u32[]{:S(2)}, u32[]{:S(2)}) collective-permute-start(bf16[384,2048]{1,0:T(8,128)(2,1)S(1)} %pad_maximum_fusion.1), channel_id=1, source_target_pairs={{0,4},{4,0},{8,12},{12,8},{16,20},{20,16},{24,28},{28,24},{1,5},{5... | collective-permute-start | bytes 4718600 | tf_op jit(solution)/shard_map/ppermute | solution.py:19
  171.3 15.2 %collective-permute-start.27 = (bf16[288,1024]{1,0:T(8,128)(2,1)S(1)}, bf16[288,1024]{1,0:T(8,128)(2,1)S(1)}, u32[]{:S(2)}, u32[]{:S(2)}) collective-permute-start(bf16[288,1024]{1,0:T(8,128)(2,1)S(1)} %constant_dynamic-slice_fusion.8.refs_7_), channel_id=1, source_target_pairs={{0,2},{4,6},{9,10},{13,14},{18,17},{22,21},{27,25},{31,29}} | collective-permute-start | bytes 1769480 | tf_op jit(solution)/shard_map/ppermute | solution.py:239
  172.7 21.6 %collective-permute-start.31 = (bf16[384,2048]{1,0:T(8,128)(2,1)}, bf16[384,2048]{1,0:T(8,128)(2,1)S(1)}, u32[]{:S(2)}, u32[]{:S(2)}) collective-permute-start(bf16[384,2048]{1,0:T(8,128)(2,1)} %collective-permute-done.9.refs_2_.refs_11_), channel_id=1, source_target_pairs={{0,4},{4,0},{8,12},{12,8},{16,20},{20,16},{24,28},{28,24},{1,5},{5... | collective-permute-start | bytes 4718600 | tf_op jit(solution)/shard_map/ppermute | solution.py:19
  189.9 24.8 %collective-permute-start.29 = (bf16[288,1024]{1,0:T(8,128)(2,1)S(1)}, bf16[288,1024]{1,0:T(8,128)(2,1)S(1)}, u32[]{:S(2)}, u32[]{:S(2)}) collective-permute-start(bf16[288,1024]{1,0:T(8,128)(2,1)S(1)} %collective-permute-done.27.refs_8_), channel_id=1, source_target_pairs={{2,1},{6,5},{10,8},{14,12},{17,19},{21,23},{25,26},{29,30}} | collective-permute-start | bytes 1769480 | tf_op jit(solution)/shard_map/ppermute | solution.py:239
  194.3 20.4 %collective-permute-start.28 = (bf16[288,1024]{1,0:T(8,128)(2,1)S(1)}, bf16[288,1024]{1,0:T(8,128)(2,1)S(1)}, u32[]{:S(2)}, u32[]{:S(2)}) collective-permute-start(bf16[288,1024]{1,0:T(8,128)(2,1)S(1)} %collective-permute-done.27.refs_8_), channel_id=1, source_target_pairs={{2,3},{6,7},{10,11},{14,15},{17,16},{21,20},{25,24},{29,28}} | collective-permute-start | bytes 1769480 | tf_op jit(solution)/shard_map/ppermute | solution.py:239
  (34 other events, 520.7 us)

commit v4 on v3

--- a/solution.py
+++ b/solution.py
@@ -165,7 +165,7 @@
     blocks = [block for block, _, _ in cols]
     row_sizes = tuple(r[0].shape[0] for r in rows)
     depth, width, height = sum(row_sizes), blocks[0].shape[1], rows[0][0].shape[1]
-    tile = min(512, width)
+    tile = min(512 if depth > height else 1024, width)
     by_tile = lambda height: pl.BlockSpec((height, tile), lambda j: (0, j))
     in_specs = (
         [pl.BlockSpec(memory_space=pltpu.SMEM)]

time: 227 us -> 225 us (level)
  no operation moved by 1% of the time
where the time goes in v4:
time: 225 us; the launch traced here: 224 us
  starting transfers between devices  83.1 us (37%)
  waiting for transfers between devices  70.1 us (31%)
  Pallas kernels  32.6 us (14%)
  local copies, waits for them, and re-layouts  19.8 us (9%)
  other arithmetic  16.8 us (7%)
    ppermute x15, waiting for transfers between devices, hop(): return lax.ppermute(block, ('samp', 'var'), pairs)  52.4 us
    ppermute x17, starting transfers between devices, swapped(): lax.ppermute(block, 'samp', [(i, i ^ distance) for i in range(lax.axis_si...  40.5 us
    pallas_call x2, Pallas kernels, gram(): pl.pallas_call(functools.partial(gram_kernel, takes, row_sizes, tuple((le...  26.9 us
    ppermute x15, starting transfers between devices, hop(): return lax.ppermute(block, ('samp', 'var'), pairs)  26.4 us
    ppermute x6, starting transfers between devices, along_var(): return lax.ppermute(block, 'var', pairs)  16.2 us
    ppermute x17, waiting for transfers between devices, swapped(): lax.ppermute(block, 'samp', [(i, i ^ distance) for i in range(lax.axis_si...  13.1 us
    unnamed x47, local copies, waits for them, and re-layouts  6.39 us
    select_n x3, other arithmetic, shards(): panel = lambda got: jnp.where(owns_rows, got[0], sum(got[2:], got[1]))  4.61 us
  transfers between devices with their start and end apart: 38, of which 14 were waited for; matrix products, arithmetic and copies ran while one was open for 13% of the time, Pallas kernels for 9%

profile of v4, /device:TPU:15, one launch (start us, length us, event | category | flops | bytes accessed | tf_op | source)
XLA Modules:
  0.0 224.2 jit_solution(15478236714372794987)
XLA Ops:
  0.9 2.6 %pad_maximum_fusion.2 = bf16[288,2176]{1,0:T(8,128)(2,1)} fusion(bf16[672,128]{1,0:T(8,128)(2,1)S(1)} %broadcast_in_dim.34, bf16[672,2048]{1,0:T(8,128)(2,1)} %dose_ref.1), kind=kLoop, calls=%fused_computation.6 | loop fusion | flops 2506752 | bytes 4177920 | tf_op jit(solution)/shard_map/concatenate | solution.py:258
  9.9 3.4 %collective-permute-start.1 = (bf16[96,2048]{1,0:T(8,128)(2,1)}, bf16[96,2048]{1,0:T(8,128)(2,1)}, u32[]{:S(2)}, u32[]{:S(2)}) collective-permute-start(bf16[96,2048]{1,0:T(8,128)(2,1)} %slice.83), channel_id=1, source_target_pairs={{0,1},{1,2},{2,3},{4,5},{5,6},{6,7},{8,9},{9,10},{10,11},{12,13},{... | collective-permute-start | bytes 1179656 | tf_op jit(solution)/shard_map/ppermute | solution.py:251
  21.7 3.1 %collective-permute-start.2 = (bf16[96,2048]{1,0:T(8,128)(2,1)}, bf16[96,2048]{1,0:T(8,128)(2,1)S(1)}, u32[]{:S(2)}, u32[]{:S(2)}) collective-permute-start(bf16[96,2048]{1,0:T(8,128)(2,1)} %collective-permute-done.1), channel_id=1, source_target_pairs={{0,1},{1,2},{2,3},{4,5},{5,6},{6,7},{8,9},{9,10},{10,11},{12,13},{... | collective-permute-start | bytes 1179656 | tf_op jit(solution)/shard_map/ppermute | solution.py:251
  24.8 7.4 %collective-permute-done = bf16[288,2176]{1,0:T(8,128)(2,1)} collective-permute-done((bf16[288,2176]{1,0:T(8,128)(2,1)}, bf16[288,2176]{1,0:T(8,128)(2,1)}, u32[]{:S(2)}, u32[]{:S(2)}) %collective-permute-start) | collective-permute-done | bytes 1253408 | tf_op jit(solution)/shard_map/ppermute | solution.py:19
  41.2 3.0 %collective-permute-start.14 = (bf16[384,2048]{1,0:T(8,128)(2,1)S(1)}, bf16[384,2048]{1,0:T(8,128)(2,1)}, u32[]{:S(2)}, u32[]{:S(2)}) collective-permute-start(bf16[384,2048]{1,0:T(8,128)(2,1)S(1)} %get-tuple-element.23.refs_1_.refs_9_), channel_id=1, source_target_pairs={{0,4},{4,0},{8,12},{12,8},{16,20},{20,16},{24,28},{28,24},{1,5},{5... | collective-permute-start | bytes 4718600 | tf_op jit(solution)/shard_map/ppermute | solution.py:19
  44.2 3.0 %collective-permute-start.8 = (bf16[384,2048]{1,0:T(8,128)(2,1)S(1)}, bf16[384,2048]{1,0:T(8,128)(2,1)}, u32[]{:S(2)}, u32[]{:S(2)}) collective-permute-start(bf16[384,2048]{1,0:T(8,128)(2,1)S(1)} %get-tuple-element.23.refs_1_.refs_9_), channel_id=1, source_target_pairs={{0,16},{4,20},{8,24},{12,28},{16,0},{20,4},{24,8},{28,12},{1,17},{... | collective-permute-start | bytes 4718600 | tf_op jit(solution)/shard_map/ppermute | solution.py:19
  47.2 3.7 %collective-permute-start.16 = (bf16[96,2048]{1,0:T(8,128)(2,1)}, bf16[96,2048]{1,0:T(8,128)(2,1)S(1)}, u32[]{:S(2)}, u32[]{:S(2)}) collective-permute-start(bf16[96,2048]{1,0:T(8,128)(2,1)} %copy-done.8), channel_id=1, source_target_pairs={{1,0},{2,1},{3,2},{5,4},{6,5},{7,6},{9,8},{10,9},{11,10},{13,12},{... | collective-permute-start | bytes 1179656 | tf_op jit(solution)/shard_map/ppermute | solution.py:251
  50.9 20.6 %collective-permute-done.10 = bf16[336,2048]{1,0:T(8,128)(2,1)} collective-permute-done((bf16[336,2048]{1,0:T(8,128)(2,1)S(1)}, bf16[336,2048]{1,0:T(8,128)(2,1)}, u32[]{:S(2)}, u32[]{:S(2)}) %collective-permute-start.10) | collective-permute-done | bytes 1376288 | tf_op jit(solution)/shard_map/ppermute | solution.py:239
  74.3 5.0 %collective-permute-start.13 = (bf16[336,2048]{1,0:T(8,128)(2,1)}, bf16[336,2048]{1,0:T(8,128)(2,1)}, u32[]{:S(2)}, u32[]{:S(2)}) collective-permute-start(bf16[336,2048]{1,0:T(8,128)(2,1)} %collective-permute-done.10), channel_id=1, source_target_pairs={{2,1},{6,5},{10,8},{14,12},{17,19},{21,23},{25,26},{29,30}} | collective-permute-start | bytes 4128776 | tf_op jit(solution)/shard_map/ppermute | solution.py:239
  83.0 2.4 %collective-permute-start.12 = (bf16[336,2048]{1,0:T(8,128)(2,1)}, bf16[336,2048]{1,0:T(8,128)(2,1)}, u32[]{:S(2)}, u32[]{:S(2)}) collective-permute-start(bf16[336,2048]{1,0:T(8,128)(2,1)} %collective-permute-done.10), channel_id=1, source_target_pairs={{2,3},{6,7},{10,11},{14,15},{17,16},{21,20},{25,24},{29,28}} | collective-permute-start | bytes 4128776 | tf_op jit(solution)/shard_map/ppermute | solution.py:239
  88.8 2.5 %slice.112 = bf16[288,2048]{1,0:T(8,128)(2,1)} slice(bf16[384,2048]{1,0:T(8,128)(2,1)} %collective-permute-done.8.refs_3_.refs_13_), slice={[96:384], [0:2048]} | slice | bytes 2359296 | tf_op jit(solution)/shard_map/slice | solution.py:320
  94.9 16.0 %collective-permute-done.17 = bf16[288,2048]{1,0:T(8,128)(2,1)} collective-permute-done((bf16[288,2048]{1,0:T(8,128)(2,1)S(1)}, bf16[288,2048]{1,0:T(8,128)(2,1)}, u32[]{:S(2)}, u32[]{:S(2)}) %collective-permute-start.17) | collective-permute-done | bytes 1179680 | tf_op jit(solution)/shard_map/ppermute | solution.py:239
  112.6 3.0 %collective-permute-start.21 = (bf16[288,2048]{1,0:T(8,128)(2,1)}, bf16[288,2048]{1,0:T(8,128)(2,1)S(1)}, u32[]{:S(2)}, u32[]{:S(2)}) collective-permute-start(bf16[288,2048]{1,0:T(8,128)(2,1)} %collective-permute-done.17), channel_id=1, source_target_pairs={{2,1},{6,5},{10,8},{14,12},{17,19},{21,23},{25,26},{29,30}} | collective-permute-start | bytes 3538952 | tf_op jit(solution)/shard_map/ppermute | solution.py:239
  118.1 9.3 %collective-permute-start.18 = (bf16[384,2048]{1,0:T(8,128)(2,1)}, bf16[384,2048]{1,0:T(8,128)(2,1)S(1)}, u32[]{:S(2)}, u32[]{:S(2)}) collective-permute-start(bf16[384,2048]{1,0:T(8,128)(2,1)} %collective-permute-done.11.refs_4_.refs_1_), channel_id=1, source_target_pairs={{0,4},{4,0},{8,12},{12,8},{16,20},{20,16},{24,28},{28,24},{1,5},{5... | collective-permute-start | bytes 4718600 | tf_op jit(solution)/shard_map/ppermute | solution.py:19
  129.4 6.8 %collective-permute-done.19 = bf16[288,2048]{1,0:T(8,128)(2,1)} collective-permute-done((bf16[288,2048]{1,0:T(8,128)(2,1)}, bf16[288,2048]{1,0:T(8,128)(2,1)}, u32[]{:S(2)}, u32[]{:S(2)}) %collective-permute-start.19) | collective-permute-done | bytes 1179680 | tf_op jit(solution)/shard_map/ppermute | solution.py:239
  144.5 5.8 %collective-permute-start.30 = (bf16[384,2048]{1,0:T(8,128)(2,1)}, bf16[384,2048]{1,0:T(8,128)(2,1)S(1)}, u32[]{:S(2)}, u32[]{:S(2)}) collective-permute-start(bf16[384,2048]{1,0:T(8,128)(2,1)} %collective-permute-done.8.refs_3_.refs_13_), channel_id=1, source_target_pairs={{0,4},{4,0},{8,12},{12,8},{16,20},{20,16},{24,28},{28,24},{1,5},{5... | collective-permute-start | bytes 4718600 | tf_op jit(solution)/shard_map/ppermute | solution.py:19
  152.7 2.9 %collective-permute-done.33 = bf16[192,2048]{1,0:T(8,128)(2,1)S(1)} collective-permute-done((bf16[192,2048]{1,0:T(8,128)(2,1)S(1)}, bf16[192,2048]{1,0:T(8,128)(2,1)S(1)}, u32[]{:S(2)}, u32[]{:S(2)}) %collective-permute-start.33) | collective-permute-done | bytes 786464 | tf_op jit(solution)/shard_map/ppermute | solution.py:19
  155.8 6.7 %collective-permute-start.34 = (bf16[384,2048]{1,0:T(8,128)(2,1)S(1)}, bf16[384,2048]{1,0:T(8,128)(2,1)S(1)}, u32[]{:S(2)}, u32[]{:S(2)}) collective-permute-start(bf16[384,2048]{1,0:T(8,128)(2,1)S(1)} %pad_maximum_fusion.1), channel_id=1, source_target_pairs={{0,4},{4,0},{8,12},{12,8},{16,20},{20,16},{24,28},{28,24},{1,5},{5... | collective-permute-start | bytes 4718600 | tf_op jit(solution)/shard_map/ppermute | solution.py:19
  164.7 3.9 %collective-permute-done.22.refs_4_ = bf16[288,1024]{1,0:T(8,128)(2,1)S(1)} collective-permute-done((bf16[288,1024]{1,0:T(8,128)(2,1)S(1)}, bf16[288,1024]{1,0:T(8,128)(2,1)S(1)}, u32[]{:S(2)}, u32[]{:S(2)}) %collective-permute-start.22) | collective-permute-done | bytes 589856 | tf_op jit(solution)/shard_map/ppermute | solution.py:239
  172.7 2.5 %collective-permute-start.31 = (bf16[384,2048]{1,0:T(8,128)(2,1)}, bf16[384,2048]{1,0:T(8,128)(2,1)S(1)}, u32[]{:S(2)}, u32[]{:S(2)}) collective-permute-start(bf16[384,2048]{1,0:T(8,128)(2,1)} %collective-permute-done.9.refs_2_.refs_11_), channel_id=1, source_target_pairs={{0,4},{4,0},{8,12},{12,8},{16,20},{20,16},{24,28},{28,24},{1,5},{5... | collective-permute-start | bytes 4718600 | tf_op jit(solution)/shard_map/ppermute | solution.py:19
  177.8 3.3 %collective-permute-done.26.refs_6_ = bf16[288,1024]{1,0:T(8,128)(2,1)S(1)} collective-permute-done((bf16[288,1024]{1,0:T(8,128)(2,1)S(1)}, bf16[288,1024]{1,0:T(8,128)(2,1)S(1)}, u32[]{:S(2)}, u32[]{:S(2)}) %collective-permute-start.26) | collective-permute-done | bytes 589856 | tf_op jit(solution)/shard_map/ppermute | solution.py:239
  186.5 3.4 %collective-permute-start.36 = (bf16[288,1024]{1,0:T(8,128)(2,1)S(1)}, bf16[288,1024]{1,0:T(8,128)(2,1)S(1)}, u32[]{:S(2)}, u32[]{:S(2)}) collective-permute-start(bf16[288,1024]{1,0:T(8,128)(2,1)S(1)} %get-tuple-element.56), channel_id=1, source_target_pairs={{0,4},{4,0},{8,12},{12,8},{16,20},{20,16},{24,28},{28,24},{1,5},{5... | collective-permute-start | bytes 1769480 | tf_op jit(solution)/shard_map/ppermute | solution.py:19
  197.1 17.5 %shard_map.67.refs_11_ = f32[1024,2048]{1,0:T(8,128)} custom-call(s32[1]{0:T(128)} %bitcast.refs_0_, bf16[384,2048]{1,0:T(8,128)(2,1)S(1)} %get-tuple-element.23.refs_1_.refs_9_, bf16[384,2048]{1,0:T(8,128)(2,1)} %collective-permute-done.9.refs_2_.refs_11_, bf16[384,2048]{1,0:T(8,128)(2,1)} %collective-permute-done.8.refs_3_.refs_13_, ...), custom_call_target="tpu_custom_call" | custom-call | flops 10468982784 | bytes 32112640 | tf_op jit(solution)/shard_map/pallas_call | solution.py:181
  214.7 9.3 %shard_map.68 = f32[1024,2048]{1,0:T(8,128)} custom-call(s32[1]{0:T(128)} %bitcast.refs_0_, bf16[384,2048]{1,0:T(8,128)(2,1)} %collective-permute-done.11.refs_4_.refs_1_, bf16[384,2048]{1,0:T(8,128)(2,1)} %copy-done.4, bf16[288,1024]{1,0:T(8,128)(2,1)S(1)} %constant_dynamic-slice_fusion.9.refs_3_, ...), custom_call_target="tpu_custom_call", output_to_operand_aliasing={{}: (11, {})} | custom-call | flops 2415919104 | bytes 20316160 | tf_op jit(solution)/shard_map/pallas_call | solution.py:181
  (170 shorter events, 75.5 us)
Async XLA Ops:
  3.4 28.7 %collective-permute-start = (bf16[288,2176]{1,0:T(8,128)(2,1)}, bf16[288,2176]{1,0:T(8,128)(2,1)}, u32[]{:S(2)}, u32[]{:S(2)}) collective-permute-start(bf16[288,2176]{1,0:T(8,128)(2,1)} %pad_maximum_fusion.2), channel_id=1, source_target_pairs={{0,16},{4,20},{8,24},{12,28},{16,0},{20,4},{24,8},{28,12},{1,17},{... | collective-permute-start | bytes 3760136 | tf_op jit(solution)/shard_map/ppermute | solution.py:19
  39.6 31.9 %collective-permute-start.10 = (bf16[336,2048]{1,0:T(8,128)(2,1)S(1)}, bf16[336,2048]{1,0:T(8,128)(2,1)}, u32[]{:S(2)}, u32[]{:S(2)}) collective-permute-start(bf16[336,2048]{1,0:T(8,128)(2,1)S(1)} %get-tuple-element.24), channel_id=1, source_target_pairs={{0,2},{4,6},{9,10},{13,14},{18,17},{22,21},{27,25},{31,29}} | collective-permute-start | bytes 4128776 | tf_op jit(solution)/shard_map/ppermute | solution.py:239
  40.9 33.4 %collective-permute-start.9 = (bf16[384,2048]{1,0:T(8,128)(2,1)S(1)}, bf16[384,2048]{1,0:T(8,128)(2,1)}, u32[]{:S(2)}, u32[]{:S(2)}) collective-permute-start(bf16[384,2048]{1,0:T(8,128)(2,1)S(1)} %get-tuple-element.23.refs_1_.refs_9_), channel_id=1, source_target_pairs={{0,8},{4,12},{8,0},{12,4},{16,24},{20,28},{24,16},{28,20},{1,9},{5... | collective-permute-start | bytes 4718600 | tf_op jit(solution)/shard_map/ppermute | solution.py:19
  41.2 44.1 %collective-permute-start.14 = (bf16[384,2048]{1,0:T(8,128)(2,1)S(1)}, bf16[384,2048]{1,0:T(8,128)(2,1)}, u32[]{:S(2)}, u32[]{:S(2)}) collective-permute-start(bf16[384,2048]{1,0:T(8,128)(2,1)S(1)} %get-tuple-element.23.refs_1_.refs_9_), channel_id=1, source_target_pairs={{0,4},{4,0},{8,12},{12,8},{16,20},{20,16},{24,28},{28,24},{1,5},{5... | collective-permute-start | bytes 4718600 | tf_op jit(solution)/shard_map/ppermute | solution.py:19
  44.2 41.1 %collective-permute-start.8 = (bf16[384,2048]{1,0:T(8,128)(2,1)S(1)}, bf16[384,2048]{1,0:T(8,128)(2,1)}, u32[]{:S(2)}, u32[]{:S(2)}) collective-permute-start(bf16[384,2048]{1,0:T(8,128)(2,1)S(1)} %get-tuple-element.23.refs_1_.refs_9_), channel_id=1, source_target_pairs={{0,16},{4,20},{8,24},{12,28},{16,0},{20,4},{24,8},{28,12},{1,17},{... | collective-permute-start | bytes 4718600 | tf_op jit(solution)/shard_map/ppermute | solution.py:19
  47.2 35.8 %collective-permute-start.16 = (bf16[96,2048]{1,0:T(8,128)(2,1)}, bf16[96,2048]{1,0:T(8,128)(2,1)S(1)}, u32[]{:S(2)}, u32[]{:S(2)}) collective-permute-start(bf16[96,2048]{1,0:T(8,128)(2,1)} %copy-done.8), channel_id=1, source_target_pairs={{1,0},{2,1},{3,2},{5,4},{6,5},{7,6},{9,8},{10,9},{11,10},{13,12},{... | collective-permute-start | bytes 1179656 | tf_op jit(solution)/shard_map/ppermute | solution.py:251
  74.3 38.3 %collective-permute-start.13 = (bf16[336,2048]{1,0:T(8,128)(2,1)}, bf16[336,2048]{1,0:T(8,128)(2,1)}, u32[]{:S(2)}, u32[]{:S(2)}) collective-permute-start(bf16[336,2048]{1,0:T(8,128)(2,1)} %collective-permute-done.10), channel_id=1, source_target_pairs={{2,1},{6,5},{10,8},{14,12},{17,19},{21,23},{25,26},{29,30}} | collective-permute-start | bytes 4128776 | tf_op jit(solution)/shard_map/ppermute | solution.py:239
  83.0 32.7 %collective-permute-start.12 = (bf16[336,2048]{1,0:T(8,128)(2,1)}, bf16[336,2048]{1,0:T(8,128)(2,1)}, u32[]{:S(2)}, u32[]{:S(2)}) collective-permute-start(bf16[336,2048]{1,0:T(8,128)(2,1)} %collective-permute-done.10), channel_id=1, source_target_pairs={{2,3},{6,7},{10,11},{14,15},{17,16},{21,20},{25,24},{29,28}} | collective-permute-start | bytes 4128776 | tf_op jit(solution)/shard_map/ppermute | solution.py:239
  85.4 25.6 %collective-permute-start.17 = (bf16[288,2048]{1,0:T(8,128)(2,1)S(1)}, bf16[288,2048]{1,0:T(8,128)(2,1)}, u32[]{:S(2)}, u32[]{:S(2)}) collective-permute-start(bf16[288,2048]{1,0:T(8,128)(2,1)S(1)} %slice.111), channel_id=1, source_target_pairs={{0,2},{4,6},{9,10},{13,14},{18,17},{22,21},{27,25},{31,29}} | collective-permute-start | bytes 3538952 | tf_op jit(solution)/shard_map/ppermute | solution.py:239
  86.7 31.5 %collective-permute-start.11 = (bf16[384,2048]{1,0:T(8,128)(2,1)}, bf16[384,2048]{1,0:T(8,128)(2,1)}, u32[]{:S(2)}, u32[]{:S(2)}) collective-permute-start(bf16[384,2048]{1,0:T(8,128)(2,1)} %collective-permute-done.8.refs_3_.refs_13_), channel_id=1, source_target_pairs={{0,8},{4,12},{8,0},{12,4},{16,24},{20,28},{24,16},{28,20},{1,9},{5... | collective-permute-start | bytes 4718600 | tf_op jit(solution)/shard_map/ppermute | solution.py:19
  91.3 44.9 %collective-permute-start.19 = (bf16[288,2048]{1,0:T(8,128)(2,1)}, bf16[288,2048]{1,0:T(8,128)(2,1)}, u32[]{:S(2)}, u32[]{:S(2)}) collective-permute-start(bf16[288,2048]{1,0:T(8,128)(2,1)} %slice.112), channel_id=1, source_target_pairs={{0,2},{4,6},{9,10},{13,14},{18,17},{22,21},{27,25},{31,29}} | collective-permute-start | bytes 3538952 | tf_op jit(solution)/shard_map/ppermute | solution.py:239
  110.9 28.6 %collective-permute-start.32 = (bf16[192,2048]{1,0:T(8,128)(2,1)}, bf16[192,2048]{1,0:T(8,128)(2,1)}, u32[]{:S(2)}, u32[]{:S(2)}) collective-permute-start(bf16[192,2048]{1,0:T(8,128)(2,1)} %pad_maximum_fusion.3), channel_id=1, source_target_pairs={{0,16},{4,20},{8,24},{12,28},{16,0},{20,4},{24,8},{28,12},{1,17},{... | collective-permute-start | bytes 2359304 | tf_op jit(solution)/shard_map/ppermute | solution.py:19
  112.6 29.5 %collective-permute-start.21 = (bf16[288,2048]{1,0:T(8,128)(2,1)}, bf16[288,2048]{1,0:T(8,128)(2,1)S(1)}, u32[]{:S(2)}, u32[]{:S(2)}) collective-permute-start(bf16[288,2048]{1,0:T(8,128)(2,1)} %collective-permute-done.17), channel_id=1, source_target_pairs={{2,1},{6,5},{10,8},{14,12},{17,19},{21,23},{25,26},{29,30}} | collective-permute-start | bytes 3538952 | tf_op jit(solution)/shard_map/ppermute | solution.py:239
  115.7 26.5 %collective-permute-start.20 = (bf16[288,2048]{1,0:T(8,128)(2,1)}, bf16[288,2048]{1,0:T(8,128)(2,1)S(1)}, u32[]{:S(2)}, u32[]{:S(2)}) collective-permute-start(bf16[288,2048]{1,0:T(8,128)(2,1)} %collective-permute-done.17), channel_id=1, source_target_pairs={{2,3},{6,7},{10,11},{14,15},{17,16},{21,20},{25,24},{29,28}} | collective-permute-start | bytes 3538952 | tf_op jit(solution)/shard_map/ppermute | solution.py:239
  118.1 26.4 %collective-permute-start.18 = (bf16[384,2048]{1,0:T(8,128)(2,1)}, bf16[384,2048]{1,0:T(8,128)(2,1)S(1)}, u32[]{:S(2)}, u32[]{:S(2)}) collective-permute-start(bf16[384,2048]{1,0:T(8,128)(2,1)} %collective-permute-done.11.refs_4_.refs_1_), channel_id=1, source_target_pairs={{0,4},{4,0},{8,12},{12,8},{16,20},{20,16},{24,28},{28,24},{1,5},{5... | collective-permute-start | bytes 4718600 | tf_op jit(solution)/shard_map/ppermute | solution.py:19
  136.2 28.5 %collective-permute-start.24 = (bf16[288,2048]{1,0:T(8,128)(2,1)}, bf16[288,2048]{1,0:T(8,128)(2,1)S(1)}, u32[]{:S(2)}, u32[]{:S(2)}) collective-permute-start(bf16[288,2048]{1,0:T(8,128)(2,1)} %collective-permute-done.19), channel_id=1, source_target_pairs={{2,1},{6,5},{10,8},{14,12},{17,19},{21,23},{25,26},{29,30}} | collective-permute-start | bytes 3538952 | tf_op jit(solution)/shard_map/ppermute | solution.py:239
  139.5 25.1 %collective-permute-start.23 = (bf16[288,2048]{1,0:T(8,128)(2,1)}, bf16[288,2048]{1,0:T(8,128)(2,1)S(1)}, u32[]{:S(2)}, u32[]{:S(2)}) collective-permute-start(bf16[288,2048]{1,0:T(8,128)(2,1)} %collective-permute-done.19), channel_id=1, source_target_pairs={{2,3},{6,7},{10,11},{14,15},{17,16},{21,20},{25,24},{29,28}} | collective-permute-start | bytes 3538952 | tf_op jit(solution)/shard_map/ppermute | solution.py:239
  144.5 28.2 %collective-permute-start.30 = (bf16[384,2048]{1,0:T(8,128)(2,1)}, bf16[384,2048]{1,0:T(8,128)(2,1)S(1)}, u32[]{:S(2)}, u32[]{:S(2)}) collective-permute-start(bf16[384,2048]{1,0:T(8,128)(2,1)} %collective-permute-done.8.refs_3_.refs_13_), channel_id=1, source_target_pairs={{0,4},{4,0},{8,12},{12,8},{16,20},{20,16},{24,28},{28,24},{1,5},{5... | collective-permute-start | bytes 4718600 | tf_op jit(solution)/shard_map/ppermute | solution.py:19
  151.4 17.2 %collective-permute-start.22 = (bf16[288,1024]{1,0:T(8,128)(2,1)S(1)}, bf16[288,1024]{1,0:T(8,128)(2,1)S(1)}, u32[]{:S(2)}, u32[]{:S(2)}) collective-permute-start(bf16[288,1024]{1,0:T(8,128)(2,1)S(1)} %constant_dynamic-slice_fusion.9.refs_3_), channel_id=1, source_target_pairs={{0,2},{4,6},{9,10},{13,14},{18,17},{22,21},{27,25},{31,29}} | collective-permute-start | bytes 1769480 | tf_op jit(solution)/shard_map/ppermute | solution.py:239
  155.8 34.1 %collective-permute-start.34 = (bf16[384,2048]{1,0:T(8,128)(2,1)S(1)}, bf16[384,2048]{1,0:T(8,128)(2,1)S(1)}, u32[]{:S(2)}, u32[]{:S(2)}) collective-permute-start(bf16[384,2048]{1,0:T(8,128)(2,1)S(1)} %pad_maximum_fusion.1), channel_id=1, source_target_pairs={{0,4},{4,0},{8,12},{12,8},{16,20},{20,16},{24,28},{28,24},{1,5},{5... | collective-permute-start | bytes 4718600 | tf_op jit(solution)/shard_map/ppermute | solution.py:19
  171.3 15.2 %collective-permute-start.27 = (bf16[288,1024]{1,0:T(8,128)(2,1)S(1)}, bf16[288,1024]{1,0:T(8,128)(2,1)S(1)}, u32[]{:S(2)}, u32[]{:S(2)}) collective-permute-start(bf16[288,1024]{1,0:T(8,128)(2,1)S(1)} %constant_dynamic-slice_fusion.8.refs_7_), channel_id=1, source_target_pairs={{0,2},{4,6},{9,10},{13,14},{18,17},{22,21},{27,25},{31,29}} | collective-permute-start | bytes 1769480 | tf_op jit(solution)/shard_map/ppermute | solution.py:239
  172.7 21.6 %collective-permute-start.31 = (bf16[384,2048]{1,0:T(8,128)(2,1)}, bf16[384,2048]{1,0:T(8,128)(2,1)S(1)}, u32[]{:S(2)}, u32[]{:S(2)}) collective-permute-start(bf16[384,2048]{1,0:T(8,128)(2,1)} %collective-permute-done.9.refs_2_.refs_11_), channel_id=1, source_target_pairs={{0,4},{4,0},{8,12},{12,8},{16,20},{20,16},{24,28},{28,24},{1,5},{5... | collective-permute-start | bytes 4718600 | tf_op jit(solution)/shard_map/ppermute | solution.py:19
  189.9 24.8 %collective-permute-start.29 = (bf16[288,1024]{1,0:T(8,128)(2,1)S(1)}, bf16[288,1024]{1,0:T(8,128)(2,1)S(1)}, u32[]{:S(2)}, u32[]{:S(2)}) collective-permute-start(bf16[288,1024]{1,0:T(8,128)(2,1)S(1)} %collective-permute-done.27.refs_8_), channel_id=1, source_target_pairs={{2,1},{6,5},{10,8},{14,12},{17,19},{21,23},{25,26},{29,30}} | collective-permute-start | bytes 1769480 | tf_op jit(solution)/shard_map/ppermute | solution.py:239
  194.3 20.4 %collective-permute-start.28 = (bf16[288,1024]{1,0:T(8,128)(2,1)S(1)}, bf16[288,1024]{1,0:T(8,128)(2,1)S(1)}, u32[]{:S(2)}, u32[]{:S(2)}) collective-permute-start(bf16[288,1024]{1,0:T(8,128)(2,1)S(1)} %collective-permute-done.27.refs_8_), channel_id=1, source_target_pairs={{2,3},{6,7},{10,11},{14,15},{17,16},{21,20},{25,24},{29,28}} | collective-permute-start | bytes 1769480 | tf_op jit(solution)/shard_map/ppermute | solution.py:239
  (34 other events, 520.7 us)

commit v5 on v4

--- a/solution.py
+++ b/solution.py
@@ -128,9 +128,11 @@
     total = refs[0] if has_total else None
     out, row_ready, col_ready, sems = refs[-4:]
 
-    @pl.when(pl.program_id(0) == 0)
+    first = pl.program_id(0) == 0
+
+    @pl.when(first)
     def _():
-        at, waits = 0, []
+        at = 0
         for j, (places, size) in enumerate(zip(rows, row_sizes)):
             to = row_ready.at[pl.ds(at, size), :]
             for i, place in enumerate(places):
@@ -140,15 +142,21 @@
                 def _():
                     pltpu.make_async_copy(place, to, sems.at[j]).start()
 
-            waits.append(pltpu.make_async_copy(places[0], to, sems.at[j]))
             at += size
-        for wait in waits:
-            wait.wait()
 
     at = 0
     for j, (start, size) in enumerate(takes):
         col_ready[at : at + size, :] = cols[j][start : start + size, :]
         at += size
+
+    @pl.when(first)
+    def _():
+        at = 0
+        for j, (places, size) in enumerate(zip(rows, row_sizes)):
+            to = row_ready.at[pl.ds(at, size), :]
+            pltpu.make_async_copy(places[0], to, sems.at[j]).wait()
+            at += size
+
     product = lax.dot_general(
         row_ready[...],
         col_ready[...],

time: 225 us -> 226 us (level)
  transfers between devices with their start and end apart: 38 -> 38, of which waited for: 14 -> 14; matrix products, arithmetic and copies ran while one was open for 13% -> 13% of each run, Pallas kernels for 9% -> 10%
where the time goes in v5:
time: 226 us; the launch traced here: 225 us
  starting transfers between devices  83.1 us (37%)
  waiting for transfers between devices  70.1 us (31%)
  Pallas kernels  33.3 us (15%)
  local copies, waits for them, and re-layouts  19.8 us (9%)
  other arithmetic  16.8 us (7%)
    ppermute x15, waiting for transfers between devices, hop(): return lax.ppermute(block, ('samp', 'var'), pairs)  52.4 us
    ppermute x17, starting transfers between devices, swapped(): lax.ppermute(block, 'samp', [(i, i ^ distance) for i in range(lax.axis_si...  40.5 us
    pallas_call x2, Pallas kernels, gram(): pl.pallas_call(functools.partial(gram_kernel, takes, row_sizes, tuple((le...  27.5 us
    ppermute x15, starting transfers between devices, hop(): return lax.ppermute(block, ('samp', 'var'), pairs)  26.4 us
    ppermute x6, starting transfers between devices, along_var(): return lax.ppermute(block, 'var', pairs)  16.2 us
    ppermute x17, waiting for transfers between devices, swapped(): lax.ppermute(block, 'samp', [(i, i ^ distance) for i in range(lax.axis_si...  13.1 us
    unnamed x47, local copies, waits for them, and re-layouts  6.39 us
    select_n x3, other arithmetic, shards(): panel = lambda got: jnp.where(owns_rows, got[0], sum(got[2:], got[1]))  4.61 us
  transfers between devices with their start and end apart: 38, of which 14 were waited for; matrix products, arithmetic and copies ran while one was open for 13% of the time, Pallas kernels for 10%

profile of v5, /device:TPU:15, one launch (start us, length us, event | category | flops | bytes accessed | tf_op | source)
XLA Modules:
  0.0 224.8 jit_solution(18060647839928961743)
XLA Ops:
  0.9 2.6 %pad_maximum_fusion.2 = bf16[288,2176]{1,0:T(8,128)(2,1)} fusion(bf16[672,128]{1,0:T(8,128)(2,1)S(1)} %broadcast_in_dim.34, bf16[672,2048]{1,0:T(8,128)(2,1)} %dose_ref.1), kind=kLoop, calls=%fused_computation.6 | loop fusion | flops 2506752 | bytes 4177920 | tf_op jit(solution)/shard_map/concatenate | solution.py:266
  9.9 3.4 %collective-permute-start.1 = (bf16[96,2048]{1,0:T(8,128)(2,1)}, bf16[96,2048]{1,0:T(8,128)(2,1)}, u32[]{:S(2)}, u32[]{:S(2)}) collective-permute-start(bf16[96,2048]{1,0:T(8,128)(2,1)} %slice.83), channel_id=1, source_target_pairs={{0,1},{1,2},{2,3},{4,5},{5,6},{6,7},{8,9},{9,10},{10,11},{12,13},{... | collective-permute-start | bytes 1179656 | tf_op jit(solution)/shard_map/ppermute | solution.py:259
  21.7 3.1 %collective-permute-start.2 = (bf16[96,2048]{1,0:T(8,128)(2,1)}, bf16[96,2048]{1,0:T(8,128)(2,1)S(1)}, u32[]{:S(2)}, u32[]{:S(2)}) collective-permute-start(bf16[96,2048]{1,0:T(8,128)(2,1)} %collective-permute-done.1), channel_id=1, source_target_pairs={{0,1},{1,2},{2,3},{4,5},{5,6},{6,7},{8,9},{9,10},{10,11},{12,13},{... | collective-permute-start | bytes 1179656 | tf_op jit(solution)/shard_map/ppermute | solution.py:259
  24.8 7.4 %collective-permute-done = bf16[288,2176]{1,0:T(8,128)(2,1)} collective-permute-done((bf16[288,2176]{1,0:T(8,128)(2,1)}, bf16[288,2176]{1,0:T(8,128)(2,1)}, u32[]{:S(2)}, u32[]{:S(2)}) %collective-permute-start) | collective-permute-done | bytes 1253408 | tf_op jit(solution)/shard_map/ppermute | solution.py:19
  41.2 3.0 %collective-permute-start.14 = (bf16[384,2048]{1,0:T(8,128)(2,1)S(1)}, bf16[384,2048]{1,0:T(8,128)(2,1)}, u32[]{:S(2)}, u32[]{:S(2)}) collective-permute-start(bf16[384,2048]{1,0:T(8,128)(2,1)S(1)} %get-tuple-element.23.refs_1_.refs_9_), channel_id=1, source_target_pairs={{0,4},{4,0},{8,12},{12,8},{16,20},{20,16},{24,28},{28,24},{1,5},{5... | collective-permute-start | bytes 4718600 | tf_op jit(solution)/shard_map/ppermute | solution.py:19
  44.2 3.0 %collective-permute-start.8 = (bf16[384,2048]{1,0:T(8,128)(2,1)S(1)}, bf16[384,2048]{1,0:T(8,128)(2,1)}, u32[]{:S(2)}, u32[]{:S(2)}) collective-permute-start(bf16[384,2048]{1,0:T(8,128)(2,1)S(1)} %get-tuple-element.23.refs_1_.refs_9_), channel_id=1, source_target_pairs={{0,16},{4,20},{8,24},{12,28},{16,0},{20,4},{24,8},{28,12},{1,17},{... | collective-permute-start | bytes 4718600 | tf_op jit(solution)/shard_map/ppermute | solution.py:19
  47.2 3.7 %collective-permute-start.16 = (bf16[96,2048]{1,0:T(8,128)(2,1)}, bf16[96,2048]{1,0:T(8,128)(2,1)S(1)}, u32[]{:S(2)}, u32[]{:S(2)}) collective-permute-start(bf16[96,2048]{1,0:T(8,128)(2,1)} %copy-done.8), channel_id=1, source_target_pairs={{1,0},{2,1},{3,2},{5,4},{6,5},{7,6},{9,8},{10,9},{11,10},{13,12},{... | collective-permute-start | bytes 1179656 | tf_op jit(solution)/shard_map/ppermute | solution.py:259
  50.9 20.6 %collective-permute-done.10 = bf16[336,2048]{1,0:T(8,128)(2,1)} collective-permute-done((bf16[336,2048]{1,0:T(8,128)(2,1)S(1)}, bf16[336,2048]{1,0:T(8,128)(2,1)}, u32[]{:S(2)}, u32[]{:S(2)}) %collective-permute-start.10) | collective-permute-done | bytes 1376288 | tf_op jit(solution)/shard_map/ppermute | solution.py:247
  74.3 5.0 %collective-permute-start.13 = (bf16[336,2048]{1,0:T(8,128)(2,1)}, bf16[336,2048]{1,0:T(8,128)(2,1)}, u32[]{:S(2)}, u32[]{:S(2)}) collective-permute-start(bf16[336,2048]{1,0:T(8,128)(2,1)} %collective-permute-done.10), channel_id=1, source_target_pairs={{2,1},{6,5},{10,8},{14,12},{17,19},{21,23},{25,26},{29,30}} | collective-permute-start | bytes 4128776 | tf_op jit(solution)/shard_map/ppermute | solution.py:247
  83.0 2.4 %collective-permute-start.12 = (bf16[336,2048]{1,0:T(8,128)(2,1)}, bf16[336,2048]{1,0:T(8,128)(2,1)}, u32[]{:S(2)}, u32[]{:S(2)}) collective-permute-start(bf16[336,2048]{1,0:T(8,128)(2,1)} %collective-permute-done.10), channel_id=1, source_target_pairs={{2,3},{6,7},{10,11},{14,15},{17,16},{21,20},{25,24},{29,28}} | collective-permute-start | bytes 4128776 | tf_op jit(solution)/shard_map/ppermute | solution.py:247
  88.8 2.5 %slice.112 = bf16[288,2048]{1,0:T(8,128)(2,1)} slice(bf16[384,2048]{1,0:T(8,128)(2,1)} %collective-permute-done.8.refs_3_.refs_13_), slice={[96:384], [0:2048]} | slice | bytes 2359296 | tf_op jit(solution)/shard_map/slice | solution.py:328
  94.9 16.0 %collective-permute-done.17 = bf16[288,2048]{1,0:T(8,128)(2,1)} collective-permute-done((bf16[288,2048]{1,0:T(8,128)(2,1)S(1)}, bf16[288,2048]{1,0:T(8,128)(2,1)}, u32[]{:S(2)}, u32[]{:S(2)}) %collective-permute-start.17) | collective-permute-done | bytes 1179680 | tf_op jit(solution)/shard_map/ppermute | solution.py:247
  112.6 3.0 %collective-permute-start.21 = (bf16[288,2048]{1,0:T(8,128)(2,1)}, bf16[288,2048]{1,0:T(8,128)(2,1)S(1)}, u32[]{:S(2)}, u32[]{:S(2)}) collective-permute-start(bf16[288,2048]{1,0:T(8,128)(2,1)} %collective-permute-done.17), channel_id=1, source_target_pairs={{2,1},{6,5},{10,8},{14,12},{17,19},{21,23},{25,26},{29,30}} | collective-permute-start | bytes 3538952 | tf_op jit(solution)/shard_map/ppermute | solution.py:247
  118.1 9.3 %collective-permute-start.18 = (bf16[384,2048]{1,0:T(8,128)(2,1)}, bf16[384,2048]{1,0:T(8,128)(2,1)S(1)}, u32[]{:S(2)}, u32[]{:S(2)}) collective-permute-start(bf16[384,2048]{1,0:T(8,128)(2,1)} %collective-permute-done.11.refs_4_.refs_1_), channel_id=1, source_target_pairs={{0,4},{4,0},{8,12},{12,8},{16,20},{20,16},{24,28},{28,24},{1,5},{5... | collective-permute-start | bytes 4718600 | tf_op jit(solution)/shard_map/ppermute | solution.py:19
  129.4 6.8 %collective-permute-done.19 = bf16[288,2048]{1,0:T(8,128)(2,1)} collective-permute-done((bf16[288,2048]{1,0:T(8,128)(2,1)}, bf16[288,2048]{1,0:T(8,128)(2,1)}, u32[]{:S(2)}, u32[]{:S(2)}) %collective-permute-start.19) | collective-permute-done | bytes 1179680 | tf_op jit(solution)/shard_map/ppermute | solution.py:247
  144.5 5.8 %collective-permute-start.30 = (bf16[384,2048]{1,0:T(8,128)(2,1)}, bf16[384,2048]{1,0:T(8,128)(2,1)S(1)}, u32[]{:S(2)}, u32[]{:S(2)}) collective-permute-start(bf16[384,2048]{1,0:T(8,128)(2,1)} %collective-permute-done.8.refs_3_.refs_13_), channel_id=1, source_target_pairs={{0,4},{4,0},{8,12},{12,8},{16,20},{20,16},{24,28},{28,24},{1,5},{5... | collective-permute-start | bytes 4718600 | tf_op jit(solution)/shard_map/ppermute | solution.py:19
  152.7 2.9 %collective-permute-done.33 = bf16[192,2048]{1,0:T(8,128)(2,1)S(1)} collective-permute-done((bf16[192,2048]{1,0:T(8,128)(2,1)S(1)}, bf16[192,2048]{1,0:T(8,128)(2,1)S(1)}, u32[]{:S(2)}, u32[]{:S(2)}) %collective-permute-start.33) | collective-permute-done | bytes 786464 | tf_op jit(solution)/shard_map/ppermute | solution.py:19
  155.8 6.7 %collective-permute-start.34 = (bf16[384,2048]{1,0:T(8,128)(2,1)S(1)}, bf16[384,2048]{1,0:T(8,128)(2,1)S(1)}, u32[]{:S(2)}, u32[]{:S(2)}) collective-permute-start(bf16[384,2048]{1,0:T(8,128)(2,1)S(1)} %pad_maximum_fusion.1), channel_id=1, source_target_pairs={{0,4},{4,0},{8,12},{12,8},{16,20},{20,16},{24,28},{28,24},{1,5},{5... | collective-permute-start | bytes 4718600 | tf_op jit(solution)/shard_map/ppermute | solution.py:19
  164.7 3.9 %collective-permute-done.22.refs_4_ = bf16[288,1024]{1,0:T(8,128)(2,1)S(1)} collective-permute-done((bf16[288,1024]{1,0:T(8,128)(2,1)S(1)}, bf16[288,1024]{1,0:T(8,128)(2,1)S(1)}, u32[]{:S(2)}, u32[]{:S(2)}) %collective-permute-start.22) | collective-permute-done | bytes 589856 | tf_op jit(solution)/shard_map/ppermute | solution.py:247
  172.7 2.5 %collective-permute-start.31 = (bf16[384,2048]{1,0:T(8,128)(2,1)}, bf16[384,2048]{1,0:T(8,128)(2,1)S(1)}, u32[]{:S(2)}, u32[]{:S(2)}) collective-permute-start(bf16[384,2048]{1,0:T(8,128)(2,1)} %collective-permute-done.9.refs_2_.refs_11_), channel_id=1, source_target_pairs={{0,4},{4,0},{8,12},{12,8},{16,20},{20,16},{24,28},{28,24},{1,5},{5... | collective-permute-start | bytes 4718600 | tf_op jit(solution)/shard_map/ppermute | solution.py:19
  177.8 3.3 %collective-permute-done.26.refs_6_ = bf16[288,1024]{1,0:T(8,128)(2,1)S(1)} collective-permute-done((bf16[288,1024]{1,0:T(8,128)(2,1)S(1)}, bf16[288,1024]{1,0:T(8,128)(2,1)S(1)}, u32[]{:S(2)}, u32[]{:S(2)}) %collective-permute-start.26) | collective-permute-done | bytes 589856 | tf_op jit(solution)/shard_map/ppermute | solution.py:247
  186.5 3.4 %collective-permute-start.36 = (bf16[288,1024]{1,0:T(8,128)(2,1)S(1)}, bf16[288,1024]{1,0:T(8,128)(2,1)S(1)}, u32[]{:S(2)}, u32[]{:S(2)}) collective-permute-start(bf16[288,1024]{1,0:T(8,128)(2,1)S(1)} %get-tuple-element.56), channel_id=1, source_target_pairs={{0,4},{4,0},{8,12},{12,8},{16,20},{20,16},{24,28},{28,24},{1,5},{5... | collective-permute-start | bytes 1769480 | tf_op jit(solution)/shard_map/ppermute | solution.py:19
  197.1 18.0 %shard_map.67.refs_11_ = f32[1024,2048]{1,0:T(8,128)} custom-call(s32[1]{0:T(128)} %bitcast.refs_0_, bf16[384,2048]{1,0:T(8,128)(2,1)S(1)} %get-tuple-element.23.refs_1_.refs_9_, bf16[384,2048]{1,0:T(8,128)(2,1)} %collective-permute-done.9.refs_2_.refs_11_, bf16[384,2048]{1,0:T(8,128)(2,1)} %collective-permute-done.8.refs_3_.refs_13_, ...), custom_call_target="tpu_custom_call" | custom-call | flops 10468982784 | bytes 32112640 | tf_op jit(solution)/shard_map/pallas_call | solution.py:189
  215.2 9.5 %shard_map.68 = f32[1024,2048]{1,0:T(8,128)} custom-call(s32[1]{0:T(128)} %bitcast.refs_0_, bf16[384,2048]{1,0:T(8,128)(2,1)} %collective-permute-done.11.refs_4_.refs_1_, bf16[384,2048]{1,0:T(8,128)(2,1)} %copy-done.4, bf16[288,1024]{1,0:T(8,128)(2,1)S(1)} %constant_dynamic-slice_fusion.9.refs_3_, ...), custom_call_target="tpu_custom_call", output_to_operand_aliasing={{}: (11, {})} | custom-call | flops 2415919104 | bytes 20316160 | tf_op jit(solution)/shard_map/pallas_call | solution.py:189
  (170 shorter events, 75.5 us)
Async XLA Ops:
  3.4 28.7 %collective-permute-start = (bf16[288,2176]{1,0:T(8,128)(2,1)}, bf16[288,2176]{1,0:T(8,128)(2,1)}, u32[]{:S(2)}, u32[]{:S(2)}) collective-permute-start(bf16[288,2176]{1,0:T(8,128)(2,1)} %pad_maximum_fusion.2), channel_id=1, source_target_pairs={{0,16},{4,20},{8,24},{12,28},{16,0},{20,4},{24,8},{28,12},{1,17},{... | collective-permute-start | bytes 3760136 | tf_op jit(solution)/shard_map/ppermute | solution.py:19
  39.6 31.9 %collective-permute-start.10 = (bf16[336,2048]{1,0:T(8,128)(2,1)S(1)}, bf16[336,2048]{1,0:T(8,128)(2,1)}, u32[]{:S(2)}, u32[]{:S(2)}) collective-permute-start(bf16[336,2048]{1,0:T(8,128)(2,1)S(1)} %get-tuple-element.24), channel_id=1, source_target_pairs={{0,2},{4,6},{9,10},{13,14},{18,17},{22,21},{27,25},{31,29}} | collective-permute-start | bytes 4128776 | tf_op jit(solution)/shard_map/ppermute | solution.py:247
  40.9 33.4 %collective-permute-start.9 = (bf16[384,2048]{1,0:T(8,128)(2,1)S(1)}, bf16[384,2048]{1,0:T(8,128)(2,1)}, u32[]{:S(2)}, u32[]{:S(2)}) collective-permute-start(bf16[384,2048]{1,0:T(8,128)(2,1)S(1)} %get-tuple-element.23.refs_1_.refs_9_), channel_id=1, source_target_pairs={{0,8},{4,12},{8,0},{12,4},{16,24},{20,28},{24,16},{28,20},{1,9},{5... | collective-permute-start | bytes 4718600 | tf_op jit(solution)/shard_map/ppermute | solution.py:19
  41.2 44.1 %collective-permute-start.14 = (bf16[384,2048]{1,0:T(8,128)(2,1)S(1)}, bf16[384,2048]{1,0:T(8,128)(2,1)}, u32[]{:S(2)}, u32[]{:S(2)}) collective-permute-start(bf16[384,2048]{1,0:T(8,128)(2,1)S(1)} %get-tuple-element.23.refs_1_.refs_9_), channel_id=1, source_target_pairs={{0,4},{4,0},{8,12},{12,8},{16,20},{20,16},{24,28},{28,24},{1,5},{5... | collective-permute-start | bytes 4718600 | tf_op jit(solution)/shard_map/ppermute | solution.py:19
  44.2 41.1 %collective-permute-start.8 = (bf16[384,2048]{1,0:T(8,128)(2,1)S(1)}, bf16[384,2048]{1,0:T(8,128)(2,1)}, u32[]{:S(2)}, u32[]{:S(2)}) collective-permute-start(bf16[384,2048]{1,0:T(8,128)(2,1)S(1)} %get-tuple-element.23.refs_1_.refs_9_), channel_id=1, source_target_pairs={{0,16},{4,20},{8,24},{12,28},{16,0},{20,4},{24,8},{28,12},{1,17},{... | collective-permute-start | bytes 4718600 | tf_op jit(solution)/shard_map/ppermute | solution.py:19
  47.2 35.8 %collective-permute-start.16 = (bf16[96,2048]{1,0:T(8,128)(2,1)}, bf16[96,2048]{1,0:T(8,128)(2,1)S(1)}, u32[]{:S(2)}, u32[]{:S(2)}) collective-permute-start(bf16[96,2048]{1,0:T(8,128)(2,1)} %copy-done.8), channel_id=1, source_target_pairs={{1,0},{2,1},{3,2},{5,4},{6,5},{7,6},{9,8},{10,9},{11,10},{13,12},{... | collective-permute-start | bytes 1179656 | tf_op jit(solution)/shard_map/ppermute | solution.py:259
  74.3 38.3 %collective-permute-start.13 = (bf16[336,2048]{1,0:T(8,128)(2,1)}, bf16[336,2048]{1,0:T(8,128)(2,1)}, u32[]{:S(2)}, u32[]{:S(2)}) collective-permute-start(bf16[336,2048]{1,0:T(8,128)(2,1)} %collective-permute-done.10), channel_id=1, source_target_pairs={{2,1},{6,5},{10,8},{14,12},{17,19},{21,23},{25,26},{29,30}} | collective-permute-start | bytes 4128776 | tf_op jit(solution)/shard_map/ppermute | solution.py:247
  83.0 32.7 %collective-permute-start.12 = (bf16[336,2048]{1,0:T(8,128)(2,1)}, bf16[336,2048]{1,0:T(8,128)(2,1)}, u32[]{:S(2)}, u32[]{:S(2)}) collective-permute-start(bf16[336,2048]{1,0:T(8,128)(2,1)} %collective-permute-done.10), channel_id=1, source_target_pairs={{2,3},{6,7},{10,11},{14,15},{17,16},{21,20},{25,24},{29,28}} | collective-permute-start | bytes 4128776 | tf_op jit(solution)/shard_map/ppermute | solution.py:247
  85.4 25.6 %collective-permute-start.17 = (bf16[288,2048]{1,0:T(8,128)(2,1)S(1)}, bf16[288,2048]{1,0:T(8,128)(2,1)}, u32[]{:S(2)}, u32[]{:S(2)}) collective-permute-start(bf16[288,2048]{1,0:T(8,128)(2,1)S(1)} %slice.111), channel_id=1, source_target_pairs={{0,2},{4,6},{9,10},{13,14},{18,17},{22,21},{27,25},{31,29}} | collective-permute-start | bytes 3538952 | tf_op jit(solution)/shard_map/ppermute | solution.py:247
  86.7 31.5 %collective-permute-start.11 = (bf16[384,2048]{1,0:T(8,128)(2,1)}, bf16[384,2048]{1,0:T(8,128)(2,1)}, u32[]{:S(2)}, u32[]{:S(2)}) collective-permute-start(bf16[384,2048]{1,0:T(8,128)(2,1)} %collective-permute-done.8.refs_3_.refs_13_), channel_id=1, source_target_pairs={{0,8},{4,12},{8,0},{12,4},{16,24},{20,28},{24,16},{28,20},{1,9},{5... | collective-permute-start | bytes 4718600 | tf_op jit(solution)/shard_map/ppermute | solution.py:19
  91.3 44.9 %collective-permute-start.19 = (bf16[288,2048]{1,0:T(8,128)(2,1)}, bf16[288,2048]{1,0:T(8,128)(2,1)}, u32[]{:S(2)}, u32[]{:S(2)}) collective-permute-start(bf16[288,2048]{1,0:T(8,128)(2,1)} %slice.112), channel_id=1, source_target_pairs={{0,2},{4,6},{9,10},{13,14},{18,17},{22,21},{27,25},{31,29}} | collective-permute-start | bytes 3538952 | tf_op jit(solution)/shard_map/ppermute | solution.py:247
  110.9 28.6 %collective-permute-start.32 = (bf16[192,2048]{1,0:T(8,128)(2,1)}, bf16[192,2048]{1,0:T(8,128)(2,1)}, u32[]{:S(2)}, u32[]{:S(2)}) collective-permute-start(bf16[192,2048]{1,0:T(8,128)(2,1)} %pad_maximum_fusion.3), channel_id=1, source_target_pairs={{0,16},{4,20},{8,24},{12,28},{16,0},{20,4},{24,8},{28,12},{1,17},{... | collective-permute-start | bytes 2359304 | tf_op jit(solution)/shard_map/ppermute | solution.py:19
  112.6 29.5 %collective-permute-start.21 = (bf16[288,2048]{1,0:T(8,128)(2,1)}, bf16[288,2048]{1,0:T(8,128)(2,1)S(1)}, u32[]{:S(2)}, u32[]{:S(2)}) collective-permute-start(bf16[288,2048]{1,0:T(8,128)(2,1)} %collective-permute-done.17), channel_id=1, source_target_pairs={{2,1},{6,5},{10,8},{14,12},{17,19},{21,23},{25,26},{29,30}} | collective-permute-start | bytes 3538952 | tf_op jit(solution)/shard_map/ppermute | solution.py:247
  115.7 26.5 %collective-permute-start.20 = (bf16[288,2048]{1,0:T(8,128)(2,1)}, bf16[288,2048]{1,0:T(8,128)(2,1)S(1)}, u32[]{:S(2)}, u32[]{:S(2)}) collective-permute-start(bf16[288,2048]{1,0:T(8,128)(2,1)} %collective-permute-done.17), channel_id=1, source_target_pairs={{2,3},{6,7},{10,11},{14,15},{17,16},{21,20},{25,24},{29,28}} | collective-permute-start | bytes 3538952 | tf_op jit(solution)/shard_map/ppermute | solution.py:247
  118.1 26.4 %collective-permute-start.18 = (bf16[384,2048]{1,0:T(8,128)(2,1)}, bf16[384,2048]{1,0:T(8,128)(2,1)S(1)}, u32[]{:S(2)}, u32[]{:S(2)}) collective-permute-start(bf16[384,2048]{1,0:T(8,128)(2,1)} %collective-permute-done.11.refs_4_.refs_1_), channel_id=1, source_target_pairs={{0,4},{4,0},{8,12},{12,8},{16,20},{20,16},{24,28},{28,24},{1,5},{5... | collective-permute-start | bytes 4718600 | tf_op jit(solution)/shard_map/ppermute | solution.py:19
  136.2 28.5 %collective-permute-start.24 = (bf16[288,2048]{1,0:T(8,128)(2,1)}, bf16[288,2048]{1,0:T(8,128)(2,1)S(1)}, u32[]{:S(2)}, u32[]{:S(2)}) collective-permute-start(bf16[288,2048]{1,0:T(8,128)(2,1)} %collective-permute-done.19), channel_id=1, source_target_pairs={{2,1},{6,5},{10,8},{14,12},{17,19},{21,23},{25,26},{29,30}} | collective-permute-start | bytes 3538952 | tf_op jit(solution)/shard_map/ppermute | solution.py:247
  139.5 25.1 %collective-permute-start.23 = (bf16[288,2048]{1,0:T(8,128)(2,1)}, bf16[288,2048]{1,0:T(8,128)(2,1)S(1)}, u32[]{:S(2)}, u32[]{:S(2)}) collective-permute-start(bf16[288,2048]{1,0:T(8,128)(2,1)} %collective-permute-done.19), channel_id=1, source_target_pairs={{2,3},{6,7},{10,11},{14,15},{17,16},{21,20},{25,24},{29,28}} | collective-permute-start | bytes 3538952 | tf_op jit(solution)/shard_map/ppermute | solution.py:247
  144.5 28.2 %collective-permute-start.30 = (bf16[384,2048]{1,0:T(8,128)(2,1)}, bf16[384,2048]{1,0:T(8,128)(2,1)S(1)}, u32[]{:S(2)}, u32[]{:S(2)}) collective-permute-start(bf16[384,2048]{1,0:T(8,128)(2,1)} %collective-permute-done.8.refs_3_.refs_13_), channel_id=1, source_target_pairs={{0,4},{4,0},{8,12},{12,8},{16,20},{20,16},{24,28},{28,24},{1,5},{5... | collective-permute-start | bytes 4718600 | tf_op jit(solution)/shard_map/ppermute | solution.py:19
  151.4 17.2 %collective-permute-start.22 = (bf16[288,1024]{1,0:T(8,128)(2,1)S(1)}, bf16[288,1024]{1,0:T(8,128)(2,1)S(1)}, u32[]{:S(2)}, u32[]{:S(2)}) collective-permute-start(bf16[288,1024]{1,0:T(8,128)(2,1)S(1)} %constant_dynamic-slice_fusion.9.refs_3_), channel_id=1, source_target_pairs={{0,2},{4,6},{9,10},{13,14},{18,17},{22,21},{27,25},{31,29}} | collective-permute-start | bytes 1769480 | tf_op jit(solution)/shard_map/ppermute | solution.py:247
  155.8 34.1 %collective-permute-start.34 = (bf16[384,2048]{1,0:T(8,128)(2,1)S(1)}, bf16[384,2048]{1,0:T(8,128)(2,1)S(1)}, u32[]{:S(2)}, u32[]{:S(2)}) collective-permute-start(bf16[384,2048]{1,0:T(8,128)(2,1)S(1)} %pad_maximum_fusion.1), channel_id=1, source_target_pairs={{0,4},{4,0},{8,12},{12,8},{16,20},{20,16},{24,28},{28,24},{1,5},{5... | collective-permute-start | bytes 4718600 | tf_op jit(solution)/shard_map/ppermute | solution.py:19
  171.3 15.2 %collective-permute-start.27 = (bf16[288,1024]{1,0:T(8,128)(2,1)S(1)}, bf16[288,1024]{1,0:T(8,128)(2,1)S(1)}, u32[]{:S(2)}, u32[]{:S(2)}) collective-permute-start(bf16[288,1024]{1,0:T(8,128)(2,1)S(1)} %constant_dynamic-slice_fusion.8.refs_7_), channel_id=1, source_target_pairs={{0,2},{4,6},{9,10},{13,14},{18,17},{22,21},{27,25},{31,29}} | collective-permute-start | bytes 1769480 | tf_op jit(solution)/shard_map/ppermute | solution.py:247
  172.7 21.6 %collective-permute-start.31 = (bf16[384,2048]{1,0:T(8,128)(2,1)}, bf16[384,2048]{1,0:T(8,128)(2,1)S(1)}, u32[]{:S(2)}, u32[]{:S(2)}) collective-permute-start(bf16[384,2048]{1,0:T(8,128)(2,1)} %collective-permute-done.9.refs_2_.refs_11_), channel_id=1, source_target_pairs={{0,4},{4,0},{8,12},{12,8},{16,20},{20,16},{24,28},{28,24},{1,5},{5... | collective-permute-start | bytes 4718600 | tf_op jit(solution)/shard_map/ppermute | solution.py:19
  189.9 25.3 %collective-permute-start.29 = (bf16[288,1024]{1,0:T(8,128)(2,1)S(1)}, bf16[288,1024]{1,0:T(8,128)(2,1)S(1)}, u32[]{:S(2)}, u32[]{:S(2)}) collective-permute-start(bf16[288,1024]{1,0:T(8,128)(2,1)S(1)} %collective-permute-done.27.refs_8_), channel_id=1, source_target_pairs={{2,1},{6,5},{10,8},{14,12},{17,19},{21,23},{25,26},{29,30}} | collective-permute-start | bytes 1769480 | tf_op jit(solution)/shard_map/ppermute | solution.py:247
  194.3 20.9 %collective-permute-start.28 = (bf16[288,1024]{1,0:T(8,128)(2,1)S(1)}, bf16[288,1024]{1,0:T(8,128)(2,1)S(1)}, u32[]{:S(2)}, u32[]{:S(2)}) collective-permute-start(bf16[288,1024]{1,0:T(8,128)(2,1)S(1)} %collective-permute-done.27.refs_8_), channel_id=1, source_target_pairs={{2,3},{6,7},{10,11},{14,15},{17,16},{21,20},{25,24},{29,28}} | collective-permute-start | bytes 1769480 | tf_op jit(solution)/shard_map/ppermute | solution.py:247
  (34 other events, 520.7 us)

commit v6 on v4

--- a/solution.py
+++ b/solution.py
@@ -336,7 +336,7 @@
     pieces[both + 1] = swapped(after(pieces[both], *legs[0][2:], legs[1][1]), 1)
     done = (legs[2][1], *legs[1][2:])
     tail = [row_part(pieces[m], early, size) for m in (both, both + 1)]
-    legs.append(along_line(after(tail[0], *done), *legs[2][2:]))
+    legs.append(along_line(after(tail[0], legs[2][1]), *legs[2][2:]))
     legs.append(along_line(after(tail[1], *done), *legs[2][2:], *legs[3][2:]))
     aside = jnp.concatenate([of_panel(chip ^ 1), up[early:]], 0)
     aside = swapped(after(aside, *done), near)

time: 225 us -> 225 us (level)
  no operation moved by 1% of the time
where the time goes in v6:
time: 225 us; the launch traced here: 224 us
  starting transfers between devices  83 us (37%)
  waiting for transfers between devices  70.2 us (31%)
  Pallas kernels  32.6 us (14%)
  local copies, waits for them, and re-layouts  19.8 us (9%)
  other arithmetic  16.8 us (7%)
    ppermute x15, waiting for transfers between devices, hop(): return lax.ppermute(block, ('samp', 'var'), pairs)  52.4 us
    ppermute x17, starting transfers between devices, swapped(): lax.ppermute(block, 'samp', [(i, i ^ distance) for i in range(lax.axis_si...  40.5 us
    pallas_call x2, Pallas kernels, gram(): pl.pallas_call(functools.partial(gram_kernel, takes, row_sizes, tuple((le...  26.9 us
    ppermute x15, starting transfers between devices, hop(): return lax.ppermute(block, ('samp', 'var'), pairs)  26.4 us
    ppermute x6, starting transfers between devices, along_var(): return lax.ppermute(block, 'var', pairs)  16.2 us
    ppermute x17, waiting for transfers between devices, swapped(): lax.ppermute(block, 'samp', [(i, i ^ distance) for i in range(lax.axis_si...  13.1 us
    unnamed x47, local copies, waits for them, and re-layouts  6.39 us
    select_n x3, other arithmetic, shards(): panel = lambda got: jnp.where(owns_rows, got[0], sum(got[2:], got[1]))  4.61 us
  transfers between devices with their start and end apart: 38, of which 14 were waited for; matrix products, arithmetic and copies ran while one was open for 13% of the time, Pallas kernels for 9%

profile of v6, /device:TPU:15, one launch (start us, length us, event | category | flops | bytes accessed | tf_op | source)
XLA Modules:
  0.0 224.2 jit_solution(8291250680795195469)
XLA Ops:
  0.9 2.6 %pad_maximum_fusion.2 = bf16[288,2176]{1,0:T(8,128)(2,1)} fusion(bf16[672,128]{1,0:T(8,128)(2,1)S(1)} %broadcast_in_dim.34, bf16[672,2048]{1,0:T(8,128)(2,1)} %dose_ref.1), kind=kLoop, calls=%fused_computation.6 | loop fusion | flops 2506752 | bytes 4177920 | tf_op jit(solution)/shard_map/concatenate | solution.py:258
  9.9 3.4 %collective-permute-start.1 = (bf16[96,2048]{1,0:T(8,128)(2,1)}, bf16[96,2048]{1,0:T(8,128)(2,1)}, u32[]{:S(2)}, u32[]{:S(2)}) collective-permute-start(bf16[96,2048]{1,0:T(8,128)(2,1)} %slice.83), channel_id=1, source_target_pairs={{0,1},{1,2},{2,3},{4,5},{5,6},{6,7},{8,9},{9,10},{10,11},{12,13},{... | collective-permute-start | bytes 1179656 | tf_op jit(solution)/shard_map/ppermute | solution.py:251
  21.7 3.1 %collective-permute-start.2 = (bf16[96,2048]{1,0:T(8,128)(2,1)}, bf16[96,2048]{1,0:T(8,128)(2,1)S(1)}, u32[]{:S(2)}, u32[]{:S(2)}) collective-permute-start(bf16[96,2048]{1,0:T(8,128)(2,1)} %collective-permute-done.1), channel_id=1, source_target_pairs={{0,1},{1,2},{2,3},{4,5},{5,6},{6,7},{8,9},{9,10},{10,11},{12,13},{... | collective-permute-start | bytes 1179656 | tf_op jit(solution)/shard_map/ppermute | solution.py:251
  24.8 7.4 %collective-permute-done = bf16[288,2176]{1,0:T(8,128)(2,1)} collective-permute-done((bf16[288,2176]{1,0:T(8,128)(2,1)}, bf16[288,2176]{1,0:T(8,128)(2,1)}, u32[]{:S(2)}, u32[]{:S(2)}) %collective-permute-start) | collective-permute-done | bytes 1253408 | tf_op jit(solution)/shard_map/ppermute | solution.py:19
  41.2 3.0 %collective-permute-start.14 = (bf16[384,2048]{1,0:T(8,128)(2,1)S(1)}, bf16[384,2048]{1,0:T(8,128)(2,1)}, u32[]{:S(2)}, u32[]{:S(2)}) collective-permute-start(bf16[384,2048]{1,0:T(8,128)(2,1)S(1)} %get-tuple-element.23.refs_1_.refs_9_), channel_id=1, source_target_pairs={{0,4},{4,0},{8,12},{12,8},{16,20},{20,16},{24,28},{28,24},{1,5},{5... | collective-permute-start | bytes 4718600 | tf_op jit(solution)/shard_map/ppermute | solution.py:19
  44.2 3.0 %collective-permute-start.8 = (bf16[384,2048]{1,0:T(8,128)(2,1)S(1)}, bf16[384,2048]{1,0:T(8,128)(2,1)}, u32[]{:S(2)}, u32[]{:S(2)}) collective-permute-start(bf16[384,2048]{1,0:T(8,128)(2,1)S(1)} %get-tuple-element.23.refs_1_.refs_9_), channel_id=1, source_target_pairs={{0,16},{4,20},{8,24},{12,28},{16,0},{20,4},{24,8},{28,12},{1,17},{... | collective-permute-start | bytes 4718600 | tf_op jit(solution)/shard_map/ppermute | solution.py:19
  47.2 3.7 %collective-permute-start.16 = (bf16[96,2048]{1,0:T(8,128)(2,1)}, bf16[96,2048]{1,0:T(8,128)(2,1)S(1)}, u32[]{:S(2)}, u32[]{:S(2)}) collective-permute-start(bf16[96,2048]{1,0:T(8,128)(2,1)} %copy-done.8), channel_id=1, source_target_pairs={{1,0},{2,1},{3,2},{5,4},{6,5},{7,6},{9,8},{10,9},{11,10},{13,12},{... | collective-permute-start | bytes 1179656 | tf_op jit(solution)/shard_map/ppermute | solution.py:251
  50.9 20.6 %collective-permute-done.10 = bf16[336,2048]{1,0:T(8,128)(2,1)} collective-permute-done((bf16[336,2048]{1,0:T(8,128)(2,1)S(1)}, bf16[336,2048]{1,0:T(8,128)(2,1)}, u32[]{:S(2)}, u32[]{:S(2)}) %collective-permute-start.10) | collective-permute-done | bytes 1376288 | tf_op jit(solution)/shard_map/ppermute | solution.py:239
  74.3 5.0 %collective-permute-start.13 = (bf16[336,2048]{1,0:T(8,128)(2,1)}, bf16[336,2048]{1,0:T(8,128)(2,1)}, u32[]{:S(2)}, u32[]{:S(2)}) collective-permute-start(bf16[336,2048]{1,0:T(8,128)(2,1)} %collective-permute-done.10), channel_id=1, source_target_pairs={{2,1},{6,5},{10,8},{14,12},{17,19},{21,23},{25,26},{29,30}} | collective-permute-start | bytes 4128776 | tf_op jit(solution)/shard_map/ppermute | solution.py:239
  83.0 2.4 %collective-permute-start.12 = (bf16[336,2048]{1,0:T(8,128)(2,1)}, bf16[336,2048]{1,0:T(8,128)(2,1)}, u32[]{:S(2)}, u32[]{:S(2)}) collective-permute-start(bf16[336,2048]{1,0:T(8,128)(2,1)} %collective-permute-done.10), channel_id=1, source_target_pairs={{2,3},{6,7},{10,11},{14,15},{17,16},{21,20},{25,24},{29,28}} | collective-permute-start | bytes 4128776 | tf_op jit(solution)/shard_map/ppermute | solution.py:239
  88.8 2.5 %slice.112 = bf16[288,2048]{1,0:T(8,128)(2,1)} slice(bf16[384,2048]{1,0:T(8,128)(2,1)} %collective-permute-done.8.refs_3_.refs_13_), slice={[96:384], [0:2048]} | slice | bytes 2359296 | tf_op jit(solution)/shard_map/slice | solution.py:320
  94.9 16.0 %collective-permute-done.17 = bf16[288,2048]{1,0:T(8,128)(2,1)} collective-permute-done((bf16[288,2048]{1,0:T(8,128)(2,1)S(1)}, bf16[288,2048]{1,0:T(8,128)(2,1)}, u32[]{:S(2)}, u32[]{:S(2)}) %collective-permute-start.17) | collective-permute-done | bytes 1179680 | tf_op jit(solution)/shard_map/ppermute | solution.py:239
  112.6 3.0 %collective-permute-start.26 = (bf16[288,2048]{1,0:T(8,128)(2,1)}, bf16[288,2048]{1,0:T(8,128)(2,1)S(1)}, u32[]{:S(2)}, u32[]{:S(2)}) collective-permute-start(bf16[288,2048]{1,0:T(8,128)(2,1)} %collective-permute-done.17), channel_id=1, source_target_pairs={{2,1},{6,5},{10,8},{14,12},{17,19},{21,23},{25,26},{29,30}} | collective-permute-start | bytes 3538952 | tf_op jit(solution)/shard_map/ppermute | solution.py:239
  118.1 9.3 %collective-permute-start.18 = (bf16[384,2048]{1,0:T(8,128)(2,1)}, bf16[384,2048]{1,0:T(8,128)(2,1)S(1)}, u32[]{:S(2)}, u32[]{:S(2)}) collective-permute-start(bf16[384,2048]{1,0:T(8,128)(2,1)} %collective-permute-done.11.refs_4_.refs_1_), channel_id=1, source_target_pairs={{0,4},{4,0},{8,12},{12,8},{16,20},{20,16},{24,28},{28,24},{1,5},{5... | collective-permute-start | bytes 4718600 | tf_op jit(solution)/shard_map/ppermute | solution.py:19
  129.4 6.8 %collective-permute-done.19 = bf16[288,2048]{1,0:T(8,128)(2,1)} collective-permute-done((bf16[288,2048]{1,0:T(8,128)(2,1)}, bf16[288,2048]{1,0:T(8,128)(2,1)}, u32[]{:S(2)}, u32[]{:S(2)}) %collective-permute-start.19) | collective-permute-done | bytes 1179680 | tf_op jit(solution)/shard_map/ppermute | solution.py:239
  144.5 5.8 %collective-permute-start.30 = (bf16[384,2048]{1,0:T(8,128)(2,1)}, bf16[384,2048]{1,0:T(8,128)(2,1)S(1)}, u32[]{:S(2)}, u32[]{:S(2)}) collective-permute-start(bf16[384,2048]{1,0:T(8,128)(2,1)} %collective-permute-done.8.refs_3_.refs_13_), channel_id=1, source_target_pairs={{0,4},{4,0},{8,12},{12,8},{16,20},{20,16},{24,28},{28,24},{1,5},{5... | collective-permute-start | bytes 4718600 | tf_op jit(solution)/shard_map/ppermute | solution.py:19
  152.7 2.9 %collective-permute-done.33 = bf16[192,2048]{1,0:T(8,128)(2,1)S(1)} collective-permute-done((bf16[192,2048]{1,0:T(8,128)(2,1)S(1)}, bf16[192,2048]{1,0:T(8,128)(2,1)S(1)}, u32[]{:S(2)}, u32[]{:S(2)}) %collective-permute-start.33) | collective-permute-done | bytes 786464 | tf_op jit(solution)/shard_map/ppermute | solution.py:19
  155.8 6.7 %collective-permute-start.34 = (bf16[384,2048]{1,0:T(8,128)(2,1)S(1)}, bf16[384,2048]{1,0:T(8,128)(2,1)S(1)}, u32[]{:S(2)}, u32[]{:S(2)}) collective-permute-start(bf16[384,2048]{1,0:T(8,128)(2,1)S(1)} %pad_maximum_fusion.1), channel_id=1, source_target_pairs={{0,4},{4,0},{8,12},{12,8},{16,20},{20,16},{24,28},{28,24},{1,5},{5... | collective-permute-start | bytes 4718600 | tf_op jit(solution)/shard_map/ppermute | solution.py:19
  164.7 4.0 %collective-permute-done.20.refs_4_ = bf16[288,1024]{1,0:T(8,128)(2,1)S(1)} collective-permute-done((bf16[288,1024]{1,0:T(8,128)(2,1)S(1)}, bf16[288,1024]{1,0:T(8,128)(2,1)S(1)}, u32[]{:S(2)}, u32[]{:S(2)}) %collective-permute-start.20) | collective-permute-done | bytes 589856 | tf_op jit(solution)/shard_map/ppermute | solution.py:239
  172.7 2.5 %collective-permute-start.31 = (bf16[384,2048]{1,0:T(8,128)(2,1)}, bf16[384,2048]{1,0:T(8,128)(2,1)S(1)}, u32[]{:S(2)}, u32[]{:S(2)}) collective-permute-start(bf16[384,2048]{1,0:T(8,128)(2,1)} %collective-permute-done.9.refs_2_.refs_11_), channel_id=1, source_target_pairs={{0,4},{4,0},{8,12},{12,8},{16,20},{20,16},{24,28},{28,24},{1,5},{5... | collective-permute-start | bytes 4718600 | tf_op jit(solution)/shard_map/ppermute | solution.py:19
  177.8 3.3 %collective-permute-done.24.refs_6_ = bf16[288,1024]{1,0:T(8,128)(2,1)S(1)} collective-permute-done((bf16[288,1024]{1,0:T(8,128)(2,1)S(1)}, bf16[288,1024]{1,0:T(8,128)(2,1)S(1)}, u32[]{:S(2)}, u32[]{:S(2)}) %collective-permute-start.24) | collective-permute-done | bytes 589856 | tf_op jit(solution)/shard_map/ppermute | solution.py:239
  186.5 3.4 %collective-permute-start.36 = (bf16[288,1024]{1,0:T(8,128)(2,1)S(1)}, bf16[288,1024]{1,0:T(8,128)(2,1)S(1)}, u32[]{:S(2)}, u32[]{:S(2)}) collective-permute-start(bf16[288,1024]{1,0:T(8,128)(2,1)S(1)} %get-tuple-element.56), channel_id=1, source_target_pairs={{0,4},{4,0},{8,12},{12,8},{16,20},{20,16},{24,28},{28,24},{1,5},{5... | collective-permute-start | bytes 1769480 | tf_op jit(solution)/shard_map/ppermute | solution.py:19
  197.1 17.5 %shard_map.67.refs_11_ = f32[1024,2048]{1,0:T(8,128)} custom-call(s32[1]{0:T(128)} %bitcast.refs_0_, bf16[384,2048]{1,0:T(8,128)(2,1)S(1)} %get-tuple-element.23.refs_1_.refs_9_, bf16[384,2048]{1,0:T(8,128)(2,1)} %collective-permute-done.9.refs_2_.refs_11_, bf16[384,2048]{1,0:T(8,128)(2,1)} %collective-permute-done.8.refs_3_.refs_13_, ...), custom_call_target="tpu_custom_call" | custom-call | flops 10468982784 | bytes 32112640 | tf_op jit(solution)/shard_map/pallas_call | solution.py:181
  214.7 9.3 %shard_map.68 = f32[1024,2048]{1,0:T(8,128)} custom-call(s32[1]{0:T(128)} %bitcast.refs_0_, bf16[384,2048]{1,0:T(8,128)(2,1)} %collective-permute-done.11.refs_4_.refs_1_, bf16[384,2048]{1,0:T(8,128)(2,1)} %copy-done.4, bf16[288,1024]{1,0:T(8,128)(2,1)S(1)} %constant_dynamic-slice_fusion.9.refs_3_, ...), custom_call_target="tpu_custom_call", output_to_operand_aliasing={{}: (11, {})} | custom-call | flops 2415919104 | bytes 20316160 | tf_op jit(solution)/shard_map/pallas_call | solution.py:181
  (170 shorter events, 75.5 us)
Async XLA Ops:
  3.4 28.7 %collective-permute-start = (bf16[288,2176]{1,0:T(8,128)(2,1)}, bf16[288,2176]{1,0:T(8,128)(2,1)}, u32[]{:S(2)}, u32[]{:S(2)}) collective-permute-start(bf16[288,2176]{1,0:T(8,128)(2,1)} %pad_maximum_fusion.2), channel_id=1, source_target_pairs={{0,16},{4,20},{8,24},{12,28},{16,0},{20,4},{24,8},{28,12},{1,17},{... | collective-permute-start | bytes 3760136 | tf_op jit(solution)/shard_map/ppermute | solution.py:19
  39.6 31.9 %collective-permute-start.10 = (bf16[336,2048]{1,0:T(8,128)(2,1)S(1)}, bf16[336,2048]{1,0:T(8,128)(2,1)}, u32[]{:S(2)}, u32[]{:S(2)}) collective-permute-start(bf16[336,2048]{1,0:T(8,128)(2,1)S(1)} %get-tuple-element.24), channel_id=1, source_target_pairs={{0,2},{4,6},{9,10},{13,14},{18,17},{22,21},{27,25},{31,29}} | collective-permute-start | bytes 4128776 | tf_op jit(solution)/shard_map/ppermute | solution.py:239
  40.9 33.4 %collective-permute-start.9 = (bf16[384,2048]{1,0:T(8,128)(2,1)S(1)}, bf16[384,2048]{1,0:T(8,128)(2,1)}, u32[]{:S(2)}, u32[]{:S(2)}) collective-permute-start(bf16[384,2048]{1,0:T(8,128)(2,1)S(1)} %get-tuple-element.23.refs_1_.refs_9_), channel_id=1, source_target_pairs={{0,8},{4,12},{8,0},{12,4},{16,24},{20,28},{24,16},{28,20},{1,9},{5... | collective-permute-start | bytes 4718600 | tf_op jit(solution)/shard_map/ppermute | solution.py:19
  41.2 44.1 %collective-permute-start.14 = (bf16[384,2048]{1,0:T(8,128)(2,1)S(1)}, bf16[384,2048]{1,0:T(8,128)(2,1)}, u32[]{:S(2)}, u32[]{:S(2)}) collective-permute-start(bf16[384,2048]{1,0:T(8,128)(2,1)S(1)} %get-tuple-element.23.refs_1_.refs_9_), channel_id=1, source_target_pairs={{0,4},{4,0},{8,12},{12,8},{16,20},{20,16},{24,28},{28,24},{1,5},{5... | collective-permute-start | bytes 4718600 | tf_op jit(solution)/shard_map/ppermute | solution.py:19
  44.2 41.1 %collective-permute-start.8 = (bf16[384,2048]{1,0:T(8,128)(2,1)S(1)}, bf16[384,2048]{1,0:T(8,128)(2,1)}, u32[]{:S(2)}, u32[]{:S(2)}) collective-permute-start(bf16[384,2048]{1,0:T(8,128)(2,1)S(1)} %get-tuple-element.23.refs_1_.refs_9_), channel_id=1, source_target_pairs={{0,16},{4,20},{8,24},{12,28},{16,0},{20,4},{24,8},{28,12},{1,17},{... | collective-permute-start | bytes 4718600 | tf_op jit(solution)/shard_map/ppermute | solution.py:19
  47.2 35.8 %collective-permute-start.16 = (bf16[96,2048]{1,0:T(8,128)(2,1)}, bf16[96,2048]{1,0:T(8,128)(2,1)S(1)}, u32[]{:S(2)}, u32[]{:S(2)}) collective-permute-start(bf16[96,2048]{1,0:T(8,128)(2,1)} %copy-done.8), channel_id=1, source_target_pairs={{1,0},{2,1},{3,2},{5,4},{6,5},{7,6},{9,8},{10,9},{11,10},{13,12},{... | collective-permute-start | bytes 1179656 | tf_op jit(solution)/shard_map/ppermute | solution.py:251
  74.3 38.3 %collective-permute-start.13 = (bf16[336,2048]{1,0:T(8,128)(2,1)}, bf16[336,2048]{1,0:T(8,128)(2,1)}, u32[]{:S(2)}, u32[]{:S(2)}) collective-permute-start(bf16[336,2048]{1,0:T(8,128)(2,1)} %collective-permute-done.10), channel_id=1, source_target_pairs={{2,1},{6,5},{10,8},{14,12},{17,19},{21,23},{25,26},{29,30}} | collective-permute-start | bytes 4128776 | tf_op jit(solution)/shard_map/ppermute | solution.py:239
  83.0 32.7 %collective-permute-start.12 = (bf16[336,2048]{1,0:T(8,128)(2,1)}, bf16[336,2048]{1,0:T(8,128)(2,1)}, u32[]{:S(2)}, u32[]{:S(2)}) collective-permute-start(bf16[336,2048]{1,0:T(8,128)(2,1)} %collective-permute-done.10), channel_id=1, source_target_pairs={{2,3},{6,7},{10,11},{14,15},{17,16},{21,20},{25,24},{29,28}} | collective-permute-start | bytes 4128776 | tf_op jit(solution)/shard_map/ppermute | solution.py:239
  85.4 25.6 %collective-permute-start.17 = (bf16[288,2048]{1,0:T(8,128)(2,1)S(1)}, bf16[288,2048]{1,0:T(8,128)(2,1)}, u32[]{:S(2)}, u32[]{:S(2)}) collective-permute-start(bf16[288,2048]{1,0:T(8,128)(2,1)S(1)} %slice.111), channel_id=1, source_target_pairs={{0,2},{4,6},{9,10},{13,14},{18,17},{22,21},{27,25},{31,29}} | collective-permute-start | bytes 3538952 | tf_op jit(solution)/shard_map/ppermute | solution.py:239
  86.7 31.5 %collective-permute-start.11 = (bf16[384,2048]{1,0:T(8,128)(2,1)}, bf16[384,2048]{1,0:T(8,128)(2,1)}, u32[]{:S(2)}, u32[]{:S(2)}) collective-permute-start(bf16[384,2048]{1,0:T(8,128)(2,1)} %collective-permute-done.8.refs_3_.refs_13_), channel_id=1, source_target_pairs={{0,8},{4,12},{8,0},{12,4},{16,24},{20,28},{24,16},{28,20},{1,9},{5... | collective-permute-start | bytes 4718600 | tf_op jit(solution)/shard_map/ppermute | solution.py:19
  91.3 44.9 %collective-permute-start.19 = (bf16[288,2048]{1,0:T(8,128)(2,1)}, bf16[288,2048]{1,0:T(8,128)(2,1)}, u32[]{:S(2)}, u32[]{:S(2)}) collective-permute-start(bf16[288,2048]{1,0:T(8,128)(2,1)} %slice.112), channel_id=1, source_target_pairs={{0,2},{4,6},{9,10},{13,14},{18,17},{22,21},{27,25},{31,29}} | collective-permute-start | bytes 3538952 | tf_op jit(solution)/shard_map/ppermute | solution.py:239
  110.9 28.6 %collective-permute-start.32 = (bf16[192,2048]{1,0:T(8,128)(2,1)}, bf16[192,2048]{1,0:T(8,128)(2,1)}, u32[]{:S(2)}, u32[]{:S(2)}) collective-permute-start(bf16[192,2048]{1,0:T(8,128)(2,1)} %pad_maximum_fusion.3), channel_id=1, source_target_pairs={{0,16},{4,20},{8,24},{12,28},{16,0},{20,4},{24,8},{28,12},{1,17},{... | collective-permute-start | bytes 2359304 | tf_op jit(solution)/shard_map/ppermute | solution.py:19
  112.6 29.5 %collective-permute-start.26 = (bf16[288,2048]{1,0:T(8,128)(2,1)}, bf16[288,2048]{1,0:T(8,128)(2,1)S(1)}, u32[]{:S(2)}, u32[]{:S(2)}) collective-permute-start(bf16[288,2048]{1,0:T(8,128)(2,1)} %collective-permute-done.17), channel_id=1, source_target_pairs={{2,1},{6,5},{10,8},{14,12},{17,19},{21,23},{25,26},{29,30}} | collective-permute-start | bytes 3538952 | tf_op jit(solution)/shard_map/ppermute | solution.py:239
  115.7 26.5 %collective-permute-start.25 = (bf16[288,2048]{1,0:T(8,128)(2,1)}, bf16[288,2048]{1,0:T(8,128)(2,1)S(1)}, u32[]{:S(2)}, u32[]{:S(2)}) collective-permute-start(bf16[288,2048]{1,0:T(8,128)(2,1)} %collective-permute-done.17), channel_id=1, source_target_pairs={{2,3},{6,7},{10,11},{14,15},{17,16},{21,20},{25,24},{29,28}} | collective-permute-start | bytes 3538952 | tf_op jit(solution)/shard_map/ppermute | solution.py:239
  118.1 26.4 %collective-permute-start.18 = (bf16[384,2048]{1,0:T(8,128)(2,1)}, bf16[384,2048]{1,0:T(8,128)(2,1)S(1)}, u32[]{:S(2)}, u32[]{:S(2)}) collective-permute-start(bf16[384,2048]{1,0:T(8,128)(2,1)} %collective-permute-done.11.refs_4_.refs_1_), channel_id=1, source_target_pairs={{0,4},{4,0},{8,12},{12,8},{16,20},{20,16},{24,28},{28,24},{1,5},{5... | collective-permute-start | bytes 4718600 | tf_op jit(solution)/shard_map/ppermute | solution.py:19
  136.2 32.4 %collective-permute-start.22 = (bf16[288,2048]{1,0:T(8,128)(2,1)}, bf16[288,2048]{1,0:T(8,128)(2,1)S(1)}, u32[]{:S(2)}, u32[]{:S(2)}) collective-permute-start(bf16[288,2048]{1,0:T(8,128)(2,1)} %collective-permute-done.19), channel_id=1, source_target_pairs={{2,1},{6,5},{10,8},{14,12},{17,19},{21,23},{25,26},{29,30}} | collective-permute-start | bytes 3538952 | tf_op jit(solution)/shard_map/ppermute | solution.py:239
  139.5 29.1 %collective-permute-start.21 = (bf16[288,2048]{1,0:T(8,128)(2,1)}, bf16[288,2048]{1,0:T(8,128)(2,1)S(1)}, u32[]{:S(2)}, u32[]{:S(2)}) collective-permute-start(bf16[288,2048]{1,0:T(8,128)(2,1)} %collective-permute-done.19), channel_id=1, source_target_pairs={{2,3},{6,7},{10,11},{14,15},{17,16},{21,20},{25,24},{29,28}} | collective-permute-start | bytes 3538952 | tf_op jit(solution)/shard_map/ppermute | solution.py:239
  144.5 28.2 %collective-permute-start.30 = (bf16[384,2048]{1,0:T(8,128)(2,1)}, bf16[384,2048]{1,0:T(8,128)(2,1)S(1)}, u32[]{:S(2)}, u32[]{:S(2)}) collective-permute-start(bf16[384,2048]{1,0:T(8,128)(2,1)} %collective-permute-done.8.refs_3_.refs_13_), channel_id=1, source_target_pairs={{0,4},{4,0},{8,12},{12,8},{16,20},{20,16},{24,28},{28,24},{1,5},{5... | collective-permute-start | bytes 4718600 | tf_op jit(solution)/shard_map/ppermute | solution.py:19
  151.4 17.2 %collective-permute-start.20 = (bf16[288,1024]{1,0:T(8,128)(2,1)S(1)}, bf16[288,1024]{1,0:T(8,128)(2,1)S(1)}, u32[]{:S(2)}, u32[]{:S(2)}) collective-permute-start(bf16[288,1024]{1,0:T(8,128)(2,1)S(1)} %constant_dynamic-slice_fusion.9.refs_3_), channel_id=1, source_target_pairs={{0,2},{4,6},{9,10},{13,14},{18,17},{22,21},{27,25},{31,29}} | collective-permute-start | bytes 1769480 | tf_op jit(solution)/shard_map/ppermute | solution.py:239
  155.8 34.1 %collective-permute-start.34 = (bf16[384,2048]{1,0:T(8,128)(2,1)S(1)}, bf16[384,2048]{1,0:T(8,128)(2,1)S(1)}, u32[]{:S(2)}, u32[]{:S(2)}) collective-permute-start(bf16[384,2048]{1,0:T(8,128)(2,1)S(1)} %pad_maximum_fusion.1), channel_id=1, source_target_pairs={{0,4},{4,0},{8,12},{12,8},{16,20},{20,16},{24,28},{28,24},{1,5},{5... | collective-permute-start | bytes 4718600 | tf_op jit(solution)/shard_map/ppermute | solution.py:19
  171.3 15.2 %collective-permute-start.27 = (bf16[288,1024]{1,0:T(8,128)(2,1)S(1)}, bf16[288,1024]{1,0:T(8,128)(2,1)S(1)}, u32[]{:S(2)}, u32[]{:S(2)}) collective-permute-start(bf16[288,1024]{1,0:T(8,128)(2,1)S(1)} %constant_dynamic-slice_fusion.8.refs_7_), channel_id=1, source_target_pairs={{0,2},{4,6},{9,10},{13,14},{18,17},{22,21},{27,25},{31,29}} | collective-permute-start | bytes 1769480 | tf_op jit(solution)/shard_map/ppermute | solution.py:239
  172.7 21.6 %collective-permute-start.31 = (bf16[384,2048]{1,0:T(8,128)(2,1)}, bf16[384,2048]{1,0:T(8,128)(2,1)S(1)}, u32[]{:S(2)}, u32[]{:S(2)}) collective-permute-start(bf16[384,2048]{1,0:T(8,128)(2,1)} %collective-permute-done.9.refs_2_.refs_11_), channel_id=1, source_target_pairs={{0,4},{4,0},{8,12},{12,8},{16,20},{20,16},{24,28},{28,24},{1,5},{5... | collective-permute-start | bytes 4718600 | tf_op jit(solution)/shard_map/ppermute | solution.py:19
  189.9 24.8 %collective-permute-start.29 = (bf16[288,1024]{1,0:T(8,128)(2,1)S(1)}, bf16[288,1024]{1,0:T(8,128)(2,1)S(1)}, u32[]{:S(2)}, u32[]{:S(2)}) collective-permute-start(bf16[288,1024]{1,0:T(8,128)(2,1)S(1)} %collective-permute-done.27.refs_8_), channel_id=1, source_target_pairs={{2,1},{6,5},{10,8},{14,12},{17,19},{21,23},{25,26},{29,30}} | collective-permute-start | bytes 1769480 | tf_op jit(solution)/shard_map/ppermute | solution.py:239
  194.3 20.4 %collective-permute-start.28 = (bf16[288,1024]{1,0:T(8,128)(2,1)S(1)}, bf16[288,1024]{1,0:T(8,128)(2,1)S(1)}, u32[]{:S(2)}, u32[]{:S(2)}) collective-permute-start(bf16[288,1024]{1,0:T(8,128)(2,1)S(1)} %collective-permute-done.27.refs_8_), channel_id=1, source_target_pairs={{2,3},{6,7},{10,11},{14,15},{17,16},{21,20},{25,24},{29,28}} | collective-permute-start | bytes 1769480 | tf_op jit(solution)/shard_map/ppermute | solution.py:239
  (34 other events, 520.7 us)
